TPU v7x, 32 devices: a whole 2x2x4 slice. The times are simulated.
32 devices in a mesh: seq: 8 (over z, y), head: 4 (over x, core).
Axes of the slice: x: 2, y: 2, z: 4, core: 2. Of those that a mesh axis runs over, the one named last changes fastest.
Arguments:
- x_in: bfloat16 [4, 1024, 2048], P(None, 'seq'), may hold values from -6 to 6
- cot: bfloat16 [4, 1024, 2048], P(None, 'seq'), may hold values from -6 to 6
- domain_ids: int32 [4, 1024], P(None, 'seq'), may hold values from 0 to 7
- domain_counts: int32 [8], replicated, may hold values from 256 to 1023
- domain_weights: float32 [8], replicated, may hold values from 0.5 to 2
- block_order: int32 [16], replicated, may hold values from 0 to 15, each once
- norm1: bfloat16 [2048], replicated, may hold values from 0.5 to 1.5
- w_query: bfloat16 [2048, 2048], P(None, 'head'), may hold values from -0.125 to 0.125
- w_key: bfloat16 [2048, 1024], P(None, 'head'), may hold values from -0.125 to 0.125
- w_value: bfloat16 [2048, 1024], P(None, 'head'), may hold values from -0.125 to 0.125
- w_gate_attn: bfloat16 [2048, 2048], P(None, 'head'), may hold values from -0.125 to 0.125
- w_out: bfloat16 [2048, 2048], P('head'), may hold values from -3 to 3
- query_gain: bfloat16 [128], replicated, may hold values from 0.5 to 1.5
- key_gain: bfloat16 [128], replicated, may hold values from 0.5 to 1.5
- norm2: bfloat16 [2048], replicated, may hold values from 0.5 to 1.5
- w_gate: bfloat16 [2048, 6144], P(None, 'head'), may hold values from -0.125 to 0.125
- w_up: bfloat16 [2048, 6144], P(None, 'head'), may hold values from -0.125 to 0.125
- w_down: bfloat16 [6144, 2048], P('head'), may hold values from -0.078125 to 0.078125
Outputs:
- block_out: bfloat16 [4, 1024, 2048], P(None, 'seq')
- x_grad: bfloat16 [4, 1024, 2048], P(None, 'seq')
- norm1_grad: float32 [2048], P('seq')
- w_query_grad: float32 [2048, 2048], P('seq', 'head')
- w_key_grad: float32 [2048, 1024], P('seq', 'head')
- w_value_grad: float32 [2048, 1024], P('seq', 'head')
- w_gate_attn_grad: float32 [2048, 2048], P('seq', 'head')
- w_out_grad: float32 [2048, 2048], P('head', 'seq')
- query_gain_grad: float32 [128], P('seq')
- key_gain_grad: float32 [128], P('seq')
- norm2_grad: float32 [2048], P('seq')
- w_gate_grad: float32 [2048, 6144], P('seq', 'head')
- w_up_grad: float32 [2048, 6144], P('seq', 'head')
- w_down_grad: float32 [6144, 2048], P('head', 'seq')
Inputs may be any that keep to these rules, and one draw needn't show every extreme that they name: `block_order`: each value 0 to 15 once.
All inputs are finite; a program needn't handle non-finite values.
Results may differ from a plain program's by a relative error of at most 0.025.
Values may be sent and summed in bfloat16 or wider, within the bound.
A program may use at most 960 MiB of HBM per device.

v0:
```python
import jax
import jax.numpy as jnp
from jax import lax
from jax.sharding import PartitionSpec as P

epsilon = 1e-06


def norm_scale(value):
    return lax.rsqrt(jnp.mean(value * value, axis=-1, keepdims=True) + epsilon)


def norm_back(grad_in, normed, scale, gain):
    scaled = grad_in * gain
    return scale * (scaled - normed * jnp.mean(scaled * normed, axis=-1, keepdims=True))


def product(left, right):
    return jnp.dot(left, right, preferred_element_type=jnp.float32)


def outer_sum(left, right):
    return lax.dot_general(
        left, right, (((0,), (0,)), ((), ())), preferred_element_type=jnp.float32
    )


def back_product(left, right):
    return lax.dot_general(
        left, right, (((1,), (1,)), ((), ())), preferred_element_type=jnp.float32
    )


def positions(block_order, first_row, row_count, block_rows):
    stored = first_row + jnp.arange(row_count, dtype=jnp.int32)
    slots = stored // block_rows
    slot_index = jnp.arange(block_order.shape[0], dtype=jnp.int32)
    picked = jnp.sum(
        jnp.where(slots[:, None] == slot_index[None, :], block_order[None, :], 0), axis=1
    )
    return picked * block_rows + stored % block_rows


def on_device(
    x_in,
    cot,
    domain_ids,
    domain_counts,
    domain_weights,
    block_order,
    norm1,
    w_query,
    w_key,
    w_value,
    w_gate_attn,
    w_out,
    query_gain,
    key_gain,
    norm2,
    w_gate,
    w_up,
    w_down,
):
    sequences, local_rows, model_width = x_in.shape
    row_total = sequences * local_rows
    head_dim = query_gain.shape[0]
    kv_local = w_key.shape[1] // head_dim
    q_local = w_query.shape[1] // head_dim
    group_size = q_local // kv_local
    block_rows = local_rows // 2
    seq_devices = lax.axis_size("seq")
    first_row = lax.axis_index("seq") * local_rows
    query_pos = positions(block_order, first_row, local_rows, block_rows)
    query_factor = head_dim ** (-0.5)
    q_gain = query_gain.astype(jnp.float32)
    k_gain = key_gain.astype(jnp.float32)
    gain_one = norm1.astype(jnp.float32)
    gain_two = norm2.astype(jnp.float32)
    x_float = x_in.reshape(row_total, model_width).astype(jnp.float32)
    scale_one = norm_scale(x_float)
    normed_one = x_float * scale_one
    x_normed = (normed_one * gain_one).astype(jnp.bfloat16)
    query_raw = product(x_normed, w_query).reshape(row_total, q_local, head_dim)
    key_raw = product(x_normed, w_key).reshape(row_total, kv_local, head_dim)
    value_rows = product(x_normed, w_value).astype(jnp.bfloat16)
    gate_pre = product(x_normed, w_gate_attn)
    query_scale = norm_scale(query_raw)
    query_normed = query_raw * query_scale
    key_scale = norm_scale(key_raw)
    key_normed = key_raw * key_scale
    query = (query_normed * q_gain * query_factor).astype(jnp.bfloat16)
    key_rows = (key_normed * k_gain).astype(jnp.bfloat16)
    project_query_heads = query.reshape(
        sequences, local_rows, kv_local, group_size, head_dim
    ).transpose(0, 2, 3, 1, 4)
    (
        query_scale,
        query_normed,
        key_scale,
        key_normed,
        query_heads,
        key_rows,
        value_rows,
        gate_pre,
    ) = (
        query_scale,
        query_normed,
        key_scale,
        key_normed,
        project_query_heads,
        key_rows,
        value_rows,
        gate_pre,
    )
    key_seq = key_rows.reshape(sequences, local_rows, kv_local * head_dim)
    value_seq = value_rows.reshape(sequences, local_rows, kv_local * head_dim)
    stat_shape = (sequences, kv_local, group_size, local_rows)
    running_max = jnp.full(stat_shape, -1e30, jnp.float32)
    key_piece = lax.all_gather(key_seq, "seq", axis=1, tiled=True)
    value_piece = lax.all_gather(value_seq, "seq", axis=1, tiled=True)
    row_count = key_piece.shape[1]
    key_block = key_piece.reshape(sequences, row_count, kv_local, head_dim)
    value_block = value_piece.reshape(sequences, row_count, kv_local, head_dim)
    key_pos = positions(block_order, jnp.int32(0), row_count, block_rows)
    allowed = key_pos[None, :] <= query_pos[:, None]
    scores = jnp.einsum(
        "skgqd,spkd->skgqp", query_heads, key_block, preferred_element_type=jnp.float32
    )
    scores = jnp.where(allowed, scores, -1e30)
    new_max = jnp.maximum(running_max, jnp.max(scores, axis=-1))
    weights = jnp.where(allowed, jnp.exp(scores - new_max[..., None]), 0.0)
    running_sum = jnp.sum(weights, axis=-1)
    weighted = jnp.einsum(
        "skgqp,spkd->skgqd",
        weights.astype(jnp.bfloat16),
        value_block,
        preferred_element_type=jnp.float32,
    )
    running_max, running_sum, weighted = (new_max, running_sum, weighted)
    log_total = running_max + jnp.log(running_sum)
    attn_heads = weighted / running_sum[..., None]
    attn_flat = attn_heads.transpose(0, 3, 1, 2, 4).reshape(row_total, q_local * head_dim)
    gate_sig = jax.nn.sigmoid(gate_pre)
    gated = (attn_flat * gate_sig).astype(jnp.bfloat16)
    attn_sum = lax.psum(product(gated, w_out).astype(jnp.bfloat16), "head").astype(jnp.float32)
    residual = x_float + attn_sum
    scale_two = norm_scale(residual)
    normed_two = residual * scale_two
    h_normed = (normed_two * gain_two).astype(jnp.bfloat16)
    gate_proj = product(h_normed, w_gate)
    up_proj = product(h_normed, w_up)
    gate_logit = jax.nn.sigmoid(gate_proj)
    gate_act = gate_proj * gate_logit
    mixed = (gate_act * up_proj).astype(jnp.bfloat16)
    mlp_sum = lax.psum(product(mixed, w_down).astype(jnp.bfloat16), "head").astype(jnp.float32)
    block_out = (
        (residual + mlp_sum).astype(jnp.bfloat16).reshape(sequences, local_rows, model_width)
    )
    domain_total = domain_weights.shape[0]
    domain_index = jnp.arange(domain_total, dtype=jnp.int32)
    factor = (
        domain_weights
        * (row_total * seq_devices)
        / (domain_total * domain_counts.astype(jnp.float32))
    )
    picked = domain_ids.reshape(row_total)[:, None] == domain_index[None, :]
    row_scale = jnp.sum(jnp.where(picked, factor[None, :], 0.0), axis=1)
    grad_out = cot.reshape(row_total, model_width).astype(jnp.float32) * row_scale[:, None]
    grad_low = grad_out.astype(jnp.bfloat16)
    grad_down = outer_sum(mixed, grad_low)
    grad_mixed = back_product(grad_low, w_down)
    grad_gate = (grad_mixed * up_proj * gate_logit * (1.0 + gate_proj * (1.0 - gate_logit))).astype(
        jnp.bfloat16
    )
    grad_up = (grad_mixed * gate_act).astype(jnp.bfloat16)
    grad_mlp_gate = outer_sum(h_normed, grad_gate)
    grad_mlp_up = outer_sum(h_normed, grad_up)
    grad_hnorm = lax.psum(
        (back_product(grad_gate, w_gate) + back_product(grad_up, w_up)).astype(jnp.bfloat16), "head"
    ).astype(jnp.float32)
    grad_norm_two = jnp.sum(grad_hnorm * normed_two, axis=0)
    grad_resid = grad_out + norm_back(grad_hnorm, normed_two, scale_two, gain_two)
    grad_attn = grad_resid.astype(jnp.bfloat16)
    grad_wout = outer_sum(gated, grad_attn)
    grad_gated = back_product(grad_attn, w_out)
    grad_heads_flat = (grad_gated * gate_sig).astype(jnp.bfloat16)
    grad_gatepre = (grad_gated * attn_flat * gate_sig * (1.0 - gate_sig)).astype(jnp.bfloat16)
    grad_wgate_attn = outer_sum(x_normed, grad_gatepre)
    grad_heads = grad_heads_flat.reshape(
        sequences, local_rows, kv_local, group_size, head_dim
    ).transpose(0, 2, 3, 1, 4)
    row_delta = jnp.sum(grad_heads.astype(jnp.float32) * attn_heads, axis=-1)
    key_piece = lax.all_gather(key_seq, "seq", axis=1, tiled=True)
    value_piece = lax.all_gather(value_seq, "seq", axis=1, tiled=True)
    row_count = key_piece.shape[1]
    key_block = key_piece.reshape(sequences, row_count, kv_local, head_dim)
    value_block = value_piece.reshape(sequences, row_count, kv_local, head_dim)
    key_pos = positions(block_order, jnp.int32(0), row_count, block_rows)
    allowed = key_pos[None, :] <= query_pos[:, None]
    scores = jnp.einsum(
        "skgqd,spkd->skgqp", query_heads, key_block, preferred_element_type=jnp.float32
    )
    probs = jnp.where(
        allowed, jnp.exp(jnp.where(allowed, scores, -1e30) - log_total[..., None]), 0.0
    )
    grad_probs = jnp.einsum(
        "skgqd,spkd->skgqp", grad_heads, value_block, preferred_element_type=jnp.float32
    )
    grad_scores = (probs * (grad_probs - row_delta[..., None])).astype(jnp.bfloat16)
    grad_query = jnp.einsum(
        "skgqp,spkd->skgqd", grad_scores, key_block, preferred_element_type=jnp.float32
    )
    key_term = jnp.einsum(
        "skgqp,skgqd->spkd", grad_scores, query_heads, preferred_element_type=jnp.float32
    ).reshape(sequences, row_count, kv_local * head_dim)
    value_term = jnp.einsum(
        "skgqp,skgqd->spkd",
        probs.astype(jnp.bfloat16),
        grad_heads,
        preferred_element_type=jnp.float32,
    ).reshape(sequences, row_count, kv_local * head_dim)
    grad_keys = key_term
    grad_values = value_term
    grad_query, grad_keys, grad_values = (grad_query, grad_keys, grad_values)
    grad_key_own, grad_value_own = (
        lax.psum_scatter(
            grad_keys.astype(jnp.bfloat16), "seq", scatter_dimension=1, tiled=True
        ).astype(jnp.float32),
        lax.psum_scatter(
            grad_values.astype(jnp.bfloat16), "seq", scatter_dimension=1, tiled=True
        ).astype(jnp.float32),
    )
    grad_query_rows = grad_query.transpose(0, 3, 1, 2, 4).reshape(row_total, q_local, head_dim)
    grad_qgain_part = jnp.sum(grad_query_rows * query_normed * query_factor, axis=(0, 1))
    grad_query_raw = (
        norm_back(grad_query_rows, query_normed, query_scale, q_gain * query_factor)
        .astype(jnp.bfloat16)
        .reshape(row_total, q_local * head_dim)
    )
    grad_key_rows = grad_key_own.reshape(row_total, kv_local, head_dim)
    grad_kgain_part = jnp.sum(grad_key_rows * key_normed, axis=(0, 1))
    grad_key_raw = (
        norm_back(grad_key_rows, key_normed, key_scale, k_gain)
        .astype(jnp.bfloat16)
        .reshape(row_total, kv_local * head_dim)
    )
    grad_value_low = grad_value_own.reshape(row_total, kv_local * head_dim).astype(jnp.bfloat16)
    grad_xnorm_part = (
        back_product(grad_query_raw, w_query)
        + back_product(grad_key_raw, w_key)
        + back_product(grad_value_low, w_value)
        + back_product(grad_gatepre, w_gate_attn)
    )
    grad_xnorm, grad_qgain, grad_kgain = (
        lax.psum(grad_xnorm_part.astype(jnp.bfloat16), "head").astype(jnp.float32),
        lax.psum(grad_qgain_part.astype(jnp.bfloat16), "head").astype(jnp.float32),
        lax.psum(grad_kgain_part.astype(jnp.bfloat16), "head").astype(jnp.float32),
    )
    grad_norm_one = jnp.sum(grad_xnorm * normed_one, axis=0)
    x_grad = (
        (grad_resid + norm_back(grad_xnorm, normed_one, scale_one, gain_one))
        .astype(jnp.bfloat16)
        .reshape(sequences, local_rows, model_width)
    )
    grad_wquery = outer_sum(x_normed, grad_query_raw)
    grad_wkey = outer_sum(x_normed, grad_key_raw)
    grad_wvalue = outer_sum(x_normed, grad_value_low)
    all_totals = (
        lax.psum_scatter(
            grad_norm_one.astype(jnp.bfloat16), "seq", scatter_dimension=0, tiled=True
        ).astype(jnp.float32),
        lax.psum_scatter(
            grad_wquery.astype(jnp.bfloat16), "seq", scatter_dimension=0, tiled=True
        ).astype(jnp.float32),
        lax.psum_scatter(
            grad_wkey.astype(jnp.bfloat16), "seq", scatter_dimension=0, tiled=True
        ).astype(jnp.float32),
        lax.psum_scatter(
            grad_wvalue.astype(jnp.bfloat16), "seq", scatter_dimension=0, tiled=True
        ).astype(jnp.float32),
        lax.psum_scatter(
            grad_wgate_attn.astype(jnp.bfloat16), "seq", scatter_dimension=0, tiled=True
        ).astype(jnp.float32),
        lax.psum_scatter(
            grad_wout.astype(jnp.bfloat16), "seq", scatter_dimension=1, tiled=True
        ).astype(jnp.float32),
        lax.psum_scatter(
            grad_qgain.astype(jnp.bfloat16), "seq", scatter_dimension=0, tiled=True
        ).astype(jnp.float32),
        lax.psum_scatter(
            grad_kgain.astype(jnp.bfloat16), "seq", scatter_dimension=0, tiled=True
        ).astype(jnp.float32),
        lax.psum_scatter(
            grad_mlp_gate.astype(jnp.bfloat16), "seq", scatter_dimension=0, tiled=True
        ).astype(jnp.float32),
        lax.psum_scatter(
            grad_mlp_up.astype(jnp.bfloat16), "seq", scatter_dimension=0, tiled=True
        ).astype(jnp.float32),
        lax.psum_scatter(
            grad_down.astype(jnp.bfloat16), "seq", scatter_dimension=1, tiled=True
        ).astype(jnp.float32),
        lax.psum_scatter(
            grad_norm_two.astype(jnp.bfloat16), "seq", scatter_dimension=0, tiled=True
        ).astype(jnp.float32),
    )
    return (
        block_out,
        x_grad,
        all_totals[0],
        all_totals[1],
        all_totals[2],
        all_totals[3],
        all_totals[4],
        all_totals[5],
        all_totals[6],
        all_totals[7],
        all_totals[11],
        all_totals[8],
        all_totals[9],
        all_totals[10],
    )


def solution(mesh):
    return jax.shard_map(
        on_device,
        mesh=mesh,
        in_specs=(
            P(None, "seq", None),
            P(None, "seq", None),
            P(None, "seq"),
            P(),
            P(),
            P(),
            P(),
            P(None, "head"),
            P(None, "head"),
            P(None, "head"),
            P(None, "head"),
            P("head", None),
            P(),
            P(),
            P(),
            P(None, "head"),
            P(None, "head"),
            P("head", None),
        ),
        out_specs=(
            P(None, "seq", None),
            P(None, "seq", None),
            P("seq"),
            P("seq", "head"),
            P("seq", "head"),
            P("seq", "head"),
            P("seq", "head"),
            P("head", "seq"),
            P("seq"),
            P("seq"),
            P("seq"),
            P("seq", "head"),
            P("seq", "head"),
            P("head", "seq"),
        ),
        check_vma=False,
    )
```

profile of v0, /device:TPU:0, one launch (start us, length us, event | category | flops | bytes accessed | tf_op | source)
XLA Modules:
  0.0 1429.9 jit_solution(1277008304027722373)
XLA Ops:
  34.5 37.7 %all-gather.3.cloned.1.call-done = bf16[4,1024,256]{1,2,0:T(8,128)(2,1)} async-done(((bf16[4,128,256]{1,2,0:T(8,128)(2,1)}), bf16[4,1024,256]{1,2,0:T(8,128)(2,1)}) %all-gather.3.cloned.1.call-update) | async-done | bytes 2097168 | tf_op jit(solution)/shard_map/all_gather | solution.py:119
  81.2 41.3 %all-gather.5.cloned.1.call-done = bf16[4,1024,256]{2,1,0:T(8,128)(2,1)} async-done(((bf16[4,128,256]{2,1,0:T(8,128)(2,1)}), bf16[4,1024,256]{2,1,0:T(8,128)(2,1)}) %all-gather.5.cloned.1.call-update) | async-done | bytes 2097168 | tf_op jit(solution)/shard_map/all_gather | solution.py:120
  126.4 7.4 bitcast_divide_fusion
  151.1 46.3 %all-reduce.11.cloned.1.call-done = bf16[512,2048]{1,0:T(8,128)(2,1)} async-done(((bf16[512,2048]{1,0:T(8,128)(2,1)}), bf16[512,2048]{1,0:T(8,128)(2,1)}) %all-reduce.11.cloned.1.call-update) | async-done | bytes 2097168 | tf_op jit(solution)/shard_map/psum | solution.py:145
  202.1 8.7 fusion.68
  210.8 5.0 fusion.67
  215.9 9.7 multiply_convert_fusion.2
  234.4 51.1 %all-reduce.13.cloned.1.call-done = bf16[512,2048]{1,0:T(8,128)(2,1)} async-done(((bf16[512,2048]{1,0:T(8,128)(2,1)}), bf16[512,2048]{1,0:T(8,128)(2,1)}) %all-reduce.13.cloned.1.call-update) | async-done | bytes 2097168 | tf_op jit(solution)/shard_map/psum | solution.py:178
  299.3 6.4 multiply_convert_fusion
  307.7 49.5 %copy.112 = bf16[4,1024,256]{0,2,1:T(8,128)(2,1)} copy(bf16[4,1024,256]{1,2,0:T(8,128)(2,1)S(1)} %bitcast.168) | data formatting | bytes 4194304
  357.2 128.6 %reshape.305 = bf16[1024,1024]{1,0:T(8,128)(2,1)} reshape(bf16[1024,256,4]{2,1,0:T(8,128)(2,1)} %bitcast.43) | data formatting | bytes 4194304
  485.9 7.0 bitcast_convert_fusion
  506.5 8.3 convolution_convert_fusion.6
  524.1 30.0 %reduce-scatter.31.cloned.1.call-done = bf16[128,1024]{1,0:T(8,128)(2,1)} async-done(((bf16[1024,1024]{1,0:T(8,128)(2,1)}), bf16[128,1024]{1,0:T(8,128)(2,1)}) %reduce-scatter.31.cloned.1.call-update) | async-done | bytes 262160
  554.1 19.9 %reshape.306 = bf16[128,256,4]{2,1,0:T(8,128)(2,1)} reshape(bf16[128,1024]{1,0:T(8,128)(2,1)} %reduce-scatter.31.cloned.1.call-done) | data formatting | bytes 524288
  573.9 8.7 copy.113
  583.1 41.4 %reduce-scatter.13.cloned.1.call-done = bf16[4,128,256]{2,1,0:T(8,128)(2,1)} async-done(((bf16[4,1024,256]{2,1,0:T(8,128)(2,1)}), bf16[4,128,256]{2,1,0:T(8,128)(2,1)}) %reduce-scatter.13.cloned.1.call-update) | async-done | bytes 262160 | tf_op jit(solution)/shard_map/reduce_scatter | solution.py:229
  643.0 8.2 convolution_convert_fusion
  652.8 6.8 convolution_convert_fusion.1
  659.6 6.8 convolution_convert_fusion.2
  669.0 25.8 %reduce-scatter.21.cloned.1.call-done = bf16[256,512]{1,0:T(8,128)(2,1)} async-done(((bf16[2048,512]{1,0:T(8,128)(2,1)}), bf16[256,512]{1,0:T(8,128)(2,1)}) %reduce-scatter.21.cloned.1.call-update) | async-done | bytes 262160 | tf_op jit(solution)/shard_map/reduce_scatter | solution.py:281
  696.6 68.9 %reduce-scatter.23.cloned.1.call-done = bf16[512,256]{1,0:T(8,128)(2,1)} async-done(((bf16[512,2048]{1,0:T(8,128)(2,1)}), bf16[512,256]{1,0:T(8,128)(2,1)}) %reduce-scatter.23.cloned.1.call-update) | async-done | bytes 262160 | tf_op jit(solution)/shard_map/reduce_scatter | solution.py:284
  767.3 85.9 %all-reduce.15.cloned.1.call-done = (bf16[512,2048]{1,0:T(8,128)(2,1)}, bf16[512,2048]{1,0:T(8,128)(2,1)}) async-done(((bf16[512,2048]{1,0:T(8,128)(2,1)}, bf16[512,2048]{1,0:T(8,128)(2,1)}), (bf16[512,2048]{1,0:T(8,128)(2,1)}, bf16[512,2048]{1,0:T(8,128)(2,1)})) %all-reduce.15.cloned.1.call-update) | async-done | bytes 4194320 | tf_op jit(solution)/shard_map/psum | solution.py:155
  856.1 22.1 %all-reduce.4 = (bf16[2048]{0:T(1024)(128)(2,1)S(1)}, bf16[128]{0:T(256)(128)(2,1)S(1)}, bf16[128]{0:T(256)(128)(2,1)S(1)}, bf16[2048]{0:T(1024)(128)(2,1)S(1)}) all-reduce(bf16[2048]{0:T(1024)(128)(2,1)S(1)} %get-tuple-element.16, bf16[128]{0:T(256)(128)(2,1)S(1)} %get-tuple-element.18, ...), channel_id=4, replica_groups=mesh['seq'=8,'head'=4] {'seq'}, use_global_device_ids=true, to_apply=%region_21.22.clone | all-reduce | flops 4352 | bytes 17408
  878.3 46.4 %reduce-scatter.15.cloned.1.call-done = bf16[256,512]{1,0:T(8,128)(2,1)} async-done(((bf16[2048,512]{1,0:T(8,128)(2,1)}), bf16[256,512]{1,0:T(8,128)(2,1)}) %reduce-scatter.15.cloned.1.call-update) | async-done | bytes 262160 | tf_op jit(solution)/shard_map/reduce_scatter | solution.py:272
  926.6 5.6 all-reduce.5
  933.2 57.8 %reduce-scatter.19.cloned.1.call-done = bf16[256,256]{1,0:T(8,128)(2,1)} async-done(((bf16[2048,256]{1,0:T(8,128)(2,1)}), bf16[256,256]{1,0:T(8,128)(2,1)}) %reduce-scatter.19.cloned.1.call-update) | async-done | bytes 131088 | tf_op jit(solution)/shard_map/reduce_scatter | solution.py:278
  992.7 64.6 %reduce-scatter.17.cloned.1.call-done = bf16[256,256]{1,0:T(8,128)(2,1)} async-done(((bf16[2048,256]{1,0:T(8,128)(2,1)}), bf16[256,256]{1,0:T(8,128)(2,1)}) %reduce-scatter.17.cloned.1.call-update) | async-done | bytes 131088 | tf_op jit(solution)/shard_map/reduce_scatter | solution.py:275
  1059.5 7.4 fusion.10
  1066.9 111.8 %reduce-scatter.29.cloned.1.call-done = bf16[1536,256]{1,0:T(8,128)(2,1)} async-done(((bf16[1536,2048]{1,0:T(8,128)(2,1)}), bf16[1536,256]{1,0:T(8,128)(2,1)}) %reduce-scatter.29.cloned.1.call-update) | async-done | bytes 786448 | tf_op jit(solution)/shard_map/reduce_scatter | solution.py:299
  1181.1 118.6 %reduce-scatter.27.cloned.1.call-done = bf16[256,1536]{1,0:T(8,128)(2,1)} async-done(((bf16[2048,1536]{1,0:T(8,128)(2,1)}), bf16[256,1536]{1,0:T(8,128)(2,1)}) %reduce-scatter.27.cloned.1.call-update) | async-done | bytes 786448 | tf_op jit(solution)/shard_map/reduce_scatter | solution.py:296
  1302.2 118.5 %reduce-scatter.25.cloned.1.call-done = bf16[256,1536]{1,0:T(8,128)(2,1)} async-done(((bf16[2048,1536]{1,0:T(8,128)(2,1)}), bf16[256,1536]{1,0:T(8,128)(2,1)}) %reduce-scatter.25.cloned.1.call-update) | async-done | bytes 786448 | tf_op jit(solution)/shard_map/reduce_scatter | solution.py:293
  (241 shorter events, 151.4 us)
Async XLA Ops:
  7.2 137.6 %copy-start = (bf16[512,2048]{1,0:T(8,128)(2,1)S(1)}, bf16[512,2048]{1,0:T(8,128)(2,1)}, u32[]{:S(2)}) copy-start(bf16[512,2048]{1,0:T(8,128)(2,1)} %param.29) | copy-start | bytes 6291460
  7.2 65.1 %all-gather.3.cloned.1.call-start = ((), (), s32[]{:S(2)}) async-start(), calls=%async_computation.10 | async-start | bytes 2359296 | tf_op jit(solution)/shard_map/all_gather | solution.py:119
  8.0 8.6 copy-start.43
  10.1 8.3 copy-start.41
  18.4 104.1 %all-gather.5.cloned.1.call-start = ((), (), s32[]{:S(2)}) async-start(), calls=%async_computation.11 | async-start | bytes 2359296 | tf_op jit(solution)/shard_map/all_gather | solution.py:120
  23.3 174.1 %all-reduce.11.cloned.1.call-start = ((), (), s32[]{:S(2)}) async-start(), calls=%async_computation.12 | async-start | bytes 4194304 | tf_op jit(solution)/shard_map/psum | solution.py:145
  147.4 138.0 %all-reduce.13.cloned.1.call-start = ((), (), s32[]{:S(2)}) async-start(), calls=%async_computation.13 | async-start | bytes 4194304 | tf_op jit(solution)/shard_map/psum | solution.py:178
  200.9 9.9 slice-start
  202.1 8.7 copy-start.23
  202.1 8.7 slice-start.1
  215.9 13.2 slice-start.2
  233.8 320.2 %reduce-scatter.31.cloned.1.call-start = ((), (), s32[]{:S(2)}) async-start(), calls=%async_computation.23 | async-start | bytes 2359296
  357.2 128.7 %copy-start.28 = (bf16[4,128,2,2,128]{1,4,3,2,0:T(8,128)(2,1)S(1)}, bf16[4,128,2,2,128]{1,4,3,2,0:T(8,128)(2,1)}, u32[]{:S(2)}) copy-start(bf16[4,128,2,2,128]{1,4,3,2,0:T(8,128)(2,1)} %copy-done.27) | copy-start | bytes 1572868
  485.9 138.7 %reduce-scatter.13.cloned.1.call-start = ((), (), s32[]{:S(2)}) async-start(), calls=%async_computation.14 | async-start | bytes 2359296 | tf_op jit(solution)/shard_map/reduce_scatter | solution.py:229
  497.0 197.8 %reduce-scatter.21.cloned.1.call-start = ((), (), s32[]{:S(2)}) async-start(), calls=%async_computation.18 | async-start | bytes 2359296 | tf_op jit(solution)/shard_map/reduce_scatter | solution.py:281
  501.5 264.0 %reduce-scatter.23.cloned.1.call-start = ((), (), s32[]{:S(2)}) async-start(), calls=%async_computation.19 | async-start | bytes 2359296 | tf_op jit(solution)/shard_map/reduce_scatter | solution.py:284
  506.5 346.7 %all-reduce.15.cloned.1.call-start = ((), (), s32[]{:S(2)}) async-start(), calls=%async_computation.24 | async-start | bytes 8388608 | tf_op jit(solution)/shard_map/psum | solution.py:155
  573.9 8.8 copy-start.16
  573.9 8.8 copy-start.40
  573.9 8.8 copy-start.44
  582.6 41.9 %copy-start.35 = (bf16[2048,256]{1,0:T(8,128)(2,1)S(1)}, bf16[2048,256]{1,0:T(8,128)(2,1)}, u32[]{:S(2)}) copy-start(bf16[2048,256]{1,0:T(8,128)(2,1)} %param.27) | copy-start | bytes 3145732
  582.9 43.3 %copy-start.19 = (bf16[2048,256]{1,0:T(8,128)(2,1)S(1)}, bf16[2048,256]{1,0:T(8,128)(2,1)}, u32[]{:S(2)}) copy-start(bf16[2048,256]{1,0:T(8,128)(2,1)} %param.26) | copy-start | bytes 3145732
  632.0 292.7 %reduce-scatter.15.cloned.1.call-start = ((), (), s32[]{:S(2)}) async-start(), calls=%async_computation.15 | async-start | bytes 2359296 | tf_op jit(solution)/shard_map/reduce_scatter | solution.py:272
  637.6 353.5 %reduce-scatter.19.cloned.1.call-start = ((), (), s32[]{:S(2)}) async-start(), calls=%async_computation.17 | async-start | bytes 1179648 | tf_op jit(solution)/shard_map/reduce_scatter | solution.py:278
  641.1 416.2 %reduce-scatter.17.cloned.1.call-start = ((), (), s32[]{:S(2)}) async-start(), calls=%async_computation.16 | async-start | bytes 1179648 | tf_op jit(solution)/shard_map/reduce_scatter | solution.py:275
  642.9 535.8 %reduce-scatter.29.cloned.1.call-start = ((), (), s32[]{:S(2)}) async-start(), calls=%async_computation.22 | async-start | bytes 7077888 | tf_op jit(solution)/shard_map/reduce_scatter | solution.py:299
  651.2 648.5 %reduce-scatter.27.cloned.1.call-start = ((), (), s32[]{:S(2)}) async-start(), calls=%async_computation.21 | async-start | bytes 7077888 | tf_op jit(solution)/shard_map/reduce_scatter | solution.py:296
  659.6 761.1 %reduce-scatter.25.cloned.1.call-start = ((), (), s32[]{:S(2)}) async-start(), calls=%async_computation.20 | async-start | bytes 7077888 | tf_op jit(solution)/shard_map/reduce_scatter | solution.py:293
  666.5 186.7 %copy-start.4 = (bf16[4,128,2048]{2,1,0:T(8,128)(2,1)S(1)}, bf16[4,128,2048]{2,1,0:T(8,128)(2,1)}, u32[]{:S(2)}) copy-start(bf16[4,128,2048]{2,1,0:T(8,128)(2,1)} %param.18) | copy-start | bytes 6291460
  666.5 186.7 %copy-start.38 = (f32[2048]{0:T(1024)S(1)}, f32[2048]{0:T(1024)}, u32[]{:S(2)}) copy-start(f32[2048]{0:T(1024)} %copy-done.37) | copy-start | bytes 24580
  666.5 186.7 %copy-start.42 = (f32[512]{0:T(512)S(1)}, f32[512]{0:T(512)}, u32[]{:S(2)}) copy-start(f32[512]{0:T(512)} %copy-done.41) | copy-start | bytes 6148
  1059.5 363.6 %copy-start.1 = (bf16[512,2048]{1,0:T(8,128)(2,1)S(1)}, bf16[512,2048]{1,0:T(8,128)(2,1)}, u32[]{:S(2)}) copy-start(bf16[512,2048]{1,0:T(8,128)(2,1)} %param.29) | copy-start | bytes 6291460
  (43 other events, 150.0 us)
Sparse Core Ops, SparseCore 0:
  18.5 53.7 all-gather.2
  75.0 47.4 all-gather.4
  147.5 49.8 all-reduce.10
  234.0 51.4 all-reduce.12
  486.0 68.0 reduce-scatter.30
  557.5 66.9 reduce-scatter.12
  628.0 66.7 reduce-scatter.20
  698.3 67.1 reduce-scatter.22
  768.5 84.6 all-reduce.14
  857.0 67.7 reduce-scatter.14
  928.6 62.4 reduce-scatter.18
  994.9 62.3 reduce-scatter.16
  1061.3 117.3 reduce-scatter.28
  1182.6 117.0 reduce-scatter.26
  1303.6 117.0 reduce-scatter.24
where the time goes:
time: 1430 us
  waiting for transfers between devices  946 us (66%)
  local copies, waits for them, and re-layouts  248 us (17%)
  matrix products  132 us (9%)
  other arithmetic  57.9 us (4%)
  blocking collectives  27.7 us (2%)
  between operations  16.3 us (1%)
    unnamed x127, local copies, waits for them, and re-layouts  223 us
    reduce_scatter x1, waiting for transfers between devices, on_device(): lax.psum_scatter(grad_mlp_up.astype(jnp.bfloat16), 'seq', scatter_dimensi...  119 us
    reduce_scatter x1, waiting for transfers between devices, on_device(): lax.psum_scatter(grad_mlp_gate.astype(jnp.bfloat16), 'seq', scatter_dimen...  119 us
    reduce_scatter x1, waiting for transfers between devices, on_device(): lax.psum_scatter(grad_down.astype(jnp.bfloat16), 'seq', scatter_dimension...  112 us
    psum x1, waiting for transfers between devices, on_device(): lax.psum(product(mixed, w_down).astype(jnp.bfloat16), 'head')  85.9 us
    reduce_scatter x1, waiting for transfers between devices, on_device(): lax.psum_scatter(grad_wout.astype(jnp.bfloat16), 'seq', scatter_dimension...  68.9 us
    reduce_scatter x1, waiting for transfers between devices, on_device(): lax.psum_scatter(grad_wkey.astype(jnp.bfloat16), 'seq', scatter_dimension...  64.6 us
    reduce_scatter x1, waiting for transfers between devices, on_device(): lax.psum_scatter(grad_wvalue.astype(jnp.bfloat16), 'seq', scatter_dimensi...  57.8 us
  transfers between devices with their start and end apart: 15, of which 15 were waited for; matrix products, arithmetic and copies ran while one was open for 11% of the time, Pallas kernels for 0%

commit v1 on v0

v1 whole, which is shorter than its diff:
```python
import jax
import jax.numpy as jnp
from jax import lax
from jax.sharding import PartitionSpec as P

epsilon = 1e-06
CHUNKS = 2


def norm_scale(value):
    return lax.rsqrt(jnp.mean(value * value, axis=-1, keepdims=True) + epsilon)


def norm_back(grad_in, normed, scale, gain):
    scaled = grad_in * gain
    return scale * (scaled - normed * jnp.mean(scaled * normed, axis=-1, keepdims=True))


def product(left, right):
    return jnp.dot(left, right, preferred_element_type=jnp.float32)


def outer_sum(left, right):
    return lax.dot_general(
        left, right, (((0,), (0,)), ((), ())), preferred_element_type=jnp.float32
    )


def back_product(left, right):
    return lax.dot_general(
        left, right, (((1,), (1,)), ((), ())), preferred_element_type=jnp.float32
    )


def low(value):
    return value.astype(jnp.bfloat16)


def wide(value):
    return value.astype(jnp.float32)


def bits_of(axis):
    return (lax.axis_size(axis) - 1).bit_length()


def swap(value, axis, mask):
    size = lax.axis_size(axis)
    return lax.ppermute(value, axis, [(i, i ^ mask) for i in range(size)])


def positions(block_order, device, row_count, block_rows):
    stored = device * row_count + jnp.arange(row_count, dtype=jnp.int32)
    slots = stored // block_rows
    slot_index = jnp.arange(block_order.shape[0], dtype=jnp.int32)
    picked = jnp.sum(
        jnp.where(slots[:, None] == slot_index[None, :], block_order[None, :], 0), axis=1
    )
    return picked * block_rows + stored % block_rows


def head_sum(left, weight, apply, cut):
    mine = lax.axis_index("head") & 1
    away = low(apply(left, cut(weight, 1 - mine)))
    got = swap(away, "head", 1)
    total = apply(left, cut(weight, mine)) + wide(got)
    for bit in range(1, bits_of("head")):
        part = low(total)
        total = wide(part) + wide(swap(part, "head", 1 << bit))
    part = low(total)
    other = swap(part, "head", 1)
    low_half = jnp.where(mine == 0, part, other)
    high_half = jnp.where(mine == 0, other, part)
    return wide(jnp.concatenate([low_half, high_half], axis=1))


def all_sum(value, axis):
    for bit in range(bits_of(axis)):
        value = value + swap(value, axis, 1 << bit)
    return value


def by_mask(value, count):
    rows, columns = value.shape
    bits = (count - 1).bit_length()
    value = value.reshape((rows,) + (2,) * bits + (columns // count,))
    own = lax.axis_index("seq")
    for bit in range(bits):
        at = bits - bit
        value = jnp.where(((own >> bit) & 1) == 1, jnp.flip(value, at), value)
    return value.reshape(rows, count, columns // count)


def halves(slots, bit):
    return [j for j in slots if not (j >> bit) & 1], [j for j in slots if (j >> bit) & 1]


def pick(value, slots):
    return jnp.concatenate([value[:, j] for j in slots], axis=1)


def scatter_product(left, right, slots, bits, left_is_slotted):
    def dot(chosen):
        if left_is_slotted:
            out = outer_sum(pick(left, chosen), right)
            return out.reshape(len(chosen), -1, out.shape[1])
        out = outer_sum(left, pick(right, chosen))
        return out.reshape(out.shape[0], len(chosen), -1)

    at = 0 if left_is_slotted else 1
    first = bits[0]
    keep, send = halves(slots, first)
    got = swap(low(dot(send)), "seq", 1 << first)
    total = dot(keep) + wide(got)
    for bit in bits[1:]:
        slots = keep
        keep, send = halves(slots, bit)
        here = jnp.stack([lax.index_in_dim(total, slots.index(j), at, False) for j in keep], at)
        away = jnp.stack([lax.index_in_dim(total, slots.index(j), at, False) for j in send], at)
        total = here + wide(swap(low(away), "seq", 1 << bit))
    return lax.index_in_dim(total, 0, at, False)


def on_device(
    x_in,
    cot,
    domain_ids,
    domain_counts,
    domain_weights,
    block_order,
    norm1,
    w_query,
    w_key,
    w_value,
    w_gate_attn,
    w_out,
    query_gain,
    key_gain,
    norm2,
    w_gate,
    w_up,
    w_down,
):
    sequences, local_rows, width = x_in.shape
    row_total = sequences * local_rows
    head_dim = query_gain.shape[0]
    kv_local = w_key.shape[1] // head_dim
    q_local = w_query.shape[1] // head_dim
    group = q_local // kv_local
    devices = lax.axis_size("seq")
    bits = list(range(bits_of("seq")))
    own = lax.axis_index("seq")
    block_rows = local_rows * devices // block_order.shape[0]
    query_factor = head_dim ** (-0.5)
    q_gain, k_gain = wide(query_gain), wide(key_gain)
    gain_one, gain_two = wide(norm1), wide(norm2)

    def cut_columns(weight, half):
        return lax.dynamic_slice_in_dim(weight, half * (width // 2), width // 2, 1)

    def cut_rows(weight, half):
        return lax.dynamic_slice_in_dim(weight, half * (width // 2), width // 2, 0)

    x_float = wide(x_in.reshape(row_total, width))
    scale_one = norm_scale(x_float)
    normed_one = x_float * scale_one
    x_normed = low(normed_one * gain_one)
    key_raw = product(x_normed, w_key).reshape(row_total, kv_local, head_dim)
    key_scale = norm_scale(key_raw)
    key_normed = key_raw * key_scale
    key_rows = low(key_normed * k_gain).reshape(row_total, kv_local * head_dim)
    value_rows = low(product(x_normed, w_value))
    pair = jnp.concatenate([key_rows, value_rows], axis=1).reshape(sequences, local_rows, -1)
    kv_width = kv_local * head_dim

    seqs_of = sequences // CHUNKS
    rows_of = row_total // CHUNKS

    def gather(value):
        slots = {0: value}
        for mask in range(2, devices, 2):
            slots[mask] = swap(value, "seq", mask)
        for mask in range(0, devices, 2):
            slots[mask + 1] = swap(slots[mask], "seq", 1)
        return jnp.stack([slots[j] for j in range(devices)], axis=1).reshape(
            seqs_of, devices * local_rows, -1
        )

    gathered = [gather(pair[c * seqs_of : (c + 1) * seqs_of]) for c in range(CHUNKS)]

    query_raw = product(x_normed, w_query).reshape(row_total, q_local, head_dim)
    gate_pre = product(x_normed, w_gate_attn)
    query_scale = norm_scale(query_raw)
    query_normed = query_raw * query_scale
    query = low(query_normed * q_gain * query_factor)
    gate_sig = jax.nn.sigmoid(gate_pre)

    query_pos = positions(block_order, own, local_rows, block_rows)
    key_pos = jnp.concatenate(
        [positions(block_order, own ^ j, local_rows, block_rows) for j in range(devices)]
    )
    allowed = key_pos[None, :] <= query_pos[:, None]

    domain_total = domain_weights.shape[0]
    domain_index = jnp.arange(domain_total, dtype=jnp.int32)
    factor = domain_weights * (row_total * devices) / (domain_total * wide(domain_counts))
    picked = domain_ids.reshape(row_total)[:, None] == domain_index[None, :]
    row_scale = jnp.sum(jnp.where(picked, factor[None, :], 0.0), axis=1)
    grad_out = wide(cot.reshape(row_total, width)) * row_scale[:, None]
    grad_low = low(grad_out)

    saved = []
    for c in range(CHUNKS):
        rows = slice(c * rows_of, (c + 1) * rows_of)
        heads = (
            query[rows]
            .reshape(seqs_of, local_rows, kv_local, group, head_dim)
            .transpose(0, 2, 3, 1, 4)
        )
        keys = gathered[c][..., :kv_width].reshape(seqs_of, -1, kv_local, head_dim)
        values = gathered[c][..., kv_width:].reshape(seqs_of, -1, kv_local, head_dim)
        scores = jnp.einsum("skgqd,spkd->skgqp", heads, keys, preferred_element_type=jnp.float32)
        scores = jnp.where(allowed, scores, -1e30)
        top = jnp.max(scores, axis=-1)
        weights = jnp.where(allowed, jnp.exp(scores - top[..., None]), 0.0)
        total = jnp.sum(weights, axis=-1)
        mixed = jnp.einsum(
            "skgqp,spkd->skgqd", low(weights), values, preferred_element_type=jnp.float32
        )
        attn_heads = mixed / total[..., None]
        log_total = top + jnp.log(total)
        attn_flat = attn_heads.transpose(0, 3, 1, 2, 4).reshape(rows_of, q_local * head_dim)
        gated = low(attn_flat * gate_sig[rows])
        attn_sum = head_sum(gated, w_out, product, cut_columns)
        saved.append((rows, heads, keys, values, log_total, attn_heads, attn_flat, gated, attn_sum))

    forward = []
    for c in range(CHUNKS):
        rows, attn_sum = saved[c][0], saved[c][-1]
        residual = x_float[rows] + attn_sum
        scale_two = norm_scale(residual)
        normed_two = residual * scale_two
        h_normed = low(normed_two * gain_two)
        gate_proj = product(h_normed, w_gate)
        up_proj = product(h_normed, w_up)
        gate_logit = jax.nn.sigmoid(gate_proj)
        gate_act = gate_proj * gate_logit
        hidden = low(gate_act * up_proj)
        grad_mixed = back_product(grad_low[rows], w_down)
        grad_gate = low(
            grad_mixed * up_proj * gate_logit * (1.0 + gate_proj * (1.0 - gate_logit))
        )
        grad_up = low(grad_mixed * gate_act)

        def both(pair_of, weights_of):
            return back_product(pair_of[0], weights_of[0]) + back_product(
                pair_of[1], weights_of[1]
            )

        grad_hnorm = head_sum(
            (grad_gate, grad_up),
            (w_gate, w_up),
            both,
            lambda ws, half: tuple(cut_rows(w, half) for w in ws),
        )
        forward.append(
            (residual, scale_two, normed_two, h_normed, hidden, grad_gate, grad_up, grad_hnorm)
        )

    def joined(at):
        return jnp.concatenate([f[at] for f in forward], axis=0)

    residual, scale_two, normed_two, h_normed, hidden, grad_gate, grad_up, grad_hnorm = (
        joined(i) for i in range(8)
    )

    all_slots = list(range(devices))
    even, odd = halves(all_slots, 0)
    rest = bits[1:]

    def paired(value):
        return jnp.concatenate([value, swap(value, "seq", 1)], axis=0)

    def paired_slots(value):
        split = by_mask(value, devices)
        stay = pick(split, even)
        come = swap(pick(split, odd), "seq", 1)
        out = jnp.concatenate([stay, come], axis=0)
        return out.reshape(out.shape[0], len(even), -1)

    rest_shifted = [b - 1 for b in rest]

    def scatter_rest(left, right, left_is_slotted):
        at = 0 if left_is_slotted else 1

        def dot(chosen):
            if left_is_slotted:
                out = outer_sum(pick(left, chosen), right)
                return out.reshape(len(chosen), -1, out.shape[1])
            out = outer_sum(left, pick(right, chosen))
            return out.reshape(out.shape[0], len(chosen), -1)

        slots = [j >> 1 for j in even]
        keep, total = None, None
        for bit in rest_shifted:
            if total is None:
                keep, send = halves(slots, bit)
                got = swap(low(dot(send)), "seq", 2 << bit)
                total = dot(keep) + wide(got)
            else:
                slots = keep
                keep, send = halves(slots, bit)
                here = jnp.stack(
                    [lax.index_in_dim(total, slots.index(j), at, False) for j in keep], at
                )
                away = jnp.stack(
                    [lax.index_in_dim(total, slots.index(j), at, False) for j in send], at
                )
                total = here + wide(swap(low(away), "seq", 2 << bit))
        return lax.index_in_dim(total, 0, at, False)

    out_slots = paired_slots(grad_low)
    norm_slots = paired_slots(h_normed)
    grad_down = scatter_rest(paired(hidden), out_slots, False)
    grad_mlp_gate = scatter_rest(norm_slots, paired(grad_gate), True)
    grad_mlp_up = scatter_rest(norm_slots, paired(grad_up), True)

    grad_norm_two = jnp.sum(grad_hnorm * normed_two, axis=0)
    grad_resid = grad_out + norm_back(grad_hnorm, normed_two, scale_two, gain_two)
    grad_attn = low(grad_resid)

    hidden_late, _ = lax.optimization_barrier((hidden, grad_hnorm))
    mlp_sum = head_sum(hidden_late, w_down, product, cut_columns)
    block_out = low(residual + mlp_sum).reshape(sequences, local_rows, width)

    back = []
    for c in range(CHUNKS):
        rows, heads, keys, values, log_total, attn_heads, attn_flat, gated, _ = saved[c]
        sig = gate_sig[rows]
        grad_gated = back_product(grad_attn[rows], w_out)
        grad_heads_flat = low(grad_gated * sig)
        grad_gatepre = low(grad_gated * attn_flat * sig * (1.0 - sig))
        grad_heads = grad_heads_flat.reshape(
            seqs_of, local_rows, kv_local, group, head_dim
        ).transpose(0, 2, 3, 1, 4)
        row_delta = jnp.sum(wide(grad_heads) * attn_heads, axis=-1)
        scores = jnp.einsum("skgqd,spkd->skgqp", heads, keys, preferred_element_type=jnp.float32)
        probs = jnp.where(
            allowed, jnp.exp(jnp.where(allowed, scores, -1e30) - log_total[..., None]), 0.0
        )
        grad_probs = jnp.einsum(
            "skgqd,spkd->skgqp", grad_heads, values, preferred_element_type=jnp.float32
        )
        grad_scores = low(probs * (grad_probs - row_delta[..., None]))
        grad_query = jnp.einsum(
            "skgqp,spkd->skgqd", grad_scores, keys, preferred_element_type=jnp.float32
        )
        key_term = jnp.einsum(
            "skgqp,skgqd->spkd", grad_scores, heads, preferred_element_type=jnp.float32
        ).reshape(seqs_of, devices, local_rows, kv_width)
        value_term = jnp.einsum(
            "skgqp,skgqd->spkd", low(probs), grad_heads, preferred_element_type=jnp.float32
        ).reshape(seqs_of, devices, local_rows, kv_width)
        terms = jnp.concatenate([key_term, value_term], axis=-1)
        parts = {j: terms[:, j] for j in range(devices)}
        for bit in bits:
            keep, send = halves(sorted(parts), bit)
            got = swap(low(jnp.stack([parts[j] for j in send])), "seq", 1 << bit)
            parts = {j: parts[j] + wide(got[i]) for i, j in enumerate(keep)}
        own_terms = parts[0].reshape(rows_of, 2 * kv_width)
        grad_query_rows = grad_query.transpose(0, 3, 1, 2, 4).reshape(rows_of, q_local, head_dim)
        back.append((grad_gatepre, grad_query_rows, own_terms))

    grad_gatepre, grad_query_rows, own_terms = (
        jnp.concatenate([b[i] for b in back], axis=0) for i in range(3)
    )
    gated = jnp.concatenate([s[7] for s in saved], axis=0)

    grad_qgain_part = jnp.sum(grad_query_rows * query_normed * query_factor, axis=(0, 1))
    grad_query_raw = low(
        norm_back(grad_query_rows, query_normed, query_scale, q_gain * query_factor)
    ).reshape(row_total, q_local * head_dim)
    grad_key_rows = own_terms[:, :kv_width].reshape(row_total, kv_local, head_dim)
    grad_kgain_part = jnp.sum(grad_key_rows * key_normed, axis=(0, 1))
    grad_key_raw = low(norm_back(grad_key_rows, key_normed, key_scale, k_gain)).reshape(
        row_total, kv_width
    )
    grad_value_low = low(own_terms[:, kv_width:])

    x_slots = by_mask(x_normed, devices)
    attn_slots = by_mask(grad_attn, devices)
    grad_wout = scatter_product(gated, attn_slots, all_slots, bits, False)
    early = scatter_product(
        x_slots, jnp.concatenate([grad_gatepre, grad_query_raw], axis=1), all_slots, bits, True
    )
    late = scatter_product(
        x_slots, jnp.concatenate([grad_key_raw, grad_value_low], axis=1), all_slots, bits, True
    )
    grad_wgate_attn, grad_wquery = jnp.split(early, 2, axis=1)
    grad_wkey, grad_wvalue = jnp.split(late, 2, axis=1)

    def all_four(grads, weights):
        return sum(back_product(g, w) for g, w in zip(grads, weights))

    grad_xnorm = head_sum(
        (grad_query_raw, grad_key_raw, grad_value_low, grad_gatepre),
        (w_query, w_key, w_value, w_gate_attn),
        all_four,
        lambda ws, half: tuple(cut_rows(w, half) for w in ws),
    )
    grad_norm_one = jnp.sum(grad_xnorm * normed_one, axis=0)
    x_grad = low(grad_resid + norm_back(grad_xnorm, normed_one, scale_one, gain_one)).reshape(
        sequences, local_rows, width
    )

    gains = all_sum(all_sum(jnp.concatenate([grad_qgain_part, grad_kgain_part]), "head"), "seq")
    norms = all_sum(jnp.concatenate([grad_norm_one, grad_norm_two]), "seq")

    def own_part(value):
        size = value.shape[0] // devices
        return lax.dynamic_slice_in_dim(value, own * size, size, 0)

    return (
        block_out,
        x_grad,
        own_part(norms[:width]),
        grad_wquery,
        grad_wkey,
        grad_wvalue,
        grad_wgate_attn,
        grad_wout,
        own_part(gains[:head_dim]),
        own_part(gains[head_dim:]),
        own_part(norms[width:]),
        grad_mlp_gate,
        grad_mlp_up,
        grad_down,
    )


def solution(mesh):
    return jax.shard_map(
        on_device,
        mesh=mesh,
        in_specs=(
            P(None, "seq", None),
            P(None, "seq", None),
            P(None, "seq"),
            P(),
            P(),
            P(),
            P(),
            P(None, "head"),
            P(None, "head"),
            P(None, "head"),
            P(None, "head"),
            P("head", None),
            P(),
            P(),
            P(),
            P(None, "head"),
            P(None, "head"),
            P("head", None),
        ),
        out_specs=(
            P(None, "seq", None),
            P(None, "seq", None),
            P("seq"),
            P("seq", "head"),
            P("seq", "head"),
            P("seq", "head"),
            P("seq", "head"),
            P("head", "seq"),
            P("seq"),
            P("seq"),
            P("seq"),
            P("seq", "head"),
            P("seq", "head"),
            P("head", "seq"),
        ),
        check_vma=False,
    )
```

time: 1430 us -> 914 us (0.64); the launches traced: 1430 us -> 899 us
  waiting for transfers between devices: 946 us -> 303 us
  other arithmetic: 57.9 us -> 156 us
  starting transfers between devices: 1.86 us -> 67.7 us
  blocking collectives: 27.7 us -> 0 us
    reduce_scatter x9 -> x0, waiting for transfers between devices: 654 us -> none  [the longest x1 119 us: on_device(): lax.psum_scatter(grad_mlp_up.astype(jnp.bfloat16), 'seq', scatter_dimensi...]
    ppermute x0 -> x66, waiting for transfers between devices: none -> 303 us  [swap(): return lax.ppermute(value, axis, [(i, i ^ mask) for i in range(size)])]
    unnamed x127 -> x428, local copies, waits for them, and re-layouts: 223 us -> 39.2 us
    psum x3 -> x0, waiting for transfers between devices: 183 us -> none  [the longest x1 85.9 us: on_device(): lax.psum(product(mixed, w_down).astype(jnp.bfloat16), 'head')]
    all_gather x2 -> x0, waiting for transfers between devices: 79 us -> none  [the longest x1 41.3 us: on_device(): value_piece = lax.all_gather(value_seq, 'seq', axis=1, tiled=True)]
    rev x0 -> x4, local copies, waits for them, and re-layouts: none -> 73.3 us  [by_mask(): value = jnp.where(own >> bit & 1 == 1, jnp.flip(value, at), value)]
    ppermute x0 -> x66, starting transfers between devices: none -> 67.7 us  [swap(): return lax.ppermute(value, axis, [(i, i ^ mask) for i in range(size)])]
    select_n x0 -> x18, other arithmetic: none -> 35.3 us  [the longest x12 34.7 us: by_mask(): value = jnp.where(own >> bit & 1 == 1, jnp.flip(value, at), value)]
  transfers between devices with their start and end apart: 15 -> 66, of which waited for: 15 -> 25; matrix products, arithmetic and copies ran while one was open for 11% -> 49% of each run, Pallas kernels for 0% -> 0%
where the time goes in v1:
time: 914 us; the launch traced here: 899 us
  waiting for transfers between devices  303 us (33%)
  local copies, waits for them, and re-layouts  234 us (26%)
  other arithmetic  156 us (17%)
  matrix products  135 us (15%)
  starting transfers between devices  67.7 us (7%)
    ppermute x66, waiting for transfers between devices, swap(): return lax.ppermute(value, axis, [(i, i ^ mask) for i in range(size)])  303 us
    rev x4, local copies, waits for them, and re-layouts, by_mask(): value = jnp.where(own >> bit & 1 == 1, jnp.flip(value, at), value)  73.3 us
    ppermute x66, starting transfers between devices, swap(): return lax.ppermute(value, axis, [(i, i ^ mask) for i in range(size)])  67.7 us
    convert_element_type x22, other arithmetic, low(): return value.astype(jnp.bfloat16)  52.3 us
    dot_general x12, matrix products, outer_sum(): lax.dot_general(left, right, (((0,), (0,)), ((), ())), preferred_element_...  40.5 us
    unnamed x428, local copies, waits for them, and re-layouts  39.2 us
    dot_general x20, matrix products, back_product(): lax.dot_general(left, right, (((1,), (1,)), ((), ())), preferred_element_...  36.6 us
    select_n x12, other arithmetic, by_mask(): value = jnp.where(own >> bit & 1 == 1, jnp.flip(value, at), value)  34.7 us
  transfers between devices with their start and end apart: 66, of which 25 were waited for; matrix products, arithmetic and copies ran while one was open for 49% of the time, Pallas kernels for 0%

profile of v1, /device:TPU:0, one launch (start us, length us, event | category | flops | bytes accessed | tf_op | source)
XLA Modules:
  0.0 898.8 jit_solution(7324256020046007685)
XLA Ops:
  22.9 5.9 fusion.101
  31.8 6.6 reshape.661
  54.4 19.3 %rev.39 = bf16[512,2,2,2,256]{4,3,2,1,0:T(2,128)(2,1)} reverse(bf16[512,2,2,2,256]{4,3,2,1,0:T(2,128)(2,1)} %multiply_convert_fusion), dimensions={3} | reverse | bytes 4194304 | tf_op jit(solution)/shard_map/jit(_flip)/rev | solution.py:90
  74.0 5.1 broadcast_select_fusion.3
  101.7 8.5 collective-permute-done.13
  167.2 6.8 reshape.662
  185.0 10.9 %collective-permute-done.8 = bf16[256,1024]{1,0:T(8,128)(2,1)S(1)} collective-permute-done((bf16[256,1024]{1,0:T(8,128)(2,1)S(1)}, bf16[256,1024]{1,0:T(8,128)(2,1)S(1)}, u32[]{:S(2)}, u32[]{:S(2)}) %collective-permute-start.8) | collective-permute-done | bytes 524320 | tf_op jit(solution)/shard_map/ppermute | solution.py:49
  197.3 8.9 collective-permute-done.18
  246.8 19.5 %rev.45 = bf16[512,2,2,2,256]{4,3,2,1,0:T(2,128)(2,1)} reverse(bf16[512,2,2,2,256]{4,3,2,1,0:T(2,128)(2,1)} %reshape.646), dimensions={3} | reverse | bytes 4194304 | tf_op jit(solution)/shard_map/jit(_flip)/rev | solution.py:90
  294.9 7.5 collective-permute-done.55
  324.5 9.8 %multiply_reduce_fusion = (f32[2048]{0:T(1024)}, f32[512]{0:T(512)S(1)}) fusion(f32[256,2048]{1,0:T(8,128)S(1)} %copy-done.9, f32[256,2048]{1,0:T(8,128)S(1)} %copy-done.8, bf16[256,1024]{1,0:T(8,128)(2,1)S(1)} %get-tuple-element.149, bf16[256,1024]{1,0:T(8,128)(2,1)S(1)} %get-tuple-element.148, bf16[256,1024]{1,0:T(8,128)(2,1)S(1)} %get-tuple-element.147, ...), kind=kLoop, calls=%fused_computation.21 | loop fusion | flops 14677504 | bytes 6309888 | tf_op jit(solution)/shard_map/reduce_sum | solution.py:328
  334.9 11.1 %add_convert_fusion = (bf16[512,2048]{1,0:T(8,128)(2,1)S(1)}, f32[512,2048]{1,0:T(8,128)}) fusion(bf16[4,128,2048]{2,1,0:T(8,128)(2,1)S(1)} %copy-done.6, f32[512]{0:T(512)S(1)} %get-tuple-element.167, f32[512]{0:T(512)S(1)} %bitcast.587, f32[2048]{0:T(1024)S(1)} %convert_element_type.498, f32[512]{0:T(512)S(1)} %select_reduce_fusion.2, ...), kind=kLoop, calls=%fused_computation.25 | loop fusion | flops 17825792 | bytes 14694400 | tf_op jit(solution)/shard_map/convert_element_type | solution.py:36
  389.5 5.3 fusion.69
  399.1 13.4 %multiply_convert_fusion.4 = (bf16[512,2,2,2,256]{4,3,2,1,0:T(2,128)(2,1)S(1)}, bf16[512,2,2,2,256]{4,3,2,1,0:T(2,128)(2,1)}) fusion(f32[512,2,2,2,256]{4,3,2,1,0:T(2,128)S(1)} %copy-done.14, f32[512]{0:T(512)S(1)} %select_reduce_fusion.2, f32[512]{0:T(512)S(1)} %copy-done.160, f32[256,2,2,2,256]{4,3,2,1,0:T(2,128)S(1)} %copy-done.30, ...), kind=kLoop, calls=%fused_computation.55 | loop fusion | flops 13631488 | bytes 14694400 | tf_op jit(solution)/shard_map/convert_element_type | solution.py:36
  412.5 19.4 %rev.42 = bf16[512,2,2,2,256]{4,3,2,1,0:T(2,128)(2,1)} reverse(bf16[512,2,2,2,256]{4,3,2,1,0:T(2,128)(2,1)} %get-tuple-element.55), dimensions={3} | reverse | bytes 4194304 | tf_op jit(solution)/shard_map/jit(_flip)/rev | solution.py:90
  441.8 15.1 %rev.48 = bf16[512,2,2,2,256]{4,3,2,1,0:T(2,128)(2,1)} reverse(bf16[512,2,2,2,256]{4,3,2,1,0:T(2,128)(2,1)S(1)} %get-tuple-element.54), dimensions={3} | reverse | bytes 4194304 | tf_op jit(solution)/shard_map/jit(_flip)/rev | solution.py:90
  487.0 5.0 fusion.95
  492.1 5.0 fusion.94
  514.3 19.2 %collective-permute-done.63 = bf16[512,1024]{1,0:T(8,128)(2,1)S(1)} collective-permute-done((bf16[512,1024]{1,0:T(8,128)(2,1)S(1)}, bf16[512,1024]{1,0:T(8,128)(2,1)S(1)}, u32[]{:S(2)}, u32[]{:S(2)}) %collective-permute-start.63) | collective-permute-done | bytes 1048608 | tf_op jit(solution)/shard_map/ppermute | solution.py:49
  548.6 55.0 %collective-permute-done.47 = bf16[512,4,256]{2,0,1:T(8,128)(2,1)S(1)} collective-permute-done((bf16[512,4,256]{2,0,1:T(8,128)(2,1)}, bf16[512,4,256]{2,0,1:T(8,128)(2,1)S(1)}, u32[]{:S(2)}, u32[]{:S(2)}) %collective-permute-start.47) | collective-permute-done | bytes 1048608 | tf_op jit(solution)/shard_map/ppermute | solution.py:49
  607.1 4.9 add_convert_fusion.6
  612.2 5.0 fusion.93
  632.2 20.2 %collective-permute-done.33 = bf16[2,2,128,512]{2,3,1,0:T(8,128)(2,1)} collective-permute-done((bf16[2,2,128,512]{2,3,1,0:T(8,128)(2,1)}, bf16[2,2,128,512]{2,3,1,0:T(8,128)(2,1)}, u32[]{:S(2)}, u32[]{:S(2)}) %collective-permute-start.33) | collective-permute-done | bytes 524320 | tf_op jit(solution)/shard_map/ppermute | solution.py:49
  655.4 6.3 collective-permute-done.30
  672.8 12.2 %collective-permute-done.48 = bf16[512,2,256]{2,0,1:T(8,128)(2,1)S(1)} collective-permute-done((bf16[512,2,256]{2,0,1:T(8,128)(2,1)S(1)}, bf16[512,2,256]{2,0,1:T(8,128)(2,1)S(1)}, u32[]{:S(2)}, u32[]{:S(2)}) %collective-permute-start.48) | collective-permute-done | bytes 524320 | tf_op jit(solution)/shard_map/ppermute | solution.py:49
  687.6 26.1 %collective-permute-done.34 = bf16[1,2,128,512]{2,3,1,0:T(8,128)(2,1)S(1)} collective-permute-done((bf16[1,2,128,512]{2,3,1,0:T(8,128)(2,1)S(1)}, bf16[1,2,128,512]{2,3,1,0:T(8,128)(2,1)S(1)}, u32[]{:S(2)}, u32[]{:S(2)}) %collective-permute-start.34) | collective-permute-done | bytes 262176 | tf_op jit(solution)/shard_map/ppermute | solution.py:49
  738.1 11.3 %collective-permute-done.53 = f32[256]{0:T(256)S(1)} collective-permute-done((f32[256]{0:T(256)S(1)}, f32[256]{0:T(256)S(1)}, u32[]{:S(2)}, u32[]{:S(2)}) %collective-permute-start.53) | collective-permute-done | bytes 1056 | tf_op jit(solution)/shard_map/ppermute | solution.py:49
  754.5 12.5 %collective-permute-done.54 = f32[256]{0:T(256)S(1)} collective-permute-done((f32[256]{0:T(256)S(1)}, f32[256]{0:T(256)S(1)}, u32[]{:S(2)}, u32[]{:S(2)}) %collective-permute-start.54) | collective-permute-done | bytes 1056 | tf_op jit(solution)/shard_map/ppermute | solution.py:49
  776.8 25.6 %collective-permute-done.61 = bf16[1,256,1536]{2,1,0:T(8,128)(2,1)} collective-permute-done((bf16[1,256,1536]{2,1,0:T(8,128)(2,1)}, bf16[1,256,1536]{2,1,0:T(8,128)(2,1)}, u32[]{:S(2)}, u32[]{:S(2)}) %collective-permute-start.61) | collective-permute-done | bytes 786464 | tf_op jit(solution)/shard_map/ppermute | solution.py:49
  813.3 32.1 %collective-permute-done.42 = bf16[2,256,1024]{2,1,0:T(8,128)(2,1)S(1)} collective-permute-done((bf16[2,256,1024]{2,1,0:T(8,128)(2,1)S(1)}, bf16[2,256,1024]{2,1,0:T(8,128)(2,1)S(1)}, u32[]{:S(2)}, u32[]{:S(2)}) %collective-permute-start.42) | collective-permute-done | bytes 1048608 | tf_op jit(solution)/shard_map/ppermute | solution.py:49
  850.0 14.0 %collective-permute-done.45 = bf16[2,256,512]{2,1,0:T(8,128)(2,1)S(1)} collective-permute-done((bf16[2,256,512]{2,1,0:T(8,128)(2,1)S(1)}, bf16[2,256,512]{2,1,0:T(8,128)(2,1)S(1)}, u32[]{:S(2)}, u32[]{:S(2)}) %collective-permute-start.45) | collective-permute-done | bytes 524320 | tf_op jit(solution)/shard_map/ppermute | solution.py:49
  866.1 13.6 %collective-permute-done.46 = bf16[1,256,512]{2,1,0:T(8,128)(2,1)S(1)} collective-permute-done((bf16[1,256,512]{2,1,0:T(8,128)(2,1)S(1)}, bf16[1,256,512]{2,1,0:T(8,128)(2,1)S(1)}, u32[]{:S(2)}, u32[]{:S(2)}) %collective-permute-start.46) | collective-permute-done | bytes 262176 | tf_op jit(solution)/shard_map/ppermute | solution.py:49
  (822 shorter events, 453.7 us)
Async XLA Ops:
  12.7 73.6 %collective-permute-start = (bf16[2,128,512]{2,1,0:T(8,128)(2,1)S(1)}, bf16[2,128,512]{2,1,0:T(8,128)(2,1)}, u32[]{:S(2)}, u32[]{:S(2)}) collective-permute-start(bf16[2,128,512]{2,1,0:T(8,128)(2,1)S(1)} %bitcast.562), channel_id=1, source_target_pairs={{0,4},{4,0},{8,12},{12,8},{16,20},{20,16},{24,28},{28,24},{1,5},{5... | collective-permute-start | bytes 786440 | tf_op jit(solution)/shard_map/ppermute | solution.py:49
  15.7 73.2 %collective-permute-start.1 = (bf16[2,128,512]{2,1,0:T(8,128)(2,1)S(1)}, bf16[2,128,512]{2,1,0:T(8,128)(2,1)}, u32[]{:S(2)}, u32[]{:S(2)}) collective-permute-start(bf16[2,128,512]{2,1,0:T(8,128)(2,1)S(1)} %bitcast.563), channel_id=1, source_target_pairs={{0,8},{4,12},{8,0},{12,4},{16,24},{20,28},{24,16},{28,20},{1,9},{5... | collective-permute-start | bytes 786440 | tf_op jit(solution)/shard_map/ppermute | solution.py:49
  17.3 82.4 %collective-permute-start.3 = (bf16[2,128,512]{2,1,0:T(8,128)(2,1)S(1)}, bf16[2,128,512]{2,1,0:T(8,128)(2,1)}, u32[]{:S(2)}, u32[]{:S(2)}) collective-permute-start(bf16[2,128,512]{2,1,0:T(8,128)(2,1)S(1)} %bitcast.564), channel_id=1, source_target_pairs={{0,16},{4,20},{8,24},{12,28},{16,0},{20,4},{24,8},{28,12},{1,17},{... | collective-permute-start | bytes 786440 | tf_op jit(solution)/shard_map/ppermute | solution.py:49
  19.9 80.0 %collective-permute-start.5 = (bf16[2,128,512]{2,1,0:T(8,128)(2,1)S(1)}, bf16[2,128,512]{2,1,0:T(8,128)(2,1)S(1)}, u32[]{:S(2)}, u32[]{:S(2)}) collective-permute-start(bf16[2,128,512]{2,1,0:T(8,128)(2,1)S(1)} %bitcast.565), channel_id=1, source_target_pairs={{0,24},{4,28},{8,16},{12,20},{16,8},{20,12},{24,0},{28,4},{1,25},{... | collective-permute-start | bytes 786440 | tf_op jit(solution)/shard_map/ppermute | solution.py:49
  20.3 73.8 %collective-permute-start.10 = (bf16[2,128,512]{2,1,0:T(8,128)(2,1)S(1)}, bf16[2,128,512]{2,1,0:T(8,128)(2,1)S(1)}, u32[]{:S(2)}, u32[]{:S(2)}) collective-permute-start(bf16[2,128,512]{2,1,0:T(8,128)(2,1)S(1)} %bitcast.567), channel_id=1, source_target_pairs={{0,4},{4,0},{8,12},{12,8},{16,20},{20,16},{24,28},{28,24},{1,5},{5... | collective-permute-start | bytes 786440 | tf_op jit(solution)/shard_map/ppermute | solution.py:49
  232.8 48.7 %collective-permute-start.23 = (bf16[256,1024]{1,0:T(8,128)(2,1)}, bf16[256,1024]{1,0:T(8,128)(2,1)}, u32[]{:S(2)}, u32[]{:S(2)}) collective-permute-start(bf16[256,1024]{1,0:T(8,128)(2,1)} %fusion.87), channel_id=1, source_target_pairs={{0,1},{1,0},{2,3},{3,2},{4,5},{5,4},{6,7},{7,6},{8,9},{9,8},{10,11... | collective-permute-start | bytes 1572872 | tf_op jit(solution)/shard_map/ppermute | solution.py:49
  236.4 51.0 %collective-permute-start.20 = (bf16[256,1024]{1,0:T(8,128)(2,1)}, bf16[256,1024]{1,0:T(8,128)(2,1)}, u32[]{:S(2)}, u32[]{:S(2)}) collective-permute-start(bf16[256,1024]{1,0:T(8,128)(2,1)} %fusion.90), channel_id=1, source_target_pairs={{0,1},{1,0},{2,3},{3,2},{4,5},{5,4},{6,7},{7,6},{8,9},{9,8},{10,11... | collective-permute-start | bytes 1572872 | tf_op jit(solution)/shard_map/ppermute | solution.py:49
  240.4 243.0 %collective-permute-start.56 = (bf16[512,1536]{1,0:T(8,128)(2,1)}, bf16[512,1536]{1,0:T(8,128)(2,1)}, u32[]{:S(2)}, u32[]{:S(2)}) collective-permute-start(bf16[512,1536]{1,0:T(8,128)(2,1)} %pad_maximum_fusion.10), channel_id=1, source_target_pairs={{0,4},{4,0},{8,12},{12,8},{16,20},{20,16},{24,28},{28,24},{1,5},{5... | collective-permute-start | bytes 4718600 | tf_op jit(solution)/shard_map/ppermute | solution.py:49
  276.3 215.7 %collective-permute-start.59 = (bf16[512,1536]{1,0:T(8,128)(2,1)}, bf16[512,1536]{1,0:T(8,128)(2,1)}, u32[]{:S(2)}, u32[]{:S(2)}) collective-permute-start(bf16[512,1536]{1,0:T(8,128)(2,1)} %pad_maximum_fusion.11), channel_id=1, source_target_pairs={{0,4},{4,0},{8,12},{12,8},{16,20},{20,16},{24,28},{28,24},{1,5},{5... | collective-permute-start | bytes 4718600 | tf_op jit(solution)/shard_map/ppermute | solution.py:49
  302.4 309.7 %collective-permute-start.62 = (bf16[512,1536]{1,0:T(8,128)(2,1)}, bf16[512,1536]{1,0:T(8,128)(2,1)}, u32[]{:S(2)}, u32[]{:S(2)}) collective-permute-start(bf16[512,1536]{1,0:T(8,128)(2,1)} %pad_maximum_fusion.9), channel_id=1, source_target_pairs={{0,4},{4,0},{8,12},{12,8},{16,20},{20,16},{24,28},{28,24},{1,5},{5... | collective-permute-start | bytes 4718600 | tf_op jit(solution)/shard_map/ppermute | solution.py:49
  394.8 210.2 %collective-permute-start.26 = (bf16[512,1024]{1,0:T(8,128)(2,1)}, bf16[512,1024]{1,0:T(8,128)(2,1)}, u32[]{:S(2)}, u32[]{:S(2)}) collective-permute-start(bf16[512,1024]{1,0:T(8,128)(2,1)} %fusion.69), channel_id=1, source_target_pairs={{0,1},{1,0},{2,3},{3,2},{4,5},{5,4},{6,7},{7,6},{8,9},{9,8},{10,11... | collective-permute-start | bytes 3145736 | tf_op jit(solution)/shard_map/ppermute | solution.py:49
  396.1 144.0 %collective-permute-start.32 = (bf16[4,2,128,512]{2,3,1,0:T(8,128)(2,1)}, bf16[4,2,128,512]{2,3,1,0:T(8,128)(2,1)}, u32[]{:S(2)}, u32[]{:S(2)}) collective-permute-start(bf16[4,2,128,512]{2,3,1,0:T(8,128)(2,1)} %pad_maximum_fusion.20), channel_id=1, source_target_pairs={{0,4},{4,0},{8,12},{12,8},{16,20},{20,16},{24,28},{28,24},{1,5},{5... | collective-permute-start | bytes 3145736 | tf_op jit(solution)/shard_map/ppermute | solution.py:49
  483.4 58.5 %collective-permute-start.29 = (bf16[4,2,128,512]{2,3,1,0:T(8,128)(2,1)}, bf16[4,2,128,512]{2,3,1,0:T(8,128)(2,1)}, u32[]{:S(2)}, u32[]{:S(2)}) collective-permute-start(bf16[4,2,128,512]{2,3,1,0:T(8,128)(2,1)} %pad_maximum_fusion.19), channel_id=1, source_target_pairs={{0,4},{4,0},{8,12},{12,8},{16,20},{20,16},{24,28},{28,24},{1,5},{5... | collective-permute-start | bytes 3145736 | tf_op jit(solution)/shard_map/ppermute | solution.py:49
  492.0 41.4 %collective-permute-start.63 = (bf16[512,1024]{1,0:T(8,128)(2,1)S(1)}, bf16[512,1024]{1,0:T(8,128)(2,1)S(1)}, u32[]{:S(2)}, u32[]{:S(2)}) collective-permute-start(bf16[512,1024]{1,0:T(8,128)(2,1)S(1)} %pad_maximum_fusion.28), channel_id=1, source_target_pairs={{0,4},{4,0},{8,12},{12,8},{16,20},{20,16},{24,28},{28,24},{1,5},{5... | collective-permute-start | bytes 3145736 | tf_op jit(solution)/shard_map/ppermute | solution.py:49
  533.4 234.8 %collective-permute-start.41 = (bf16[4,256,1024]{2,1,0:T(8,128)(2,1)}, bf16[4,256,1024]{2,1,0:T(8,128)(2,1)}, u32[]{:S(2)}, u32[]{:S(2)}) collective-permute-start(bf16[4,256,1024]{2,1,0:T(8,128)(2,1)} %bitcast.124), channel_id=1, source_target_pairs={{0,4},{4,0},{8,12},{12,8},{16,20},{20,16},{24,28},{28,24},{1,5},{5... | collective-permute-start | bytes 6291464 | tf_op jit(solution)/shard_map/ppermute | solution.py:49
  540.1 63.4 %collective-permute-start.47 = (bf16[512,4,256]{2,0,1:T(8,128)(2,1)}, bf16[512,4,256]{2,0,1:T(8,128)(2,1)S(1)}, u32[]{:S(2)}, u32[]{:S(2)}) collective-permute-start(bf16[512,4,256]{2,0,1:T(8,128)(2,1)} %bitcast.557), channel_id=1, source_target_pairs={{0,4},{4,0},{8,12},{12,8},{16,20},{20,16},{24,28},{28,24},{1,5},{5... | collective-permute-start | bytes 3145736 | tf_op jit(solution)/shard_map/ppermute | solution.py:49
  541.9 123.7 %collective-permute-start.57 = (bf16[2,256,1536]{2,1,0:T(8,128)(2,1)}, bf16[2,256,1536]{2,1,0:T(8,128)(2,1)}, u32[]{:S(2)}, u32[]{:S(2)}) collective-permute-start(bf16[2,256,1536]{2,1,0:T(8,128)(2,1)} %bitcast.157), channel_id=1, source_target_pairs={{0,8},{4,12},{8,0},{12,4},{16,24},{20,28},{24,16},{28,20},{1,9},{5... | collective-permute-start | bytes 4718600 | tf_op jit(solution)/shard_map/ppermute | solution.py:49
  603.5 66.0 %collective-permute-start.60 = (bf16[2,256,1536]{2,1,0:T(8,128)(2,1)}, bf16[2,256,1536]{2,1,0:T(8,128)(2,1)}, u32[]{:S(2)}, u32[]{:S(2)}) collective-permute-start(bf16[2,256,1536]{2,1,0:T(8,128)(2,1)} %bitcast.160), channel_id=1, source_target_pairs={{0,8},{4,12},{8,0},{12,4},{16,24},{20,28},{24,16},{28,20},{1,9},{5... | collective-permute-start | bytes 4718600 | tf_op jit(solution)/shard_map/ppermute | solution.py:49
  605.0 47.4 %collective-permute-start.33 = (bf16[2,2,128,512]{2,3,1,0:T(8,128)(2,1)}, bf16[2,2,128,512]{2,3,1,0:T(8,128)(2,1)}, u32[]{:S(2)}, u32[]{:S(2)}) collective-permute-start(bf16[2,2,128,512]{2,3,1,0:T(8,128)(2,1)} %pad_maximum_fusion.35), channel_id=1, source_target_pairs={{0,8},{4,12},{8,0},{12,4},{16,24},{20,28},{24,16},{28,20},{1,9},{5... | collective-permute-start | bytes 1572872 | tf_op jit(solution)/shard_map/ppermute | solution.py:49
  612.1 49.6 %collective-permute-start.30 = (bf16[2,2,128,512]{2,3,1,0:T(8,128)(2,1)}, bf16[2,2,128,512]{2,3,1,0:T(8,128)(2,1)}, u32[]{:S(2)}, u32[]{:S(2)}) collective-permute-start(bf16[2,2,128,512]{2,3,1,0:T(8,128)(2,1)} %pad_maximum_fusion.34), channel_id=1, source_target_pairs={{0,8},{4,12},{8,0},{12,4},{16,24},{20,28},{24,16},{28,20},{1,9},{5... | collective-permute-start | bytes 1572872 | tf_op jit(solution)/shard_map/ppermute | solution.py:49
  652.4 118.7 %collective-permute-start.27 = (bf16[512,1024]{1,0:T(8,128)(2,1)S(1)}, bf16[512,1024]{1,0:T(8,128)(2,1)S(1)}, u32[]{:S(2)}, u32[]{:S(2)}) collective-permute-start(bf16[512,1024]{1,0:T(8,128)(2,1)S(1)} %copy-done.83), channel_id=1, source_target_pairs={{0,2},{1,3},{2,0},{3,1},{4,6},{5,7},{6,4},{7,5},{8,10},{9,11},{10,... | collective-permute-start | bytes 3145736 | tf_op jit(solution)/shard_map/ppermute | solution.py:49
  665.6 139.3 %collective-permute-start.64 = (bf16[1536,2,256]{2,0,1:T(8,128)(2,1)S(1)}, bf16[1536,2,256]{2,0,1:T(8,128)(2,1)S(1)}, u32[]{:S(2)}, u32[]{:S(2)}) collective-permute-start(bf16[1536,2,256]{2,0,1:T(8,128)(2,1)S(1)} %copy-done.82), channel_id=1, source_target_pairs={{0,8},{4,12},{8,0},{12,4},{16,24},{20,28},{24,16},{28,20},{1,9},{5... | collective-permute-start | bytes 4718600 | tf_op jit(solution)/shard_map/ppermute | solution.py:49
  669.5 44.1 %collective-permute-start.34 = (bf16[1,2,128,512]{2,3,1,0:T(8,128)(2,1)S(1)}, bf16[1,2,128,512]{2,3,1,0:T(8,128)(2,1)S(1)}, u32[]{:S(2)}, u32[]{:S(2)}) collective-permute-start(bf16[1,2,128,512]{2,3,1,0:T(8,128)(2,1)S(1)} %add_convert_fusion.15), channel_id=1, source_target_pairs={{0,16},{4,20},{8,24},{12,28},{16,0},{20,4},{24,8},{28,12},{1,17},{... | collective-permute-start | bytes 786440 | tf_op jit(solution)/shard_map/ppermute | solution.py:49
  730.1 43.9 %collective-permute-start.58 = (bf16[1,256,1536]{2,1,0:T(8,128)(2,1)}, bf16[1,256,1536]{2,1,0:T(8,128)(2,1)}, u32[]{:S(2)}, u32[]{:S(2)}) collective-permute-start(bf16[1,256,1536]{2,1,0:T(8,128)(2,1)} %slice.743), channel_id=1, source_target_pairs={{0,16},{4,20},{8,24},{12,28},{16,0},{20,4},{24,8},{28,12},{1,17},{... | collective-permute-start | bytes 2359304 | tf_op jit(solution)/shard_map/ppermute | solution.py:49
  767.0 35.4 %collective-permute-start.61 = (bf16[1,256,1536]{2,1,0:T(8,128)(2,1)}, bf16[1,256,1536]{2,1,0:T(8,128)(2,1)}, u32[]{:S(2)}, u32[]{:S(2)}) collective-permute-start(bf16[1,256,1536]{2,1,0:T(8,128)(2,1)} %slice.742), channel_id=1, source_target_pairs={{0,16},{4,20},{8,24},{12,28},{16,0},{20,4},{24,8},{28,12},{1,17},{... | collective-permute-start | bytes 2359304 | tf_op jit(solution)/shard_map/ppermute | solution.py:49
  768.2 39.0 %collective-permute-start.35 = (bf16[512,1024]{1,0:T(8,128)(2,1)}, bf16[512,1024]{1,0:T(8,128)(2,1)}, u32[]{:S(2)}, u32[]{:S(2)}) collective-permute-start(bf16[512,1024]{1,0:T(8,128)(2,1)} %add_convert_fusion.4), channel_id=1, source_target_pairs={{0,1},{1,0},{2,3},{3,2},{4,5},{5,4},{6,7},{7,6},{8,9},{9,8},{10,11... | collective-permute-start | bytes 3145736 | tf_op jit(solution)/shard_map/ppermute | solution.py:49
  772.2 39.1 %collective-permute-start.44 = (bf16[4,256,512]{2,1,0:T(8,128)(2,1)S(1)}, bf16[4,256,512]{2,1,0:T(8,128)(2,1)S(1)}, u32[]{:S(2)}, u32[]{:S(2)}) collective-permute-start(bf16[4,256,512]{2,1,0:T(8,128)(2,1)S(1)} %bitcast.604), channel_id=1, source_target_pairs={{0,4},{4,0},{8,12},{12,8},{16,20},{20,16},{24,28},{28,24},{1,5},{5... | collective-permute-start | bytes 3145736 | tf_op jit(solution)/shard_map/ppermute | solution.py:49
  774.0 71.9 %collective-permute-start.28 = (bf16[512,1024]{1,0:T(8,128)(2,1)S(1)}, bf16[512,1024]{1,0:T(8,128)(2,1)S(1)}, u32[]{:S(2)}, u32[]{:S(2)}) collective-permute-start(bf16[512,1024]{1,0:T(8,128)(2,1)S(1)} %add_convert_fusion.5), channel_id=1, source_target_pairs={{0,1},{1,0},{2,3},{3,2},{4,5},{5,4},{6,7},{7,6},{8,9},{9,8},{10,11... | collective-permute-start | bytes 3145736 | tf_op jit(solution)/shard_map/ppermute | solution.py:49
  802.4 42.9 %collective-permute-start.42 = (bf16[2,256,1024]{2,1,0:T(8,128)(2,1)S(1)}, bf16[2,256,1024]{2,1,0:T(8,128)(2,1)S(1)}, u32[]{:S(2)}, u32[]{:S(2)}) collective-permute-start(bf16[2,256,1024]{2,1,0:T(8,128)(2,1)S(1)} %pad_maximum_fusion.24), channel_id=1, source_target_pairs={{0,8},{4,12},{8,0},{12,4},{16,24},{20,28},{24,16},{28,20},{1,9},{5... | collective-permute-start | bytes 3145736 | tf_op jit(solution)/shard_map/ppermute | solution.py:49
  805.4 59.4 %collective-permute-start.65 = (bf16[1536,1,256]{2,0,1:T(8,128)(2,1)S(1)}, bf16[1536,1,256]{2,0,1:T(8,128)(2,1)S(1)}, u32[]{:S(2)}, u32[]{:S(2)}) collective-permute-start(bf16[1536,1,256]{2,0,1:T(8,128)(2,1)S(1)} %slice.741), channel_id=1, source_target_pairs={{0,16},{4,20},{8,24},{12,28},{16,0},{20,4},{24,8},{28,12},{1,17},{... | collective-permute-start | bytes 2359304 | tf_op jit(solution)/shard_map/ppermute | solution.py:49
  809.7 54.6 %collective-permute-start.36 = (bf16[512,1024]{1,0:T(8,128)(2,1)S(1)}, bf16[512,1024]{1,0:T(8,128)(2,1)S(1)}, u32[]{:S(2)}, u32[]{:S(2)}) collective-permute-start(bf16[512,1024]{1,0:T(8,128)(2,1)S(1)} %add_convert_fusion.3), channel_id=1, source_target_pairs={{0,2},{1,3},{2,0},{3,1},{4,6},{5,7},{6,4},{7,5},{8,10},{9,11},{10,... | collective-permute-start | bytes 3145736 | tf_op jit(solution)/shard_map/ppermute | solution.py:49
  811.8 52.2 %collective-permute-start.45 = (bf16[2,256,512]{2,1,0:T(8,128)(2,1)S(1)}, bf16[2,256,512]{2,1,0:T(8,128)(2,1)S(1)}, u32[]{:S(2)}, u32[]{:S(2)}) collective-permute-start(bf16[2,256,512]{2,1,0:T(8,128)(2,1)S(1)} %pad_maximum_fusion.38), channel_id=1, source_target_pairs={{0,8},{4,12},{8,0},{12,4},{16,24},{20,28},{24,16},{28,20},{1,9},{5... | collective-permute-start | bytes 1572872 | tf_op jit(solution)/shard_map/ppermute | solution.py:49
  (234 other events, 2219.7 us)

commit v2 on v0

--- a/solution.py
+++ b/solution.py
@@ -1,9 +1,12 @@
 import jax
 import jax.numpy as jnp
 from jax import lax
+from jax.experimental import pallas as pl
+from jax.experimental.pallas import tpu as pltpu
 from jax.sharding import PartitionSpec as P
 
 epsilon = 1e-06
+CHUNKS = 2
 
 
 def norm_scale(value):
@@ -31,8 +34,25 @@
     )
 
 
-def positions(block_order, first_row, row_count, block_rows):
-    stored = first_row + jnp.arange(row_count, dtype=jnp.int32)
+def low(value):
+    return value.astype(jnp.bfloat16)
+
+
+def wide(value):
+    return value.astype(jnp.float32)
+
+
+def bits_of(axis):
+    return (lax.axis_size(axis) - 1).bit_length()
+
+
+def swap(value, axis, mask):
+    size = lax.axis_size(axis)
+    return lax.ppermute(value, axis, [(i, i ^ mask) for i in range(size)])
+
+
+def positions(block_order, device, row_count, block_rows):
+    stored = device * row_count + jnp.arange(row_count, dtype=jnp.int32)
     slots = stored // block_rows
     slot_index = jnp.arange(block_order.shape[0], dtype=jnp.int32)
     picked = jnp.sum(
@@ -41,7 +61,1091 @@
     return picked * block_rows + stored % block_rows
 
 
+def head_sum(left, weight, apply, cut):
+    mine = lax.axis_index("head") & 1
+    away = low(apply(left, cut(weight, 1 - mine)))
+    got = swap(away, "head", 1)
+    total = apply(left, cut(weight, mine)) + wide(got)
+    for bit in range(1, bits_of("head")):
+        part = low(total)
+        total = wide(part) + wide(swap(part, "head", 1 << bit))
+    part = low(total)
+    other = swap(part, "head", 1)
+    low_half = jnp.where(mine == 0, part, other)
+    high_half = jnp.where(mine == 0, other, part)
+    return wide(jnp.concatenate([low_half, high_half], axis=1))
+
+
+MESH = pl.DeviceIdType.MESH
+TILE = 256
+
+
+def other_z(z, t):
+    low_z, high_z = lax.rem(z, 2), lax.div(z, 2)
+    low_t, high_t = lax.rem(t, 2), lax.div(t, 2)
+    return (low_z + low_t - 2 * low_z * low_t) + 2 * (high_z + high_t - 2 * high_z * high_t)
+
+
+def dot_plain(left, right):
+    return jnp.dot(left, right, preferred_element_type=jnp.float32)
+
+
+def dot_rows(left, right):
+    return lax.dot_general(
+        left, right, (((1,), (1,)), ((), ())), preferred_element_type=jnp.float32
+    )
+
+
+def dot_first(left, right):
+    return lax.dot_general(
+        left, right, (((0,), (0,)), ((), ())), preferred_element_type=jnp.float32
+    )
+
+
+def back_kernel(
+    h_hbm, cot_hbm, x_hbm, xt_hbm, q_hbm, kv_hbm, o_hbm, sig_hbm, y_hbm, qraw_hbm, kraw_hbm,
+    wg_hbm, wu_hbm, wd_hbm, wo_hbm, wq_hbm, wk_hbm, wv_hbm, wga_hbm,
+    factor_ref, lse_ref, kpos_ref, qpos_ref, n1_ref, n2_ref, qg_ref, kg_ref,
+    block_out, x_out, items_out, norms_out, gains_out, dh_hbm, zlo_hbm, zhi_hbm,
+    acts, lt, odd, csend, crecv, xrecv, fin, yrecv, lrecv, hrecv,
+    zlo_send, zhi_send, stage, ostage, wide_a, wide_b, delta,
+    vec, vec_got, gvec, gvec_got,
+    ya_s, ya_r, zl_s, zl_r, zh_s, zh_r, lt_s, lt_r, lc_s, lc_r,
+    c1_s, c1_r, x_s, x_r, c2_s, c2_r, ky_s, ky_r, kl_s, kl_r, kh_s, kh_r,
+    nv_s, nv_r, gv_s, gv_r, st_sem, out_sem, misc, credit,
+):
+    seq, head = lax.axis_index("seq"), lax.axis_index("head")
+    z, y = lax.div(seq, 2), lax.rem(seq, 2)
+    c = lax.rem(head, 2)
+    y_dev = {"seq": z * 2 + 1 - y}
+    lo_dev = {"seq": other_z(z, 1) * 2 + y}
+    hi_dev = {"seq": other_z(z, 2) * 2 + y}
+    core_dev = {"head": head + 1 - 2 * c}
+    x_dev = {"head": head + 2 - 4 * lax.div(head, 2)}
+    tokens = cot_hbm.shape[0]
+    rows = kpos_ref.shape[0] // 8
+    seqs = tokens // rows
+    hidden_tiles = wd_hbm.shape[0] // TILE
+    ff_items = 3 * hidden_tiles
+    width = cot_hbm.shape[1]
+    epsilon_k = 1e-06
+
+    barrier = pltpu.get_barrier_semaphore()
+    for device in (y_dev, lo_dev, hi_dev, core_dev, x_dev):
+        pl.semaphore_signal(barrier, inc=1, device_id=device, device_id_type=MESH)
+    pl.semaphore_wait(barrier, 5)
+
+    def remote(src, dst, send, recv, device):
+        return pltpu.make_async_remote_copy(
+            src_ref=src, dst_ref=dst, send_sem=send, recv_sem=recv, device_id=device, device_id_type=MESH
+        )
+
+    def act_copy(i):
+        return remote(acts.at[i, 0], acts.at[i, 1], ya_s.at[i], ya_r.at[i], y_dev)
+
+    def lt_copy(l):
+        return remote(odd.at[l], lt.at[l, 1, pl.ds(2 * c, 2)], lt_s.at[l], lt_r.at[l], y_dev)
+
+    def lt_relay(l):
+        piece = lt.at[l, 1, pl.ds(2 * c, 2)]
+        return remote(piece, piece, lc_s.at[l], lc_r.at[l], core_dev)
+
+    def lt_relay_in(l):
+        piece = lt.at[l, 1, pl.ds(2 - 2 * c, 2)]
+        return remote(piece, piece, lc_s.at[l], lc_r.at[l], core_dev)
+
+    def zlo_copy(i):
+        return remote(zlo_send.at[lax.rem(i, 4)], zlo_hbm.at[i], zl_s.at[i], zl_r.at[i], lo_dev)
+
+    def zhi_copy(i):
+        return remote(zhi_send.at[lax.rem(i, 4)], zhi_hbm.at[i], zh_s.at[i], zh_r.at[i], hi_dev)
+
+    def item_dot(i, l, t):
+        return dot_plain(lt[l, 0, t], acts[i, 0]) + dot_plain(lt[l, 1, t], acts[i, 1])
+
+    def stage_one(first, last, l_of):
+        @pl.loop(first, last)
+        def _(i):
+            l = l_of(i)
+            act_copy(i).wait_recv()
+
+            @pl.when(i >= 4)
+            def _():
+                zlo_copy(i - 4).wait_send()
+
+            slot = lax.rem(i, 4)
+            for k in range(2):
+                zlo_send[slot, k] = low(item_dot(i, l, 2 * k + 1))
+            zlo_copy(i).start()
+
+    def stage_two(first, last, l_of):
+        @pl.loop(first, last)
+        def _(i):
+            l = l_of(i)
+            zlo_copy(i).wait_recv()
+            here = pltpu.make_async_copy(zlo_hbm.at[i, 1], stage.at[0], st_sem.at[0])
+            here.start()
+
+            @pl.when(i >= 4)
+            def _():
+                zhi_copy(i - 4).wait_send()
+
+            total = item_dot(i, l, 2)
+            here.wait()
+            zhi_send[lax.rem(i, 4)] = low(total + wide(stage[0]))
+            zhi_copy(i).start()
+
+    def out_copy(i):
+        slot = lax.rem(i, 2)
+        return pltpu.make_async_copy(ostage.at[slot], items_out.at[i], out_sem.at[slot])
+
+    def stage_three(first, last, l_of):
+        @pl.loop(first, last)
+        def _(i):
+            l = l_of(i)
+            zhi_copy(i).wait_recv()
+            one = pltpu.make_async_copy(zlo_hbm.at[i, 0], stage.at[0], st_sem.at[0])
+            two = pltpu.make_async_copy(zhi_hbm.at[i], stage.at[1], st_sem.at[1])
+            one.start()
+            two.start()
+
+            @pl.when(i >= 2)
+            def _():
+                out_copy(i - 2).wait()
+
+            total = item_dot(i, l, 0)
+            one.wait()
+            two.wait()
+            ostage[lax.rem(i, 2)] = total + wide(stage[0]) + wide(stage[1])
+            out_copy(i).start()
+
+    def ff_l(i):
+        return 1 - lax.div(lax.rem(i, 3) + 1, 2)
+
+    def const_l(l):
+        return lambda i: l
+
+    def back(stages):
+        for stage_of, first, last in stages:
+            for a, b, l_of in (
+                (0, ff_items, ff_l),
+                (ff_items, ff_items + 2, const_l(2)),
+                (ff_items + 2, ff_items + 4, const_l(3)),
+                (ff_items + 4, ff_items + 8, const_l(2)),
+            ):
+                lo_i, hi_i = max(first, a), min(last, b)
+                if lo_i < hi_i:
+                    stage_of(lo_i, hi_i, l_of)
+
+    def spread(l, source):
+        @pl.loop(0, 4)
+        def _(t):
+            at = pl.multiple_of((other_z(z, t) * 2 + y) * TILE, TILE)
+            lt[l, 0, t] = source[:, pl.ds(at, TILE)].T
+
+        @pl.loop(0, 2)
+        def _(k):
+            at = pl.multiple_of((other_z(z, 2 * c + k) * 2 + 1 - y) * TILE, TILE)
+            odd[l, k] = source[:, pl.ds(at, TILE)].T
+
+        lt_copy(l).start()
+
+    def relay(l):
+        lt_copy(l).wait_recv()
+        lt_relay(l).start()
+
+    def core_copy(k, b):
+        return remote(csend.at[b], crecv.at[k % 2, b], c1_s.at[k, b], c1_r.at[k, b], core_dev)
+
+    def x_copy(k, b):
+        return remote(fin.at[k % 2, c * 4 + b], xrecv.at[k % 2, b], x_s.at[k, b], x_r.at[k, b], x_dev)
+
+    def fin_copy(k, b):
+        piece = fin.at[k % 2, c * 4 + b]
+        return remote(piece, piece, c2_s.at[k, b], c2_r.at[k, b], core_dev)
+
+    def fin_copy_in(k, b):
+        piece = fin.at[k % 2, (1 - c) * 4 + b]
+        return remote(piece, piece, c2_s.at[k, b], c2_r.at[k, b], core_dev)
+
+    def reduce_start(k, loads, compute):
+        def block_of(step):
+            return lax.rem(c + 1 + step, 2) * 4 + lax.div(step, 2)
+
+        for copy in loads(block_of(0), 0):
+            copy.start()
+
+        @pl.loop(0, 8)
+        def _(step):
+            slot, b = lax.rem(step, 2), lax.div(step, 2)
+
+            @pl.when(step < 7)
+            def _():
+                for copy in loads(block_of(step + 1), 1 - slot):
+                    copy.start()
+
+            for copy in loads(block_of(step), slot):
+                copy.wait()
+            part = compute(slot)
+
+            @pl.when(slot == 0)
+            def _():
+                csend[b] = low(part)
+                core_copy(k, b).start()
+
+            @pl.when(slot == 1)
+            def _():
+                core_copy(k, b).wait_recv()
+                fin[k % 2, c * 4 + b] = low(part + wide(crecv[k % 2, b]))
+                x_copy(k, b).start()
+
+        @pl.loop(0, 4)
+        def _(b):
+            core_copy(k, b).wait_send()
+
+    def reduce_end(k):
+        @pl.loop(0, 4)
+        def _(b):
+            x_copy(k, b).wait()
+            fin[k % 2, c * 4 + b] = low(wide(fin[k % 2, c * 4 + b]) + wide(xrecv[k % 2, b]))
+            fin_copy(k, b).start()
+
+        @pl.loop(0, 4)
+        def _(b):
+            fin_copy_in(k, b).wait_recv()
+            fin_copy(k, b).wait_send()
+
+    def fin_rows(k, at, count):
+        return jnp.concatenate([wide(fin[k % 2, n, pl.ds(at, count)]) for n in range(8)], axis=1)
+
+    def rms(value):
+        return lax.rsqrt(jnp.mean(value * value, axis=-1, keepdims=True) + epsilon_k)
+
+    n_chunks = tokens // 128
+
+    def first_phase(hbuf, cbuf, wgb, wub, wdb, sems, w_sems):
+        def row_loads(r, slot):
+            at = pl.ds(r * 128, 128)
+            return (
+                pltpu.make_async_copy(h_hbm.at[at], hbuf.at[slot], sems.at[slot, 0]),
+                pltpu.make_async_copy(cot_hbm.at[at], cbuf.at[slot], sems.at[slot, 1]),
+            )
+
+        def tile_loads(j, slot):
+            at = pl.ds(pl.multiple_of(j * TILE, TILE), TILE)
+            return (
+                pltpu.make_async_copy(wg_hbm.at[:, at], wgb.at[slot], w_sems.at[slot, 0]),
+                pltpu.make_async_copy(wu_hbm.at[:, at], wub.at[slot], w_sems.at[slot, 1]),
+                pltpu.make_async_copy(wd_hbm.at[at], wdb.at[slot], w_sems.at[slot, 2]),
+            )
+
+        for copy in row_loads(0, 0):
+            copy.start()
+        for copy in tile_loads(0, 0):
+            copy.start()
+
+        @pl.loop(0, n_chunks)
+        def _(r):
+            slot = lax.rem(r, 2)
+
+            @pl.when(r < n_chunks - 1)
+            def _():
+                for copy in row_loads(r + 1, 1 - slot):
+                    copy.start()
+
+            for copy in row_loads(r, slot):
+                copy.wait()
+            value = hbuf[slot]
+            at = pl.ds(pl.multiple_of(r * 128, 128), 128)
+            wide_a[at] = low(value * rms(value) * n2_ref[...])
+            wide_b[at] = low(wide(cbuf[slot]) * factor_ref[at])
+
+        @pl.loop(0, hidden_tiles)
+        def _(j):
+            slot = lax.rem(j, 2)
+
+            @pl.when(j < hidden_tiles - 1)
+            def _():
+                for copy in tile_loads(j + 1, 1 - slot):
+                    copy.start()
+
+            for copy in tile_loads(j, slot):
+                copy.wait()
+
+            @pl.loop(0, 2)
+            def _(half):
+                at = pl.ds(pl.multiple_of(half * (tokens // 2), 128), tokens // 2)
+                a = dot_plain(wide_a[at], wgb[slot])
+                u = dot_plain(wide_a[at], wub[slot])
+                dm = dot_rows(wide_b[at], wdb[slot])
+                sig = jax.nn.sigmoid(a)
+                act = a * sig
+                acts[3 * j, 0, at] = low(act * u)
+                acts[3 * j + 1, 0, at] = low(dm * u * sig * (1.0 + a * (1.0 - sig)))
+                acts[3 * j + 2, 0, at] = low(dm * act)
+
+            for k in range(3):
+                act_copy(3 * j + k).start()
+
+            @pl.when(j == 0)
+            def _():
+                spread(1, wide_b)
+                spread(0, wide_a)
+
+    pl.run_scoped(
+        first_phase,
+        pltpu.VMEM((2, 128, width), jnp.float32),
+        pltpu.VMEM((2, 128, width), jnp.bfloat16),
+        pltpu.VMEM((2, width, TILE), jnp.bfloat16),
+        pltpu.VMEM((2, width, TILE), jnp.bfloat16),
+        pltpu.VMEM((2, TILE, width), jnp.bfloat16),
+        pltpu.SemaphoreType.DMA((2, 2)),
+        pltpu.SemaphoreType.DMA((2, 3)),
+    )
+
+    def second_phase(wa, wb, sems):
+        def loads(n, slot):
+            at = pl.ds(pl.multiple_of(n * TILE, TILE), TILE)
+            return (
+                pltpu.make_async_copy(wg_hbm.at[at], wa.at[slot], sems.at[slot, 0]),
+                pltpu.make_async_copy(wu_hbm.at[at], wb.at[slot], sems.at[slot, 1]),
+            )
+
+        def compute(slot):
+            total = None
+            for j in range(hidden_tiles):
+                at = pl.ds(j * TILE, TILE)
+                part = dot_rows(acts[3 * j + 1, 0], wa[slot, :, at])
+                part += dot_rows(acts[3 * j + 2, 0], wb[slot, :, at])
+                total = part if total is None else total + part
+            return total
+
+        reduce_start(0, loads, compute)
+
+    pl.run_scoped(
+        second_phase,
+        pltpu.VMEM((2, TILE, wg_hbm.shape[1]), jnp.bfloat16),
+        pltpu.VMEM((2, TILE, wg_hbm.shape[1]), jnp.bfloat16),
+        pltpu.SemaphoreType.DMA((2, 2)),
+    )
+
+    def third_phase(wa, sems):
+        def loads(n, slot):
+            at = pl.ds(pl.multiple_of(n * TILE, TILE), TILE)
+            return (pltpu.make_async_copy(wd_hbm.at[:, at], wa.at[slot], sems.at[slot]),)
+
+        def compute(slot):
+            total = None
+            for j in range(hidden_tiles):
+                part = dot_plain(acts[3 * j, 0], wa[slot, pl.ds(j * TILE, TILE)])
+                total = part if total is None else total + part
+            return total
+
+        reduce_start(1, loads, compute)
+
+    pl.run_scoped(
+        third_phase,
+        pltpu.VMEM((2, wd_hbm.shape[0], TILE), jnp.bfloat16),
+        pltpu.SemaphoreType.DMA((2,)),
+    )
+
+    base = ff_items
+    for n in range(2):
+        pltpu.make_async_copy(
+            y_hbm.at[:, pl.ds(n * TILE, TILE)], acts.at[base + 2 + n, 0], misc.at[n]
+        ).start()
+
+    def xt_own(t):
+        shard = other_z(z, t) * 2 + y
+        return pltpu.make_async_copy(xt_hbm.at[shard], lt.at[2, 0, t], misc.at[2 + t])
+
+    def xt_odd(k):
+        shard = other_z(z, 2 * c + k) * 2 + 1 - y
+        return pltpu.make_async_copy(xt_hbm.at[shard], odd.at[2, k], misc.at[6 + k])
+
+    for t in range(4):
+        xt_own(t).start()
+    for k in range(2):
+        xt_odd(k).start()
+    relay(1)
+    relay(0)
+    lt_relay_in(1).wait_recv()
+    lt_relay_in(0).wait_recv()
+    back([(stage_one, 0, 6)])
+    for t in range(4):
+        xt_own(t).wait()
+    for k in range(2):
+        xt_odd(k).wait()
+    lt_copy(2).start()
+    for n in range(2):
+        pltpu.make_async_copy(
+            y_hbm.at[:, pl.ds(n * TILE, TILE)], acts.at[base + 2 + n, 0], misc.at[n]
+        ).wait()
+        act_copy(base + 2 + n).start()
+
+    reduce_end(0)
+
+    def fourth_phase(hbuf, cbuf, dbuf, wob, obuf, sbuf, sems, d_sems, w_sems):
+        def row_loads(r, slot):
+            at = pl.ds(r * 128, 128)
+            return (
+                pltpu.make_async_copy(h_hbm.at[at], hbuf.at[slot], sems.at[slot, 0]),
+                pltpu.make_async_copy(cot_hbm.at[at], cbuf.at[slot], sems.at[slot, 1]),
+            )
+
+        def spill(r, slot):
+            return pltpu.make_async_copy(dbuf.at[slot], dh_hbm.at[pl.ds(r * 128, 128)], d_sems.at[slot])
+
+        def tile_loads(n):
+            at = pl.ds(n * TILE, TILE)
+            return (
+                pltpu.make_async_copy(wo_hbm.at[at], wob.at[n], w_sems.at[n, 0]),
+                pltpu.make_async_copy(o_hbm.at[:, at], obuf.at[n], w_sems.at[n, 1]),
+                pltpu.make_async_copy(sig_hbm.at[:, at], sbuf.at[n], w_sems.at[n, 2]),
+            )
+
+        for copy in row_loads(0, 0):
+            copy.start()
+        for n in range(2):
+            for copy in tile_loads(n):
+                copy.start()
+        vec[0] = jnp.zeros_like(vec[0])
+
+        @pl.loop(0, n_chunks)
+        def _(r):
+            slot = lax.rem(r, 2)
+
+            @pl.when(r < n_chunks - 1)
+            def _():
+                for copy in row_loads(r + 1, 1 - slot):
+                    copy.start()
+
+            for copy in row_loads(r, slot):
+                copy.wait()
+
+            @pl.when(r >= 2)
+            def _():
+                spill(r - 2, slot).wait()
+
+            at = pl.ds(pl.multiple_of(r * 128, 128), 128)
+            value = hbuf[slot]
+            scale = rms(value)
+            normed = value * scale
+            grad = fin_rows(0, pl.multiple_of(r * 128, 128), 128)
+            vec[0, 1:2] += jnp.sum(grad * normed, axis=0, keepdims=True)
+            scaled = grad * n2_ref[...]
+            inner = jnp.mean(scaled * normed, axis=-1, keepdims=True)
+            dh = wide(cbuf[slot]) * factor_ref[at] + scale * (scaled - normed * inner)
+            dbuf[slot] = dh
+            wide_a[at] = low(dh)
+            spill(r, slot).start()
+
+        spill(n_chunks - 2, n_chunks % 2).wait()
+        spill(n_chunks - 1, (n_chunks - 1) % 2).wait()
+
+        ones = jnp.ones((8, 128), jnp.bfloat16)
+        for n in range(2):
+            for copy in tile_loads(n):
+                copy.wait()
+            dy = dot_rows(wide_a[...], wob[n])
+            sig, o = sbuf[n], obuf[n]
+            do = low(dy * sig)
+            acts[base + n, 0] = low(dy * o * sig * (1.0 - sig))
+            act_copy(base + n).start()
+            wide_b[:, n * TILE : (n + 1) * TILE] = do
+            both = wide(do) * o
+            for g in range(2):
+                part = both[:, g * 128 : (g + 1) * 128]
+                top = low(part)
+                rest = low(part - wide(top))
+                delta[n, g] = dot_rows(ones, top) + dot_rows(ones, rest)
+
+        spread(3, wide_a)
+        for device in (core_dev, x_dev):
+            pl.semaphore_signal(credit, inc=1, device_id=device, device_id_type=MESH)
+
+    pl.run_scoped(
+        fourth_phase,
+        pltpu.VMEM((2, 128, width), jnp.float32),
+        pltpu.VMEM((2, 128, width), jnp.bfloat16),
+        pltpu.VMEM((2, 128, width), jnp.float32),
+        pltpu.VMEM((2, TILE, width), jnp.bfloat16),
+        pltpu.VMEM((2, tokens, TILE), jnp.float32),
+        pltpu.VMEM((2, tokens, TILE), jnp.float32),
+        pltpu.SemaphoreType.DMA((2, 2)),
+        pltpu.SemaphoreType.DMA((2,)),
+        pltpu.SemaphoreType.DMA((2, 3)),
+    )
+
+    def attention_back(keep, ysend, lsend, hsend, dq_ref, dkv_ref):
+        def ky_copy(s):
+            return remote(ysend.at[lax.rem(s, 2)], yrecv.at[s], ky_s.at[s], ky_r.at[s], y_dev)
+
+        def kl_copy(s):
+            return remote(lsend.at[s], lrecv.at[s], kl_s.at[s], kl_r.at[s], lo_dev)
+
+        def kh_copy(s):
+            return remote(hsend.at[s], hrecv.at[s], kh_s.at[s], kh_r.at[s], hi_dev)
+
+        keys_total = kpos_ref.shape[0]
+
+        def fifth_phase(qbuf, kvbuf, q_sem, sems):
+            def kv_load(s, slot):
+                return pltpu.make_async_copy(kv_hbm.at[s], kvbuf.at[slot], sems.at[slot])
+
+            q_load = pltpu.make_async_copy(q_hbm, qbuf, q_sem)
+            q_load.start()
+            kv_load(0, 0).start()
+            q_load.wait()
+
+            @pl.loop(0, seqs)
+            def _(s):
+                slot = lax.rem(s, 2)
+
+                @pl.when(s < seqs - 1)
+                def _():
+                    kv_load(s + 1, 1 - slot).start()
+
+                kv_load(s, slot).wait()
+                at = pl.ds(pl.multiple_of(s * rows, 128), rows)
+                @pl.when(s >= 2)
+                def _():
+                    ky_copy(s - 2).wait_send()
+
+                allowed = kpos_ref[...] <= qpos_ref[...]
+                for n in range(2):
+                    lanes = [slice((2 * n + g) * 128, (2 * n + g + 1) * 128) for g in range(2)]
+                    key = kvbuf[slot, :, n * 128 : (n + 1) * 128]
+                    value = kvbuf[slot, :, 256 + n * 128 : 256 + (n + 1) * 128]
+                    q = jnp.concatenate([qbuf[at, lane] for lane in lanes], axis=0)
+                    do = jnp.concatenate([wide_b[at, lane] for lane in lanes], axis=0)
+                    drow = jnp.concatenate([delta[n, g, 0:1, at] for g in range(2)], axis=1)
+                    scores = dot_rows(key, q)
+                    probs = jnp.exp(jnp.where(allowed, scores - lse_ref[s, n], -1e30))
+                    grad_probs = dot_rows(value, do)
+                    ds = low(probs * (grad_probs - drow))
+                    for start, grad in ((0, dot_plain(ds, q)), (256, dot_plain(low(probs), do))):
+                        into = slice(start + n * 128, start + (n + 1) * 128)
+                        for m in range(4):
+                            keep[s, m, :, into] = grad[2 * m * rows : (2 * m + 1) * rows]
+                            ysend[slot, m, :, into] = low(grad[(2 * m + 1) * rows : (2 * m + 2) * rows])
+                    dq = dot_first(key, ds).T
+                    for g in range(2):
+                        dq_ref[at, lanes[g]] = dq[g * rows : (g + 1) * rows]
+
+                ky_copy(s).start()
+
+        pl.run_scoped(
+            fifth_phase,
+            pltpu.VMEM(q_hbm.shape, jnp.bfloat16),
+            pltpu.VMEM((2, keys_total, 512), jnp.bfloat16),
+            pltpu.SemaphoreType.DMA,
+            pltpu.SemaphoreType.DMA((2,)),
+        )
+
+        relay(2)
+        relay(3)
+        back([(stage_two, 0, 4)])
+
+        @pl.loop(0, seqs)
+        def _(s):
+            ky_copy(s).wait_recv()
+            for m in range(4):
+                keep[s, m] += wide(yrecv[s, m])
+            for k in range(2):
+                lsend[s, k] = low(keep[s, 2 * k + 1])
+            kl_copy(s).start()
+
+        back([(stage_one, 6, 9)])
+
+        def query_phase(rbuf, sem):
+            load = pltpu.make_async_copy(qraw_hbm, rbuf, sem)
+            load.start()
+            load.wait()
+            factor = 128.0**-0.5
+            for hd in range(4):
+                lane = slice(hd * 128, (hd + 1) * 128)
+                raw = rbuf[:, lane]
+                scale = rms(raw)
+                normed = raw * scale
+                grad = dq_ref[:, lane]
+                gvec[0, 0:1, 0:128] = (
+                    jnp.sum(grad * normed * factor, axis=0, keepdims=True)
+                    + (gvec[0, 0:1, 0:128] if hd else 0.0)
+                )
+                scaled = grad * (qg_ref[...] * factor)
+                out = scale * (scaled - normed * jnp.mean(scaled * normed, axis=-1, keepdims=True))
+                acts[base + 4 + hd // 2, 0, :, (hd % 2) * 128 : (hd % 2 + 1) * 128] = low(out)
+            for n in range(2):
+                act_copy(base + 4 + n).start()
+
+        gvec[0] = jnp.zeros_like(gvec[0])
+        pl.run_scoped(query_phase, pltpu.VMEM(qraw_hbm.shape, jnp.float32), pltpu.SemaphoreType.DMA)
+
+        @pl.loop(0, seqs)
+        def _(s):
+            kl_copy(s).wait_recv()
+            for k in range(2):
+                keep[s, 2 * k] += wide(lrecv[s, k])
+            hsend[s] = low(keep[s, 2])
+            kh_copy(s).start()
+
+        reduce_end(1)
+
+        def out_phase(hbuf, obuf, sems, o_sems):
+            def load(r, slot):
+                return pltpu.make_async_copy(h_hbm.at[pl.ds(r * 128, 128)], hbuf.at[slot], sems.at[slot])
+
+            def store(r, slot):
+                return pltpu.make_async_copy(obuf.at[slot], block_out.at[pl.ds(r * 128, 128)], o_sems.at[slot])
+
+            load(0, 0).start()
+
+            @pl.loop(0, n_chunks)
+            def _(r):
+                slot = lax.rem(r, 2)
+
+                @pl.when(r < n_chunks - 1)
+                def _():
+                    load(r + 1, 1 - slot).start()
+
+                load(r, slot).wait()
+
+                @pl.when(r >= 2)
+                def _():
+                    store(r - 2, slot).wait()
+
+                obuf[slot] = low(hbuf[slot] + fin_rows(1, pl.multiple_of(r * 128, 128), 128))
+                store(r, slot).start()
+
+            store(n_chunks - 2, n_chunks % 2).wait()
+            store(n_chunks - 1, (n_chunks - 1) % 2).wait()
+
+        pl.run_scoped(
+            out_phase,
+            pltpu.VMEM((2, 128, width), jnp.float32),
+            pltpu.VMEM((2, 128, width), jnp.bfloat16),
+            pltpu.SemaphoreType.DMA((2,)),
+            pltpu.SemaphoreType.DMA((2,)),
+        )
+
+        @pl.loop(0, seqs)
+        def _(s):
+            kh_copy(s).wait_recv()
+            dkv_ref[pl.ds(pl.multiple_of(s * rows, 128), rows)] = keep[s, 0] + wide(hrecv[s])
+
+        def key_phase(rbuf, sem):
+            load = pltpu.make_async_copy(kraw_hbm, rbuf, sem)
+            load.start()
+            load.wait()
+            for hd in range(2):
+                lane = slice(hd * 128, (hd + 1) * 128)
+                raw = rbuf[:, lane]
+                scale = rms(raw)
+                normed = raw * scale
+                grad = dkv_ref[:, lane]
+                gvec[0, 0:1, 128:256] = (
+                    jnp.sum(grad * normed, axis=0, keepdims=True)
+                    + (gvec[0, 0:1, 128:256] if hd else 0.0)
+                )
+                scaled = grad * kg_ref[...]
+                out = scale * (scaled - normed * jnp.mean(scaled * normed, axis=-1, keepdims=True))
+                acts[base + 6, 0, :, lane] = low(out)
+            acts[base + 7, 0] = low(dkv_ref[:, 256:512])
+            for n in range(2):
+                act_copy(base + 6 + n).start()
+
+        pl.run_scoped(key_phase, pltpu.VMEM(kraw_hbm.shape, jnp.float32), pltpu.SemaphoreType.DMA)
+
+        @pl.loop(seqs - 2, seqs)
+        def _(s):
+            ky_copy(s).wait_send()
+
+        @pl.loop(0, seqs)
+        def _(s):
+            kl_copy(s).wait_send()
+            kh_copy(s).wait_send()
+
+    pl.run_scoped(
+        attention_back,
+        pltpu.VMEM((seqs, 4, rows, 512), jnp.float32),
+        pltpu.VMEM((2, 4, rows, 512), jnp.bfloat16),
+        pltpu.VMEM((seqs, 2, rows, 512), jnp.bfloat16),
+        pltpu.VMEM((seqs, rows, 512), jnp.bfloat16),
+        pltpu.VMEM((tokens, 512), jnp.float32),
+        pltpu.VMEM((tokens, 512), jnp.float32),
+    )
+
+    def sixth_phase(wb, sems):
+        pieces = ((wga_hbm, base, 2), (wq_hbm, base + 4, 2), (wk_hbm, base + 6, 1), (wv_hbm, base + 7, 1))
+
+        def loads(n, slot):
+            at = pl.ds(pl.multiple_of(n * TILE, TILE), TILE)
+            out, start = [], 0
+            for p, (ref, _, count) in enumerate(pieces):
+                out.append(
+                    pltpu.make_async_copy(
+                        ref.at[at], wb.at[slot, :, pl.ds(start, count * TILE)], sems.at[slot, p]
+                    )
+                )
+                start += count * TILE
+            return out
+
+        def compute(slot):
+            total, start = None, 0
+            for _, first, count in pieces:
+                for n in range(count):
+                    part = dot_rows(acts[first + n, 0], wb[slot, :, pl.ds(start, TILE)])
+                    total = part if total is None else total + part
+                    start += TILE
+            return total
+
+        pl.semaphore_wait(credit, 2)
+        reduce_start(2, loads, compute)
+
+    pl.run_scoped(
+        sixth_phase,
+        pltpu.VMEM((2, TILE, 6 * TILE), jnp.bfloat16),
+        pltpu.SemaphoreType.DMA((2, 4)),
+    )
+
+    for step in range(5):
+        device = (y_dev, lo_dev, hi_dev, core_dev, x_dev)[step]
+        copy = remote(gvec.at[step], gvec_got.at[step], gv_s.at[step], gv_r.at[step], device)
+        copy.start()
+        copy.wait()
+        gvec[step + 1] = gvec[step] + gvec_got[step]
+    gains_out[...] = gvec[5]
+
+    lt_relay_in(2).wait_recv()
+    lt_relay_in(3).wait_recv()
+    back([(stage_one, 9, 12), (stage_two, 4, 8), (stage_three, 0, 4)])
+    reduce_end(2)
+
+    def last_phase(xbuf, dbuf, obuf, sems, o_sems):
+        def loads(r, slot):
+            at = pl.ds(r * 128, 128)
+            return (
+                pltpu.make_async_copy(x_hbm.at[at], xbuf.at[slot], sems.at[slot, 0]),
+                pltpu.make_async_copy(dh_hbm.at[at], dbuf.at[slot], sems.at[slot, 1]),
+            )
+
+        def store(r, slot):
+            return pltpu.make_async_copy(obuf.at[slot], x_out.at[pl.ds(r * 128, 128)], o_sems.at[slot])
+
+        for copy in loads(0, 0):
+            copy.start()
+
+        @pl.loop(0, n_chunks)
+        def _(r):
+            slot = lax.rem(r, 2)
+
+            @pl.when(r < n_chunks - 1)
+            def _():
+                for copy in loads(r + 1, 1 - slot):
+                    copy.start()
+
+            for copy in loads(r, slot):
+                copy.wait()
+
+            @pl.when(r >= 2)
+            def _():
+                store(r - 2, slot).wait()
+
+            value = wide(xbuf[slot])
+            scale = rms(value)
+            normed = value * scale
+            grad = fin_rows(2, pl.multiple_of(r * 128, 128), 128)
+            vec[0, 0:1] += jnp.sum(grad * normed, axis=0, keepdims=True)
+            scaled = grad * n1_ref[...]
+            inner = jnp.mean(scaled * normed, axis=-1, keepdims=True)
+            obuf[slot] = low(dbuf[slot] + scale * (scaled - normed * inner))
+            store(r, slot).start()
+
+        store(n_chunks - 2, n_chunks % 2).wait()
+        store(n_chunks - 1, (n_chunks - 1) % 2).wait()
+
+    pl.run_scoped(
+        last_phase,
+        pltpu.VMEM((2, 128, width), jnp.bfloat16),
+        pltpu.VMEM((2, 128, width), jnp.float32),
+        pltpu.VMEM((2, 128, width), jnp.bfloat16),
+        pltpu.SemaphoreType.DMA((2, 2)),
+        pltpu.SemaphoreType.DMA((2,)),
+    )
+
+    for step in range(3):
+        device = (y_dev, lo_dev, hi_dev)[step]
+        copy = remote(vec.at[step], vec_got.at[step], nv_s.at[step], nv_r.at[step], device)
+        copy.start()
+        copy.wait()
+        vec[step + 1] = vec[step] + vec_got[step]
+    norms_out[...] = vec[3]
+
+    count = ff_items + 8
+    one, two, three = 12, 8, 4
+    while three < count:
+        step = []
+        if one < count:
+            step.append((stage_one, one, min(one + 2, count)))
+            one = min(one + 2, count)
+        if two < one - 2 or one == count:
+            step.append((stage_two, two, min(two + 2, one)))
+            two = min(two + 2, one)
+        if three < two - 2 or two == count:
+            step.append((stage_three, three, min(three + 2, two)))
+            three = min(three + 2, two)
+        back(step)
+
+    @pl.loop(0, count)
+    def _(i):
+        act_copy(i).wait_send()
+
+    @pl.loop(count - 4, count)
+    def _(i):
+        zlo_copy(i).wait_send()
+        zhi_copy(i).wait_send()
+
+    @pl.loop(count - 2, count)
+    def _(i):
+        out_copy(i).wait()
+
+    for l in range(4):
+        lt_copy(l).wait_send()
+        lt_relay(l).wait_send()
+
+
+def back_call(hbm, vmem, sizes):
+    tokens, width, seqs, rows, keys_total, hidden = sizes
+    count = 3 * (hidden // TILE) + 8
+    bf, f32 = jnp.bfloat16, jnp.float32
+    dma = pltpu.SemaphoreType.DMA
+    scratch = [
+        pltpu.VMEM((count, 2, tokens, TILE), bf),
+        pltpu.VMEM((4, 2, 4, TILE, tokens), bf),
+        pltpu.VMEM((4, 2, TILE, tokens), bf),
+        pltpu.VMEM((4, tokens, TILE), bf),
+        pltpu.VMEM((2, 4, tokens, TILE), bf),
+        pltpu.VMEM((2, 4, tokens, TILE), bf),
+        pltpu.VMEM((2, 8, tokens, TILE), bf),
+        pltpu.VMEM((seqs, 4, rows, 512), bf),
+        pltpu.VMEM((seqs, 2, rows, 512), bf),
+        pltpu.VMEM((seqs, rows, 512), bf),
+        pltpu.VMEM((4, 2, TILE, TILE), bf),
+        pltpu.VMEM((4, TILE, TILE), bf),
+        pltpu.VMEM((2, TILE, TILE), bf),
+        pltpu.VMEM((2, TILE, TILE), f32),
+        pltpu.VMEM((tokens, width), bf),
+        pltpu.VMEM((tokens, width), bf),
+        pltpu.VMEM((2, 2, 8, tokens), f32),
+        pltpu.VMEM((4, 8, width), f32),
+        pltpu.VMEM((3, 8, width), f32),
+        pltpu.VMEM((6, 8, 256), f32),
+        pltpu.VMEM((5, 8, 256), f32),
+        *(dma((count,)) for _ in range(6)),
+        *(dma((4,)) for _ in range(4)),
+        *(dma((3, 4)) for _ in range(6)),
+        *(dma((seqs,)) for _ in range(6)),
+        dma((3,)), dma((3,)), dma((5,)), dma((5,)),
+        dma((2,)), dma((2,)), dma((8,)), pltpu.SemaphoreType.REGULAR,
+    ]
+    any_spec = pl.BlockSpec(memory_space=pl.ANY)
+    vmem_spec = pl.BlockSpec(memory_space=pltpu.VMEM)
+    return pl.pallas_call(
+        back_kernel,
+        out_shape=[
+            jax.ShapeDtypeStruct((tokens, width), bf),
+            jax.ShapeDtypeStruct((tokens, width), bf),
+            jax.ShapeDtypeStruct((count, TILE, TILE), f32),
+            jax.ShapeDtypeStruct((8, width), f32),
+            jax.ShapeDtypeStruct((8, 256), f32),
+            jax.ShapeDtypeStruct((tokens, width), f32),
+            jax.ShapeDtypeStruct((count, 2, TILE, TILE), bf),
+            jax.ShapeDtypeStruct((count, TILE, TILE), bf),
+        ],
+        in_specs=[any_spec] * len(hbm) + [vmem_spec] * len(vmem),
+        out_specs=[any_spec] * 3 + [vmem_spec] * 2 + [any_spec] * 3,
+        scratch_shapes=scratch,
+        compiler_params=pltpu.CompilerParams(
+            collective_id=1, has_side_effects=True, vmem_limit_bytes=61 << 20
+        ),
+    )(*hbm, *vmem)
+
+
 def on_device(
+    x_in,
+    cot,
+    domain_ids,
+    domain_counts,
+    domain_weights,
+    block_order,
+    norm1,
+    w_query,
+    w_key,
+    w_value,
+    w_gate_attn,
+    w_out,
+    query_gain,
+    key_gain,
+    norm2,
+    w_gate,
+    w_up,
+    w_down,
+):
+    sequences, local_rows, width = x_in.shape
+    row_total = sequences * local_rows
+    head_dim = query_gain.shape[0]
+    kv_local = w_key.shape[1] // head_dim
+    q_local = w_query.shape[1] // head_dim
+    group = q_local // kv_local
+    devices = lax.axis_size("seq")
+    own = lax.axis_index("seq")
+    block_rows = local_rows * devices // block_order.shape[0]
+    query_factor = head_dim ** (-0.5)
+    q_gain, k_gain = wide(query_gain), wide(key_gain)
+    gain_one, gain_two = wide(norm1), wide(norm2)
+
+    def cut_columns(weight, half):
+        return lax.dynamic_slice_in_dim(weight, half * (width // 2), width // 2, 1)
+
+    x_rows = x_in.reshape(row_total, width)
+    x_float = wide(x_rows)
+    x_normed = low(x_float * norm_scale(x_float) * gain_one)
+    key_raw = product(x_normed, w_key)
+    by_head = key_raw.reshape(row_total, kv_local, head_dim)
+    key_rows = low(by_head * norm_scale(by_head) * k_gain).reshape(row_total, -1)
+    value_rows = low(product(x_normed, w_value))
+    pair = jnp.concatenate([key_rows, value_rows], axis=1).reshape(sequences, local_rows, -1)
+    kv_width = kv_local * head_dim
+
+    seqs_of = sequences // CHUNKS
+    rows_of = row_total // CHUNKS
+
+    def gather(value):
+        slots = {0: value}
+        for mask in range(2, devices, 2):
+            slots[mask] = swap(value, "seq", mask)
+        for mask in range(0, devices, 2):
+            slots[mask + 1] = swap(slots[mask], "seq", 1)
+        return jnp.stack([slots[j] for j in range(devices)], axis=1).reshape(
+            seqs_of, devices * local_rows, -1
+        )
+
+    gathered = [gather(pair[c * seqs_of : (c + 1) * seqs_of]) for c in range(CHUNKS)]
+
+    query_raw = product(x_normed, w_query)
+    gate_pre = product(x_normed, w_gate_attn)
+    by_head = query_raw.reshape(row_total, q_local, head_dim)
+    query = low(by_head * norm_scale(by_head) * q_gain * query_factor)
+    gate_sig = jax.nn.sigmoid(gate_pre)
+
+    query_pos = positions(block_order, own, local_rows, block_rows)
+    key_pos = jnp.concatenate(
+        [positions(block_order, own ^ j, local_rows, block_rows) for j in range(devices)]
+    )
+    allowed = key_pos[None, :] <= query_pos[:, None]
+
+    domain_total = domain_weights.shape[0]
+    domain_index = jnp.arange(domain_total, dtype=jnp.int32)
+    factor = domain_weights * (row_total * devices) / (domain_total * wide(domain_counts))
+    picked = domain_ids.reshape(row_total)[:, None] == domain_index[None, :]
+    row_scale = jnp.sum(jnp.where(picked, factor[None, :], 0.0), axis=1)
+
+    saved = []
+    for c in range(CHUNKS):
+        rows = slice(c * rows_of, (c + 1) * rows_of)
+        heads = (
+            query[rows]
+            .reshape(seqs_of, local_rows, kv_local, group, head_dim)
+            .transpose(0, 2, 3, 1, 4)
+        )
+        keys = gathered[c][..., :kv_width].reshape(seqs_of, -1, kv_local, head_dim)
+        values = gathered[c][..., kv_width:].reshape(seqs_of, -1, kv_local, head_dim)
+        scores = jnp.einsum("skgqd,spkd->skgqp", heads, keys, preferred_element_type=jnp.float32)
+        scores = jnp.where(allowed, scores, -1e30)
+        top = jnp.max(scores, axis=-1)
+        weights = jnp.where(allowed, jnp.exp(scores - top[..., None]), 0.0)
+        total = jnp.sum(weights, axis=-1)
+        mixed = jnp.einsum(
+            "skgqp,spkd->skgqd", low(weights), values, preferred_element_type=jnp.float32
+        )
+        attn_heads = mixed / total[..., None]
+        log_total = top + jnp.log(total)
+        attn_flat = attn_heads.transpose(0, 3, 1, 2, 4).reshape(rows_of, q_local * head_dim)
+        gated = low(attn_flat * gate_sig[rows])
+        attn_sum = head_sum(gated, w_out, product, cut_columns)
+        residual = x_float[rows] + attn_sum
+        log_total = log_total.reshape(seqs_of, kv_local, 1, group * local_rows)
+        saved.append((residual, attn_flat, gated, log_total))
+
+    residual, attn_flat, gated, log_total = (
+        jnp.concatenate([part[i] for part in saved], axis=0) for i in range(4)
+    )
+    out, x_grad, items, norms, gains, _, _, _ = back_call(
+        (
+            residual,
+            cot.reshape(row_total, width),
+            x_rows,
+            x_normed.T.reshape(devices, width // devices, row_total),
+            query.reshape(row_total, q_local * head_dim),
+            jnp.concatenate(gathered, axis=0),
+            attn_flat,
+            gate_sig,
+            gated,
+            query_raw,
+            key_raw,
+            w_gate,
+            w_up,
+            w_down,
+            w_out,
+            w_query,
+            w_key,
+            w_value,
+            w_gate_attn,
+        ),
+        (
+            row_scale[:, None],
+            log_total,
+            key_pos[:, None],
+            jnp.concatenate([query_pos] * group)[None, :],
+            gain_one[None, :],
+            gain_two[None, :],
+            q_gain[None, :],
+            k_gain[None, :],
+        ),
+        (row_total, width, sequences, local_rows, local_rows * devices, w_down.shape[0]),
+    )
+
+    def rows_item(chosen):
+        return jnp.concatenate([items[i] for i in chosen], axis=1)
+
+    def columns_item(chosen):
+        return jnp.concatenate([items[i].T for i in chosen], axis=0)
+
+    def own_part(value):
+        size = value.shape[0] // devices
+        return lax.dynamic_slice_in_dim(value, own * size, size, 0)
+
+    base = 3 * (w_down.shape[0] // TILE)
+    return (
+        out.reshape(x_in.shape),
+        x_grad.reshape(x_in.shape),
+        own_part(norms[0]),
+        rows_item((base + 4, base + 5)),
+        rows_item((base + 6,)),
+        rows_item((base + 7,)),
+        rows_item((base, base + 1)),
+        columns_item((base + 2, base + 3)),
+        own_part(gains[0, :head_dim]),
+        own_part(gains[0, head_dim:]),
+        own_part(norms[1]),
+        rows_item(range(1, base, 3)),
+        rows_item(range(2, base, 3)),
+        columns_item(range(0, base, 3)),
+    )
+
+
+def on_device_plain(
     x_in,
     cot,
     domain_ids,
@@ -322,8 +1426,9 @@
 
 
 def solution(mesh):
+    fits = mesh.shape["seq"] == 8 and mesh.shape["head"] == 4
     return jax.shard_map(
-        on_device,
+        on_device if fits else on_device_plain,
         mesh=mesh,
         in_specs=(
             P(None, "seq", None),

time: 1430 us -> 673 us (0.47)
  waiting for transfers between devices: 946 us -> 42.2 us
  Pallas kernels: 0 us -> 477 us
  local copies, waits for them, and re-layouts: 248 us -> 74.9 us
  matrix products: 132 us -> 19.4 us
  other arithmetic: 57.9 us -> 26.2 us
  blocking collectives: 27.7 us -> 0 us
  starting transfers between devices: 1.86 us -> 22.1 us
  between operations: 16.3 us -> 1.75 us
    reduce_scatter x9 -> x0, waiting for transfers between devices: 654 us -> none  [the longest x1 119 us: on_device(): lax.psum_scatter(grad_mlp_up.astype(jnp.bfloat16), 'seq', scatter_dimensi...]
    pallas_call x0 -> x1, Pallas kernels: none -> 477 us  [back_call(): pl.pallas_call(back_kernel, out_shape=[jax.ShapeDtypeStruct((tokens, widt...]
    unnamed x127 -> x83, local copies, waits for them, and re-layouts: 223 us -> 36.8 us
    psum x3 -> x0, waiting for transfers between devices: 183 us -> none  [the longest x1 85.9 us: on_device(): lax.psum(product(mixed, w_down).astype(jnp.bfloat16), 'head')]
    dot_general x22 -> x4, matrix products: 96.4 us -> 7.63 us  [the longest x2 4.84 us: on_device(): jnp.einsum('skgqp,spkd->skgqd', low(weights), values, preferred_element_t...]
    all_gather x2 -> x0, waiting for transfers between devices: 79 us -> none  [the longest x1 41.3 us: on_device(): value_piece = lax.all_gather(value_seq, 'seq', axis=1, tiled=True)]
    ppermute x0 -> x20, waiting for transfers between devices: none -> 42.2 us  [swap(): return lax.ppermute(value, axis, [(i, i ^ mask) for i in range(size)])]
    unnamed x16 -> x0, waiting for transfers between devices: 30.3 us -> none
  transfers between devices with their start and end apart: 15 -> 20, of which waited for: 15 -> 8; matrix products, arithmetic and copies ran while one was open for 11% -> 8% of each run, Pallas kernels for 0% -> 0%
where the time goes in v2:
time: 673 us; the launch traced here: 664 us
  Pallas kernels  477 us (71%)
  local copies, waits for them, and re-layouts  74.9 us (11%)
  waiting for transfers between devices  42.2 us (6%)
  other arithmetic  26.2 us (4%)
  starting transfers between devices  22.1 us (3%)
  matrix products  19.4 us (3%)
    pallas_call x1, Pallas kernels, back_call(): pl.pallas_call(back_kernel, out_shape=[jax.ShapeDtypeStruct((tokens, widt...  477 us
    ppermute x20, waiting for transfers between devices, swap(): return lax.ppermute(value, axis, [(i, i ^ mask) for i in range(size)])  42.2 us
    unnamed x83, local copies, waits for them, and re-layouts  36.8 us
    ppermute x20, starting transfers between devices, swap(): return lax.ppermute(value, axis, [(i, i ^ mask) for i in range(size)])  22.1 us
  transfers between devices with their start and end apart: 20, of which 8 were waited for; matrix products, arithmetic and copies ran while one was open for 8% of the time, Pallas kernels for 0%

profile of v2, /device:TPU:0, one launch (start us, length us, event | category | flops | bytes accessed | tf_op | source)
XLA Modules:
  0.0 663.7 jit_solution(3138152439510034820)
XLA Ops:
  1.5 2.1 multiply_reduce_fusion
  8.6 3.0 collective-permute-start
  13.2 2.6 collective-permute-start.3
  17.1 2.6 bitcast_convert_fusion
  20.7 4.5 multiply_reduce_fusion.1
  26.8 2.9 copy.95
  33.0 4.0 fusion.18.sig_hbm
  41.5 2.0 copy.124.kraw_hbm
  44.5 4.1 copy.120
  51.9 3.5 collective-permute-start.13
  56.6 4.3 collective-permute-done.11
  66.8 7.1 %collective-permute-done.13 = bf16[2,128,512]{2,1,0:T(8,128)(2,1)S(1)} collective-permute-done((bf16[2,128,512]{2,1,0:T(8,128)(2,1)}, bf16[2,128,512]{2,1,0:T(8,128)(2,1)S(1)}, u32[]{:S(2)}, u32[]{:S(2)}) %collective-permute-start.13) | collective-permute-done | bytes 262176 | tf_op jit(solution)/shard_map/ppermute | solution.py:51
  78.4 3.1 collective-permute-done.4
  82.6 4.6 collective-permute-done.6
  95.3 2.6 fusion.83
  97.9 2.2 reshape.361
  102.5 1.9 fusion
  108.5 3.4 fusion.39
  119.7 2.0 collective-permute-start.8
  122.6 11.4 %collective-permute-done.18 = bf16[256,1024]{1,0:T(8,128)(2,1)S(1)} collective-permute-done((bf16[256,1024]{1,0:T(8,128)(2,1)S(1)}, bf16[256,1024]{1,0:T(8,128)(2,1)S(1)}, u32[]{:S(2)}, u32[]{:S(2)}) %collective-permute-start.18) | collective-permute-done | bytes 524320 | tf_op jit(solution)/shard_map/ppermute | solution.py:51
  134.3 10.0 %collective-permute-done.8 = bf16[256,1024]{1,0:T(8,128)(2,1)S(1)} collective-permute-done((bf16[256,1024]{1,0:T(8,128)(2,1)S(1)}, bf16[256,1024]{1,0:T(8,128)(2,1)S(1)}, u32[]{:S(2)}, u32[]{:S(2)}) %collective-permute-start.8) | collective-permute-done | bytes 524320 | tf_op jit(solution)/shard_map/ppermute | solution.py:51
  145.2 3.9 pad_maximum_fusion.1.kv_hbm
  149.3 2.0 copy-done.2
  152.2 2.3 pad_maximum_fusion.h_hbm
  154.5 477.2 %shard_map.281 = (bf16[512,2048]{1,0:T(8,128)(2,1)}, bf16[512,2048]{1,0:T(8,128)(2,1)}, f32[26,256,256]{2,1,0:T(8,128)}, f32[8,2048]{1,0:T(8,128)}, f32[8,256]{1...) custom-call(f32[512,2048]{1,0:T(8,128)} %pad_maximum_fusion.h_hbm, ...), custom_call_target="tpu_custom_call" | custom-call | tf_op jit(solution)/shard_map/pallas_call | solution.py:954
  632.6 1.9 bitcast_dynamic-update-slice_fusion.17
  634.5 2.5 slice_bitcast_fusion.1
  648.5 1.9 bitcast_dynamic-update-slice_fusion.16
  650.3 1.9 bitcast_dynamic-update-slice_fusion.15
  652.2 1.9 bitcast_dynamic-update-slice_fusion.14
  654.1 2.0 bitcast_dynamic-update-slice_fusion.13
  656.1 1.9 bitcast_dynamic-update-slice_fusion.12
  (186 shorter events, 78.8 us)
Async XLA Ops:
  0.6 2.9 copy-start
  4.8 2.8 copy-start.6
  8.6 41.4 %collective-permute-start = (bf16[2,128,512]{2,1,0:T(8,128)(2,1)}, bf16[2,128,512]{2,1,0:T(8,128)(2,1)}, u32[]{:S(2)}, u32[]{:S(2)}) collective-permute-start(bf16[2,128,512]{2,1,0:T(8,128)(2,1)} %bitcast.96), channel_id=1, source_target_pairs={{0,4},{4,0},{8,12},{12,8},{16,20},{20,16},{24,28},{28,24},{1,5},{5... | collective-permute-start | bytes 786440 | tf_op jit(solution)/shard_map/ppermute | solution.py:51
  11.6 40.3 %collective-permute-start.1 = (bf16[2,128,512]{2,1,0:T(8,128)(2,1)}, bf16[2,128,512]{2,1,0:T(8,128)(2,1)}, u32[]{:S(2)}, u32[]{:S(2)}) collective-permute-start(bf16[2,128,512]{2,1,0:T(8,128)(2,1)} %bitcast.96), channel_id=1, source_target_pairs={{0,8},{4,12},{8,0},{12,4},{16,24},{20,28},{24,16},{28,20},{1,9},{5... | collective-permute-start | bytes 786440 | tf_op jit(solution)/shard_map/ppermute | solution.py:51
  13.2 51.6 %collective-permute-start.3 = (bf16[2,128,512]{2,1,0:T(8,128)(2,1)}, bf16[2,128,512]{2,1,0:T(8,128)(2,1)}, u32[]{:S(2)}, u32[]{:S(2)}) collective-permute-start(bf16[2,128,512]{2,1,0:T(8,128)(2,1)} %bitcast.96), channel_id=1, source_target_pairs={{0,16},{4,20},{8,24},{12,28},{16,0},{20,4},{24,8},{28,12},{1,17},{... | collective-permute-start | bytes 786440 | tf_op jit(solution)/shard_map/ppermute | solution.py:51
  15.8 49.5 %collective-permute-start.5 = (bf16[2,128,512]{2,1,0:T(8,128)(2,1)}, bf16[2,128,512]{2,1,0:T(8,128)(2,1)}, u32[]{:S(2)}, u32[]{:S(2)}) collective-permute-start(bf16[2,128,512]{2,1,0:T(8,128)(2,1)} %bitcast.96), channel_id=1, source_target_pairs={{0,24},{4,28},{8,16},{12,20},{16,8},{20,12},{24,0},{28,4},{1,25},{... | collective-permute-start | bytes 786440 | tf_op jit(solution)/shard_map/ppermute | solution.py:51
  16.8 39.7 %collective-permute-start.10 = (bf16[2,128,512]{2,1,0:T(8,128)(2,1)}, bf16[2,128,512]{2,1,0:T(8,128)(2,1)}, u32[]{:S(2)}, u32[]{:S(2)}) collective-permute-start(bf16[2,128,512]{2,1,0:T(8,128)(2,1)} %bitcast.100), channel_id=1, source_target_pairs={{0,4},{4,0},{8,12},{12,8},{16,20},{20,16},{24,28},{28,24},{1,5},{5... | collective-permute-start | bytes 786440 | tf_op jit(solution)/shard_map/ppermute | solution.py:51
  25.2 4.5 copy-start.24
  26.8 11.3 %copy-start.5 = (f32[512,512]{1,0:T(8,128)}, f32[512,512]{1,0:T(8,128)S(1)}, u32[]{:S(2)}) copy-start(f32[512,512]{1,0:T(8,128)S(1)} %copy.122.qraw_hbm) | copy-start | bytes 3145732
  33.0 4.1 copy-start.22
  33.0 4.5 copy-start.25
  33.0 4.5 copy-start.26
  44.5 4.9 copy-start.20
  50.1 10.8 %collective-permute-start.11 = (bf16[2,128,512]{2,1,0:T(8,128)(2,1)}, bf16[2,128,512]{2,1,0:T(8,128)(2,1)S(1)}, u32[]{:S(2)}, u32[]{:S(2)}) collective-permute-start(bf16[2,128,512]{2,1,0:T(8,128)(2,1)} %bitcast.100), channel_id=1, source_target_pairs={{0,8},{4,12},{8,0},{12,4},{16,24},{20,28},{24,16},{28,20},{1,9},{5... | collective-permute-start | bytes 786440 | tf_op jit(solution)/shard_map/ppermute | solution.py:51
  51.9 21.9 %collective-permute-start.13 = (bf16[2,128,512]{2,1,0:T(8,128)(2,1)}, bf16[2,128,512]{2,1,0:T(8,128)(2,1)S(1)}, u32[]{:S(2)}, u32[]{:S(2)}) collective-permute-start(bf16[2,128,512]{2,1,0:T(8,128)(2,1)} %bitcast.100), channel_id=1, source_target_pairs={{0,16},{4,20},{8,24},{12,28},{16,0},{20,4},{24,8},{28,12},{1,17},{... | collective-permute-start | bytes 786440 | tf_op jit(solution)/shard_map/ppermute | solution.py:51
  56.5 18.9 %collective-permute-start.15 = (bf16[2,128,512]{2,1,0:T(8,128)(2,1)}, bf16[2,128,512]{2,1,0:T(8,128)(2,1)S(1)}, u32[]{:S(2)}, u32[]{:S(2)}) collective-permute-start(bf16[2,128,512]{2,1,0:T(8,128)(2,1)} %bitcast.100), channel_id=1, source_target_pairs={{0,24},{4,28},{8,16},{12,20},{16,8},{20,12},{24,0},{28,4},{1,25},{... | collective-permute-start | bytes 786440 | tf_op jit(solution)/shard_map/ppermute | solution.py:51
  60.9 15.0 %collective-permute-start.2 = (bf16[2,128,512]{2,1,0:T(8,128)(2,1)}, bf16[2,128,512]{2,1,0:T(8,128)(2,1)S(1)}, u32[]{:S(2)}, u32[]{:S(2)}) collective-permute-start(bf16[2,128,512]{2,1,0:T(8,128)(2,1)} %collective-permute-done.1), channel_id=1, source_target_pairs={{0,4},{4,0},{8,12},{12,8},{16,20},{20,16},{24,28},{28,24},{1,5},{5... | collective-permute-start | bytes 786440 | tf_op jit(solution)/shard_map/ppermute | solution.py:51
  64.8 24.1 %collective-permute-start.12 = (bf16[2,128,512]{2,1,0:T(8,128)(2,1)S(1)}, bf16[2,128,512]{2,1,0:T(8,128)(2,1)S(1)}, u32[]{:S(2)}, u32[]{:S(2)}) collective-permute-start(bf16[2,128,512]{2,1,0:T(8,128)(2,1)S(1)} %collective-permute-done.11), channel_id=1, source_target_pairs={{0,4},{4,0},{8,12},{12,8},{16,20},{20,16},{24,28},{28,24},{1,5},{5... | collective-permute-start | bytes 786440 | tf_op jit(solution)/shard_map/ppermute | solution.py:51
  65.3 16.3 %collective-permute-start.4 = (bf16[2,128,512]{2,1,0:T(8,128)(2,1)}, bf16[2,128,512]{2,1,0:T(8,128)(2,1)S(1)}, u32[]{:S(2)}, u32[]{:S(2)}) collective-permute-start(bf16[2,128,512]{2,1,0:T(8,128)(2,1)} %collective-permute-done.3), channel_id=1, source_target_pairs={{0,4},{4,0},{8,12},{12,8},{16,20},{20,16},{24,28},{28,24},{1,5},{5... | collective-permute-start | bytes 786440 | tf_op jit(solution)/shard_map/ppermute | solution.py:51
  73.9 13.3 %collective-permute-start.6 = (bf16[2,128,512]{2,1,0:T(8,128)(2,1)}, bf16[2,128,512]{2,1,0:T(8,128)(2,1)S(1)}, u32[]{:S(2)}, u32[]{:S(2)}) collective-permute-start(bf16[2,128,512]{2,1,0:T(8,128)(2,1)} %collective-permute-done.5), channel_id=1, source_target_pairs={{0,4},{4,0},{8,12},{12,8},{16,20},{20,16},{24,28},{28,24},{1,5},{5... | collective-permute-start | bytes 786440 | tf_op jit(solution)/shard_map/ppermute | solution.py:51
  75.4 15.3 %collective-permute-start.14 = (bf16[2,128,512]{2,1,0:T(8,128)(2,1)S(1)}, bf16[2,128,512]{2,1,0:T(8,128)(2,1)S(1)}, u32[]{:S(2)}, u32[]{:S(2)}) collective-permute-start(bf16[2,128,512]{2,1,0:T(8,128)(2,1)S(1)} %collective-permute-done.13), channel_id=1, source_target_pairs={{0,4},{4,0},{8,12},{12,8},{16,20},{20,16},{24,28},{28,24},{1,5},{5... | collective-permute-start | bytes 786440 | tf_op jit(solution)/shard_map/ppermute | solution.py:51
  75.9 17.7 %collective-permute-start.16 = (bf16[2,128,512]{2,1,0:T(8,128)(2,1)S(1)}, bf16[2,128,512]{2,1,0:T(8,128)(2,1)}, u32[]{:S(2)}, u32[]{:S(2)}) collective-permute-start(bf16[2,128,512]{2,1,0:T(8,128)(2,1)S(1)} %collective-permute-done.15), channel_id=1, source_target_pairs={{0,4},{4,0},{8,12},{12,8},{16,20},{20,16},{24,28},{28,24},{1,5},{5... | collective-permute-start | bytes 786440 | tf_op jit(solution)/shard_map/ppermute | solution.py:51
  97.9 3.3 copy-start.17
  113.1 3.0 copy-start.1
  116.5 2.1 collective-permute-start.17
  117.1 2.2 collective-permute-start.7
  119.1 14.8 %collective-permute-start.18 = (bf16[256,1024]{1,0:T(8,128)(2,1)S(1)}, bf16[256,1024]{1,0:T(8,128)(2,1)S(1)}, u32[]{:S(2)}, u32[]{:S(2)}) collective-permute-start(bf16[256,1024]{1,0:T(8,128)(2,1)S(1)} %add_convert_fusion.1), channel_id=1, source_target_pairs={{0,2},{1,3},{2,0},{3,1},{4,6},{5,7},{6,4},{7,5},{8,10},{9,11},{10,... | collective-permute-start | bytes 1572872 | tf_op jit(solution)/shard_map/ppermute | solution.py:51
  119.7 25.5 %copy-start.4 = (bf16[2,8,128,512]{3,2,1,0:T(8,128)(2,1)S(1)}, bf16[2,8,128,512]{3,2,1,0:T(8,128)(2,1)}, u32[]{:S(2)}) copy-start(bf16[2,8,128,512]{3,2,1,0:T(8,128)(2,1)} %copy-done.3) | copy-start | bytes 6291460
  119.7 24.6 %collective-permute-start.8 = (bf16[256,1024]{1,0:T(8,128)(2,1)S(1)}, bf16[256,1024]{1,0:T(8,128)(2,1)S(1)}, u32[]{:S(2)}, u32[]{:S(2)}) collective-permute-start(bf16[256,1024]{1,0:T(8,128)(2,1)S(1)} %add_convert_fusion.3), channel_id=1, source_target_pairs={{0,2},{1,3},{2,0},{3,1},{4,6},{5,7},{6,4},{7,5},{8,10},{9,11},{10,... | collective-permute-start | bytes 1572872 | tf_op jit(solution)/shard_map/ppermute | solution.py:51
  134.2 14.9 %collective-permute-start.19 = (bf16[256,1024]{1,0:T(8,128)(2,1)S(1)}, bf16[256,1024]{1,0:T(8,128)(2,1)S(1)}, u32[]{:S(2)}, u32[]{:S(2)}) collective-permute-start(bf16[256,1024]{1,0:T(8,128)(2,1)S(1)} %add_convert_fusion), channel_id=1, source_target_pairs={{0,1},{1,0},{2,3},{3,2},{4,5},{5,4},{6,7},{7,6},{8,9},{9,8},{10,11... | collective-permute-start | bytes 1572872 | tf_op jit(solution)/shard_map/ppermute | solution.py:51
  144.5 4.7 collective-permute-start.9
  654.1 5.6 copy-start.11
  (15 other events, 28.5 us)

commit v3 on v2

--- a/solution.py
+++ b/solution.py
@@ -106,7 +106,8 @@
     h_hbm, cot_hbm, x_hbm, xt_hbm, q_hbm, kv_hbm, o_hbm, sig_hbm, y_hbm, qraw_hbm, kraw_hbm,
     wg_hbm, wu_hbm, wd_hbm, wo_hbm, wq_hbm, wk_hbm, wv_hbm, wga_hbm,
     factor_ref, lse_ref, kpos_ref, qpos_ref, n1_ref, n2_ref, qg_ref, kg_ref,
-    block_out, x_out, items_out, norms_out, gains_out, dh_hbm, zlo_hbm, zhi_hbm,
+    block_out, x_out, dwd_out, dwg_out, dwu_out, dwo_out, dwga_out, dwq_out, dwk_out, dwv_out,
+    norms_out, gains_out, dh_hbm, zlo_hbm, zhi_hbm,
     acts, lt, odd, csend, crecv, xrecv, fin, yrecv, lrecv, hrecv,
     zlo_send, zhi_send, stage, ostage, wide_a, wide_b, delta,
     vec, vec_got, gvec, gvec_got,
@@ -163,79 +164,105 @@
     def item_dot(i, l, t):
         return dot_plain(lt[l, 0, t], acts[i, 0]) + dot_plain(lt[l, 1, t], acts[i, 1])
 
-    def stage_one(first, last, l_of):
-        @pl.loop(first, last)
-        def _(i):
-            l = l_of(i)
-            act_copy(i).wait_recv()
-
-            @pl.when(i >= 4)
-            def _():
-                zlo_copy(i - 4).wait_send()
-
-            slot = lax.rem(i, 4)
-            for k in range(2):
-                zlo_send[slot, k] = low(item_dot(i, l, 2 * k + 1))
-            zlo_copy(i).start()
-
-    def stage_two(first, last, l_of):
-        @pl.loop(first, last)
-        def _(i):
-            l = l_of(i)
-            zlo_copy(i).wait_recv()
-            here = pltpu.make_async_copy(zlo_hbm.at[i, 1], stage.at[0], st_sem.at[0])
-            here.start()
-
-            @pl.when(i >= 4)
-            def _():
-                zhi_copy(i - 4).wait_send()
-
-            total = item_dot(i, l, 2)
-            here.wait()
-            zhi_send[lax.rem(i, 4)] = low(total + wide(stage[0]))
-            zhi_copy(i).start()
-
-    def out_copy(i):
+    def stage_one(i, l):
+        act_copy(i).wait_recv()
+
+        @pl.when(i >= 4)
+        def _():
+            zlo_copy(i - 4).wait_send()
+
+        slot = lax.rem(i, 4)
+        for k in range(2):
+            zlo_send[slot, k] = low(item_dot(i, l, 2 * k + 1))
+        zlo_copy(i).start()
+
+    def stage_two(i, l):
+        zlo_copy(i).wait_recv()
+        here = pltpu.make_async_copy(zlo_hbm.at[i, 1], stage.at[0], st_sem.at[0])
+        here.start()
+
+        @pl.when(i >= 4)
+        def _():
+            zhi_copy(i - 4).wait_send()
+
+        total = item_dot(i, l, 2)
+        here.wait()
+        zhi_send[lax.rem(i, 4)] = low(total + wide(stage[0]))
+        zhi_copy(i).start()
+
+    def out_wait(i):
         slot = lax.rem(i, 2)
-        return pltpu.make_async_copy(ostage.at[slot], items_out.at[i], out_sem.at[slot])
-
-    def stage_three(first, last, l_of):
-        @pl.loop(first, last)
-        def _(i):
-            l = l_of(i)
-            zhi_copy(i).wait_recv()
-            one = pltpu.make_async_copy(zlo_hbm.at[i, 0], stage.at[0], st_sem.at[0])
-            two = pltpu.make_async_copy(zhi_hbm.at[i], stage.at[1], st_sem.at[1])
-            one.start()
-            two.start()
-
-            @pl.when(i >= 2)
-            def _():
-                out_copy(i - 2).wait()
-
-            total = item_dot(i, l, 0)
-            one.wait()
-            two.wait()
-            ostage[lax.rem(i, 2)] = total + wide(stage[0]) + wide(stage[1])
-            out_copy(i).start()
+        pltpu.make_async_copy(ostage.at[slot], dwk_out, out_sem.at[slot]).wait()
+
+    def stage_three(i, l, places):
+        zhi_copy(i).wait_recv()
+        one = pltpu.make_async_copy(zlo_hbm.at[i, 0], stage.at[1], st_sem.at[1])
+        two = pltpu.make_async_copy(zhi_hbm.at[i], stage.at[2], st_sem.at[2])
+        one.start()
+        two.start()
+
+        @pl.when(i >= 2)
+        def _():
+            out_wait(i - 2)
+
+        total = item_dot(i, l, 0)
+        one.wait()
+        two.wait()
+        total = total + wide(stage[1]) + wide(stage[2])
+        slot = lax.rem(i, 2)
+        for chosen, ref, n, turned in places:
+
+            def put():
+                at = pl.ds(pl.multiple_of(n * TILE, TILE), TILE)
+                ostage[slot] = total.T if turned else total
+                target = ref.at[at] if turned else ref.at[:, at]
+                pltpu.make_async_copy(ostage.at[slot], target, out_sem.at[slot]).start()
+
+            if chosen is None:
+                put()
+            else:
+                pl.when(chosen)(put)
 
     def ff_l(i):
         return 1 - lax.div(lax.rem(i, 3) + 1, 2)
 
-    def const_l(l):
-        return lambda i: l
-
-    def back(stages):
-        for stage_of, first, last in stages:
-            for a, b, l_of in (
-                (0, ff_items, ff_l),
-                (ff_items, ff_items + 2, const_l(2)),
-                (ff_items + 2, ff_items + 4, const_l(3)),
-                (ff_items + 4, ff_items + 8, const_l(2)),
-            ):
-                lo_i, hi_i = max(first, a), min(last, b)
-                if lo_i < hi_i:
-                    stage_of(lo_i, hi_i, l_of)
+    def ff_places(i):
+        kind, j = lax.rem(i, 3), lax.div(i, 3)
+        return (
+            (kind == 0, dwd_out, j, True),
+            (kind == 1, dwg_out, j, False),
+            (kind == 2, dwu_out, j, False),
+        )
+
+    late = (
+        (3, dwo_out, 0, True),
+        (3, dwo_out, 1, True),
+        (2, dwga_out, 0, False),
+        (2, dwga_out, 1, False),
+        (2, dwq_out, 0, False),
+        (2, dwq_out, 1, False),
+        (2, dwk_out, 0, False),
+        (2, dwv_out, 0, False),
+    )
+    item_count = ff_items + 8
+    lead, lag = 4, 2
+
+    def tick(k, steady=False):
+        if steady or k + lead < item_count:
+            act_copy(k + lead).start()
+        for stage_of, i in ((stage_one, k), (stage_two, k - lag), (stage_three, k - 2 * lag)):
+            if not steady and not 0 <= i < item_count:
+                continue
+            is_ff = steady or i < ff_items
+            l = ff_l(i) if is_ff else late[i - ff_items][0]
+            if stage_of is stage_three:
+                if is_ff:
+                    stage_three(i, l, ff_places(i))
+                else:
+                    _, ref, n, turned = late[i - ff_items]
+                    stage_three(i, l, ((None, ref, n, turned),))
+            else:
+                stage_of(i, l)
 
     def spread(l, source):
         @pl.loop(0, 4)
@@ -268,7 +295,7 @@
         piece = fin.at[k % 2, (1 - c) * 4 + b]
         return remote(piece, piece, c2_s.at[k, b], c2_r.at[k, b], core_dev)
 
-    def reduce_start(k, loads, compute):
+    def reduce_start(k, loads, compute, hooks=()):
         def block_of(step):
             return lax.rem(c + 1 + step, 2) * 4 + lax.div(step, 2)
 
@@ -298,6 +325,9 @@
                 core_copy(k, b).wait_recv()
                 fin[k % 2, c * 4 + b] = low(part + wide(crecv[k % 2, b]))
                 x_copy(k, b).start()
+
+            for when, hook in hooks:
+                pl.when(step == when)(hook)
 
         @pl.loop(0, 4)
         def _(b):
@@ -359,6 +389,8 @@
             at = pl.ds(pl.multiple_of(r * 128, 128), 128)
             wide_a[at] = low(value * rms(value) * n2_ref[...])
             wide_b[at] = low(wide(cbuf[slot]) * factor_ref[at])
+
+        spread(1, wide_b)
 
         @pl.loop(0, hidden_tiles)
         def _(j):
@@ -384,13 +416,20 @@
                 acts[3 * j + 1, 0, at] = low(dm * u * sig * (1.0 + a * (1.0 - sig)))
                 acts[3 * j + 2, 0, at] = low(dm * act)
 
-            for k in range(3):
-                act_copy(3 * j + k).start()
-
             @pl.when(j == 0)
             def _():
-                spread(1, wide_b)
+                act_copy(0).start()
                 spread(0, wide_a)
+                act_copy(1).start()
+                act_copy(2).start()
+
+            @pl.when(j == 1)
+            def _():
+                act_copy(3).start()
+
+            @pl.when(j == 3)
+            def _():
+                relay(1)
 
     pl.run_scoped(
         first_phase,
@@ -403,6 +442,9 @@
         pltpu.SemaphoreType.DMA((2, 3)),
     )
 
+    lt_relay_in(1).wait_recv()
+    tick(0)
+
     def second_phase(wa, wb, sems):
         def loads(n, slot):
             at = pl.ds(pl.multiple_of(n * TILE, TILE), TILE)
@@ -420,7 +462,7 @@
                 total = part if total is None else total + part
             return total
 
-        reduce_start(0, loads, compute)
+        reduce_start(0, loads, compute, ((5, lambda: relay(0)),))
 
     pl.run_scoped(
         second_phase,
@@ -428,6 +470,9 @@
         pltpu.VMEM((2, TILE, wg_hbm.shape[1]), jnp.bfloat16),
         pltpu.SemaphoreType.DMA((2, 2)),
     )
+
+    lt_relay_in(0).wait_recv()
+    tick(1)
 
     def third_phase(wa, sems):
         def loads(n, slot):
@@ -449,10 +494,12 @@
         pltpu.SemaphoreType.DMA((2,)),
     )
 
+    tick(2)
+
     base = ff_items
     for n in range(2):
         pltpu.make_async_copy(
-            y_hbm.at[:, pl.ds(n * TILE, TILE)], acts.at[base + 2 + n, 0], misc.at[n]
+            y_hbm.at[:, pl.ds(n * TILE, TILE)], acts.at[base + n, 0], misc.at[n]
         ).start()
 
     def xt_own(t):
@@ -467,22 +514,16 @@
         xt_own(t).start()
     for k in range(2):
         xt_odd(k).start()
-    relay(1)
-    relay(0)
-    lt_relay_in(1).wait_recv()
-    lt_relay_in(0).wait_recv()
-    back([(stage_one, 0, 6)])
     for t in range(4):
         xt_own(t).wait()
     for k in range(2):
         xt_odd(k).wait()
-    lt_copy(2).start()
     for n in range(2):
         pltpu.make_async_copy(
-            y_hbm.at[:, pl.ds(n * TILE, TILE)], acts.at[base + 2 + n, 0], misc.at[n]
+            y_hbm.at[:, pl.ds(n * TILE, TILE)], acts.at[base + n, 0], misc.at[n]
         ).wait()
-        act_copy(base + 2 + n).start()
-
+
+    tick(3)
     reduce_end(0)
 
     def fourth_phase(hbuf, cbuf, dbuf, wob, obuf, sbuf, sems, d_sems, w_sems):
@@ -543,6 +584,7 @@
         spill(n_chunks - 2, n_chunks % 2).wait()
         spill(n_chunks - 1, (n_chunks - 1) % 2).wait()
 
+        tick(4)
         ones = jnp.ones((8, 128), jnp.bfloat16)
         for n in range(2):
             for copy in tile_loads(n):
@@ -550,8 +592,7 @@
             dy = dot_rows(wide_a[...], wob[n])
             sig, o = sbuf[n], obuf[n]
             do = low(dy * sig)
-            acts[base + n, 0] = low(dy * o * sig * (1.0 - sig))
-            act_copy(base + n).start()
+            acts[base + 2 + n, 0] = low(dy * o * sig * (1.0 - sig))
             wide_b[:, n * TILE : (n + 1) * TILE] = do
             both = wide(do) * o
             for g in range(2):
@@ -576,6 +617,8 @@
         pltpu.SemaphoreType.DMA((2,)),
         pltpu.SemaphoreType.DMA((2, 3)),
     )
+
+    tick(5)
 
     def attention_back(keep, ysend, lsend, hsend, dq_ref, dkv_ref):
         def ky_copy(s):
@@ -634,6 +677,7 @@
                         dq_ref[at, lanes[g]] = dq[g * rows : (g + 1) * rows]
 
                 ky_copy(s).start()
+                tick(6 + s, True)
 
         pl.run_scoped(
             fifth_phase,
@@ -643,9 +687,10 @@
             pltpu.SemaphoreType.DMA((2,)),
         )
 
-        relay(2)
+        lt_copy(2).start()
         relay(3)
-        back([(stage_two, 0, 4)])
+        tick(6 + seqs)
+        tick(7 + seqs)
 
         @pl.loop(0, seqs)
         def _(s):
@@ -656,7 +701,7 @@
                 lsend[s, k] = low(keep[s, 2 * k + 1])
             kl_copy(s).start()
 
-        back([(stage_one, 6, 9)])
+        tick(8 + seqs)
 
         def query_phase(rbuf, sem):
             load = pltpu.make_async_copy(qraw_hbm, rbuf, sem)
@@ -676,8 +721,6 @@
                 scaled = grad * (qg_ref[...] * factor)
                 out = scale * (scaled - normed * jnp.mean(scaled * normed, axis=-1, keepdims=True))
                 acts[base + 4 + hd // 2, 0, :, (hd % 2) * 128 : (hd % 2 + 1) * 128] = low(out)
-            for n in range(2):
-                act_copy(base + 4 + n).start()
 
         gvec[0] = jnp.zeros_like(gvec[0])
         pl.run_scoped(query_phase, pltpu.VMEM(qraw_hbm.shape, jnp.float32), pltpu.SemaphoreType.DMA)
@@ -690,6 +733,8 @@
             hsend[s] = low(keep[s, 2])
             kh_copy(s).start()
 
+        tick(9 + seqs)
+        relay(2)
         reduce_end(1)
 
         def out_phase(hbuf, obuf, sems, o_sems):
@@ -728,6 +773,8 @@
             pltpu.SemaphoreType.DMA((2,)),
             pltpu.SemaphoreType.DMA((2,)),
         )
+
+        tick(10 + seqs)
 
         @pl.loop(0, seqs)
         def _(s):
@@ -752,8 +799,6 @@
                 out = scale * (scaled - normed * jnp.mean(scaled * normed, axis=-1, keepdims=True))
                 acts[base + 6, 0, :, lane] = low(out)
             acts[base + 7, 0] = low(dkv_ref[:, 256:512])
-            for n in range(2):
-                act_copy(base + 6 + n).start()
 
         pl.run_scoped(key_phase, pltpu.VMEM(kraw_hbm.shape, jnp.float32), pltpu.SemaphoreType.DMA)
 
@@ -777,7 +822,7 @@
     )
 
     def sixth_phase(wb, sems):
-        pieces = ((wga_hbm, base, 2), (wq_hbm, base + 4, 2), (wk_hbm, base + 6, 1), (wv_hbm, base + 7, 1))
+        pieces = ((wga_hbm, base + 2, 2), (wq_hbm, base + 4, 2), (wk_hbm, base + 6, 1), (wv_hbm, base + 7, 1))
 
         def loads(n, slot):
             at = pl.ds(pl.multiple_of(n * TILE, TILE), TILE)
@@ -801,7 +846,7 @@
             return total
 
         pl.semaphore_wait(credit, 2)
-        reduce_start(2, loads, compute)
+        reduce_start(2, loads, compute, ((3, lambda: tick(11 + seqs)),))
 
     pl.run_scoped(
         sixth_phase,
@@ -819,7 +864,8 @@
 
     lt_relay_in(2).wait_recv()
     lt_relay_in(3).wait_recv()
-    back([(stage_one, 9, 12), (stage_two, 4, 8), (stage_three, 0, 4)])
+    tick(12 + seqs)
+    tick(13 + seqs)
     reduce_end(2)
 
     def last_phase(xbuf, dbuf, obuf, sems, o_sems):
@@ -882,33 +928,21 @@
         vec[step + 1] = vec[step] + vec_got[step]
     norms_out[...] = vec[3]
 
-    count = ff_items + 8
-    one, two, three = 12, 8, 4
-    while three < count:
-        step = []
-        if one < count:
-            step.append((stage_one, one, min(one + 2, count)))
-            one = min(one + 2, count)
-        if two < one - 2 or one == count:
-            step.append((stage_two, two, min(two + 2, one)))
-            two = min(two + 2, one)
-        if three < two - 2 or two == count:
-            step.append((stage_three, three, min(three + 2, two)))
-            three = min(three + 2, two)
-        back(step)
-
-    @pl.loop(0, count)
+    for k in range(14 + seqs, item_count + 2 * lag):
+        tick(k)
+
+    @pl.loop(0, item_count)
     def _(i):
         act_copy(i).wait_send()
 
-    @pl.loop(count - 4, count)
+    @pl.loop(item_count - 4, item_count)
     def _(i):
         zlo_copy(i).wait_send()
         zhi_copy(i).wait_send()
 
-    @pl.loop(count - 2, count)
+    @pl.loop(item_count - 2, item_count)
     def _(i):
-        out_copy(i).wait()
+        out_wait(i)
 
     for l in range(4):
         lt_copy(l).wait_send()
@@ -933,7 +967,7 @@
         pltpu.VMEM((seqs, rows, 512), bf),
         pltpu.VMEM((4, 2, TILE, TILE), bf),
         pltpu.VMEM((4, TILE, TILE), bf),
-        pltpu.VMEM((2, TILE, TILE), bf),
+        pltpu.VMEM((3, TILE, TILE), bf),
         pltpu.VMEM((2, TILE, TILE), f32),
         pltpu.VMEM((tokens, width), bf),
         pltpu.VMEM((tokens, width), bf),
@@ -947,7 +981,7 @@
         *(dma((3, 4)) for _ in range(6)),
         *(dma((seqs,)) for _ in range(6)),
         dma((3,)), dma((3,)), dma((5,)), dma((5,)),
-        dma((2,)), dma((2,)), dma((8,)), pltpu.SemaphoreType.REGULAR,
+        dma((3,)), dma((2,)), dma((8,)), pltpu.SemaphoreType.REGULAR,
     ]
     any_spec = pl.BlockSpec(memory_space=pl.ANY)
     vmem_spec = pl.BlockSpec(memory_space=pltpu.VMEM)
@@ -956,7 +990,14 @@
         out_shape=[
             jax.ShapeDtypeStruct((tokens, width), bf),
             jax.ShapeDtypeStruct((tokens, width), bf),
-            jax.ShapeDtypeStruct((count, TILE, TILE), f32),
+            jax.ShapeDtypeStruct((hidden, TILE), f32),
+            jax.ShapeDtypeStruct((TILE, hidden), f32),
+            jax.ShapeDtypeStruct((TILE, hidden), f32),
+            jax.ShapeDtypeStruct((512, TILE), f32),
+            jax.ShapeDtypeStruct((TILE, 512), f32),
+            jax.ShapeDtypeStruct((TILE, 512), f32),
+            jax.ShapeDtypeStruct((TILE, TILE), f32),
+            jax.ShapeDtypeStruct((TILE, TILE), f32),
             jax.ShapeDtypeStruct((8, width), f32),
             jax.ShapeDtypeStruct((8, 256), f32),
             jax.ShapeDtypeStruct((tokens, width), f32),
@@ -964,7 +1005,7 @@
             jax.ShapeDtypeStruct((count, TILE, TILE), bf),
         ],
         in_specs=[any_spec] * len(hbm) + [vmem_spec] * len(vmem),
-        out_specs=[any_spec] * 3 + [vmem_spec] * 2 + [any_spec] * 3,
+        out_specs=[any_spec] * 10 + [vmem_spec] * 2 + [any_spec] * 3,
         scratch_shapes=scratch,
         compiler_params=pltpu.CompilerParams(
             collective_id=1, has_side_effects=True, vmem_limit_bytes=61 << 20
@@ -1081,7 +1122,7 @@
     residual, attn_flat, gated, log_total = (
         jnp.concatenate([part[i] for part in saved], axis=0) for i in range(4)
     )
-    out, x_grad, items, norms, gains, _, _, _ = back_call(
+    out, x_grad, down, gate, up, wout, wga, wquery, wkey, wvalue, norms, gains, *_ = back_call(
         (
             residual,
             cot.reshape(row_total, width),
@@ -1116,32 +1157,25 @@
         (row_total, width, sequences, local_rows, local_rows * devices, w_down.shape[0]),
     )
 
-    def rows_item(chosen):
-        return jnp.concatenate([items[i] for i in chosen], axis=1)
-
-    def columns_item(chosen):
-        return jnp.concatenate([items[i].T for i in chosen], axis=0)
-
     def own_part(value):
         size = value.shape[0] // devices
         return lax.dynamic_slice_in_dim(value, own * size, size, 0)
 
-    base = 3 * (w_down.shape[0] // TILE)
     return (
         out.reshape(x_in.shape),
         x_grad.reshape(x_in.shape),
         own_part(norms[0]),
-        rows_item((base + 4, base + 5)),
-        rows_item((base + 6,)),
-        rows_item((base + 7,)),
-        rows_item((base, base + 1)),
-        columns_item((base + 2, base + 3)),
+        wquery,
+        wkey,
+        wvalue,
+        wga,
+        wout,
         own_part(gains[0, :head_dim]),
         own_part(gains[0, head_dim:]),
         own_part(norms[1]),
-        rows_item(range(1, base, 3)),
-        rows_item(range(2, base, 3)),
-        columns_item(range(0, base, 3)),
+        gate,
+        up,
+        down,
     )
 
 

time: 673 us -> 529 us (0.79)
  Pallas kernels: 477 us -> 347 us
  local copies, waits for them, and re-layouts: 74.9 us -> 62 us
    pallas_call x1, Pallas kernels: 477 us -> 347 us  [back_call(): pl.pallas_call(back_kernel, out_shape=[jax.ShapeDtypeStruct((tokens, widt...]
    unnamed x83 -> x93, local copies, waits for them, and re-layouts: 36.8 us -> 28.9 us
  transfers between devices with their start and end apart: 20 -> 20, of which waited for: 8 -> 8; matrix products, arithmetic and copies ran while one was open for 8% -> 10% of each run, Pallas kernels for 0% -> 0%
where the time goes in v3:
time: 529 us; the launch traced here: 519 us
  Pallas kernels  347 us (66%)
  local copies, waits for them, and re-layouts  62 us (12%)
  waiting for transfers between devices  42.2 us (8%)
  other arithmetic  24.5 us (5%)
  starting transfers between devices  22.1 us (4%)
  matrix products  19.4 us (4%)
    pallas_call x1, Pallas kernels, back_call(): pl.pallas_call(back_kernel, out_shape=[jax.ShapeDtypeStruct((tokens, widt...  347 us
    ppermute x20, waiting for transfers between devices, swap(): return lax.ppermute(value, axis, [(i, i ^ mask) for i in range(size)])  42.2 us
    unnamed x93, local copies, waits for them, and re-layouts  28.9 us
    ppermute x20, starting transfers between devices, swap(): return lax.ppermute(value, axis, [(i, i ^ mask) for i in range(size)])  22.1 us
    dot_general x8, matrix products, product(): return jnp.dot(left, right, preferred_element_type=jnp.float32)  11.8 us
  transfers between devices with their start and end apart: 20, of which 8 were waited for; matrix products, arithmetic and copies ran while one was open for 10% of the time, Pallas kernels for 0%

profile of v3, /device:TPU:0, one launch (start us, length us, event | category | flops | bytes accessed | tf_op | source)
XLA Modules:
  0.0 519.5 jit_solution(14492852787055797980)
XLA Ops:
  1.5 2.1 multiply_reduce_fusion
  8.6 3.0 collective-permute-start
  11.6 1.6 collective-permute-start.1
  13.2 2.6 collective-permute-start.3
  17.1 2.6 bitcast_convert_fusion
  20.7 4.5 multiply_reduce_fusion.1
  26.8 2.9 copy.91
  30.4 1.7 multiply_convert_fusion.1
  33.0 4.0 fusion.18.sig_hbm
  39.2 1.7 constant_dynamic-update-slice_fusion.2
  41.5 2.0 copy.120.kraw_hbm
  44.5 4.4 copy.116
  52.3 3.5 collective-permute-start.13
  56.9 4.3 collective-permute-done.11
  62.7 1.7 bitcast_dynamic-update-slice_fusion.9
  67.2 7.0 %collective-permute-done.13 = bf16[2,128,512]{2,1,0:T(8,128)(2,1)S(1)} collective-permute-done((bf16[2,128,512]{2,1,0:T(8,128)(2,1)}, bf16[2,128,512]{2,1,0:T(8,128)(2,1)S(1)}, u32[]{:S(2)}, u32[]{:S(2)}) %collective-permute-start.13) | collective-permute-done | bytes 262176 | tf_op jit(solution)/shard_map/ppermute | solution.py:51
  78.8 3.2 collective-permute-done.4
  82.9 4.6 collective-permute-done.6
  94.0 1.7 bitcast_dynamic-update-slice_fusion.6
  95.7 2.6 fusion.83
  98.3 2.2 reshape.361
  102.8 1.9 fusion
  108.8 3.4 fusion.39
  113.4 1.6 reshape.358
  120.0 2.0 collective-permute-start.8
  122.9 11.4 %collective-permute-done.18 = bf16[256,1024]{1,0:T(8,128)(2,1)S(1)} collective-permute-done((bf16[256,1024]{1,0:T(8,128)(2,1)S(1)}, bf16[256,1024]{1,0:T(8,128)(2,1)S(1)}, u32[]{:S(2)}, u32[]{:S(2)}) %collective-permute-start.18) | collective-permute-done | bytes 524320 | tf_op jit(solution)/shard_map/ppermute | solution.py:51
  134.6 10.0 %collective-permute-done.8 = bf16[256,1024]{1,0:T(8,128)(2,1)S(1)} collective-permute-done((bf16[256,1024]{1,0:T(8,128)(2,1)S(1)}, bf16[256,1024]{1,0:T(8,128)(2,1)S(1)}, u32[]{:S(2)}, u32[]{:S(2)}) %collective-permute-start.8) | collective-permute-done | bytes 524320 | tf_op jit(solution)/shard_map/ppermute | solution.py:51
  145.5 4.0 pad_maximum_fusion.1.kv_hbm
  149.7 2.0 copy-done.2
  152.6 2.3 pad_maximum_fusion.h_hbm
  154.9 347.4 %shard_map.281 = (bf16[512,2048]{1,0:T(8,128)(2,1)}, bf16[512,2048]{1,0:T(8,128)(2,1)}, f32[1536,256]{1,0:T(8,128)}, f32[256,1536]{1,0:T(8,128)}, f32[256,1536]{...) custom-call(f32[512,2048]{1,0:T(8,128)} %pad_maximum_fusion.h_hbm, ...), custom_call_target="tpu_custom_call" | custom-call | tf_op jit(solution)/shard_map/pallas_call | solution.py:988
  506.3 3.3 copy.202
  (190 shorter events, 64.3 us)
Async XLA Ops:
  8.6 41.8 %collective-permute-start = (bf16[2,128,512]{2,1,0:T(8,128)(2,1)}, bf16[2,128,512]{2,1,0:T(8,128)(2,1)}, u32[]{:S(2)}, u32[]{:S(2)}) collective-permute-start(bf16[2,128,512]{2,1,0:T(8,128)(2,1)} %bitcast.62), channel_id=1, source_target_pairs={{0,4},{4,0},{8,12},{12,8},{16,20},{20,16},{24,28},{28,24},{1,5},{5... | collective-permute-start | bytes 786440 | tf_op jit(solution)/shard_map/ppermute | solution.py:51
  11.6 40.7 %collective-permute-start.1 = (bf16[2,128,512]{2,1,0:T(8,128)(2,1)}, bf16[2,128,512]{2,1,0:T(8,128)(2,1)}, u32[]{:S(2)}, u32[]{:S(2)}) collective-permute-start(bf16[2,128,512]{2,1,0:T(8,128)(2,1)} %bitcast.62), channel_id=1, source_target_pairs={{0,8},{4,12},{8,0},{12,4},{16,24},{20,28},{24,16},{28,20},{1,9},{5... | collective-permute-start | bytes 786440 | tf_op jit(solution)/shard_map/ppermute | solution.py:51
  13.2 51.9 %collective-permute-start.3 = (bf16[2,128,512]{2,1,0:T(8,128)(2,1)}, bf16[2,128,512]{2,1,0:T(8,128)(2,1)}, u32[]{:S(2)}, u32[]{:S(2)}) collective-permute-start(bf16[2,128,512]{2,1,0:T(8,128)(2,1)} %bitcast.62), channel_id=1, source_target_pairs={{0,16},{4,20},{8,24},{12,28},{16,0},{20,4},{24,8},{28,12},{1,17},{... | collective-permute-start | bytes 786440 | tf_op jit(solution)/shard_map/ppermute | solution.py:51
  15.8 49.9 %collective-permute-start.5 = (bf16[2,128,512]{2,1,0:T(8,128)(2,1)}, bf16[2,128,512]{2,1,0:T(8,128)(2,1)}, u32[]{:S(2)}, u32[]{:S(2)}) collective-permute-start(bf16[2,128,512]{2,1,0:T(8,128)(2,1)} %bitcast.62), channel_id=1, source_target_pairs={{0,24},{4,28},{8,16},{12,20},{16,8},{20,12},{24,0},{28,4},{1,25},{... | collective-permute-start | bytes 786440 | tf_op jit(solution)/shard_map/ppermute | solution.py:51
  16.9 39.9 %collective-permute-start.10 = (bf16[2,128,512]{2,1,0:T(8,128)(2,1)}, bf16[2,128,512]{2,1,0:T(8,128)(2,1)}, u32[]{:S(2)}, u32[]{:S(2)}) collective-permute-start(bf16[2,128,512]{2,1,0:T(8,128)(2,1)} %bitcast.66), channel_id=1, source_target_pairs={{0,4},{4,0},{8,12},{12,8},{16,20},{20,16},{24,28},{28,24},{1,5},{5... | collective-permute-start | bytes 786440 | tf_op jit(solution)/shard_map/ppermute | solution.py:51
  25.2 4.5 copy-start.31
  26.8 11.3 %copy-start.5 = (f32[512,512]{1,0:T(8,128)}, f32[512,512]{1,0:T(8,128)S(1)}, u32[]{:S(2)}) copy-start(f32[512,512]{1,0:T(8,128)S(1)} %copy.118.qraw_hbm) | copy-start | bytes 3145732
  33.0 4.1 copy-start.29
  33.0 4.5 copy-start.32
  33.0 4.5 copy-start.33
  44.5 5.3 %copy-start.27 = (bf16[2048]{0:T(1024)(128)(2,1)S(1)}, bf16[2048]{0:T(1024)(128)(2,1)}, u32[]{:S(2)}) copy-start(bf16[2048]{0:T(1024)(128)(2,1)} %param.32) | copy-start | bytes 12292
  50.4 10.8 %collective-permute-start.11 = (bf16[2,128,512]{2,1,0:T(8,128)(2,1)}, bf16[2,128,512]{2,1,0:T(8,128)(2,1)S(1)}, u32[]{:S(2)}, u32[]{:S(2)}) collective-permute-start(bf16[2,128,512]{2,1,0:T(8,128)(2,1)} %bitcast.66), channel_id=1, source_target_pairs={{0,8},{4,12},{8,0},{12,4},{16,24},{20,28},{24,16},{28,20},{1,9},{5... | collective-permute-start | bytes 786440 | tf_op jit(solution)/shard_map/ppermute | solution.py:51
  52.3 21.9 %collective-permute-start.13 = (bf16[2,128,512]{2,1,0:T(8,128)(2,1)}, bf16[2,128,512]{2,1,0:T(8,128)(2,1)S(1)}, u32[]{:S(2)}, u32[]{:S(2)}) collective-permute-start(bf16[2,128,512]{2,1,0:T(8,128)(2,1)} %bitcast.66), channel_id=1, source_target_pairs={{0,16},{4,20},{8,24},{12,28},{16,0},{20,4},{24,8},{28,12},{1,17},{... | collective-permute-start | bytes 786440 | tf_op jit(solution)/shard_map/ppermute | solution.py:51
  56.8 18.9 %collective-permute-start.15 = (bf16[2,128,512]{2,1,0:T(8,128)(2,1)}, bf16[2,128,512]{2,1,0:T(8,128)(2,1)S(1)}, u32[]{:S(2)}, u32[]{:S(2)}) collective-permute-start(bf16[2,128,512]{2,1,0:T(8,128)(2,1)} %bitcast.66), channel_id=1, source_target_pairs={{0,24},{4,28},{8,16},{12,20},{16,8},{20,12},{24,0},{28,4},{1,25},{... | collective-permute-start | bytes 786440 | tf_op jit(solution)/shard_map/ppermute | solution.py:51
  61.2 15.0 %collective-permute-start.2 = (bf16[2,128,512]{2,1,0:T(8,128)(2,1)}, bf16[2,128,512]{2,1,0:T(8,128)(2,1)S(1)}, u32[]{:S(2)}, u32[]{:S(2)}) collective-permute-start(bf16[2,128,512]{2,1,0:T(8,128)(2,1)} %collective-permute-done.1), channel_id=1, source_target_pairs={{0,4},{4,0},{8,12},{12,8},{16,20},{20,16},{24,28},{28,24},{1,5},{5... | collective-permute-start | bytes 786440 | tf_op jit(solution)/shard_map/ppermute | solution.py:51
  65.1 24.1 %collective-permute-start.12 = (bf16[2,128,512]{2,1,0:T(8,128)(2,1)S(1)}, bf16[2,128,512]{2,1,0:T(8,128)(2,1)S(1)}, u32[]{:S(2)}, u32[]{:S(2)}) collective-permute-start(bf16[2,128,512]{2,1,0:T(8,128)(2,1)S(1)} %collective-permute-done.11), channel_id=1, source_target_pairs={{0,4},{4,0},{8,12},{12,8},{16,20},{20,16},{24,28},{28,24},{1,5},{5... | collective-permute-start | bytes 786440 | tf_op jit(solution)/shard_map/ppermute | solution.py:51
  65.6 16.3 %collective-permute-start.4 = (bf16[2,128,512]{2,1,0:T(8,128)(2,1)}, bf16[2,128,512]{2,1,0:T(8,128)(2,1)S(1)}, u32[]{:S(2)}, u32[]{:S(2)}) collective-permute-start(bf16[2,128,512]{2,1,0:T(8,128)(2,1)} %collective-permute-done.3), channel_id=1, source_target_pairs={{0,4},{4,0},{8,12},{12,8},{16,20},{20,16},{24,28},{28,24},{1,5},{5... | collective-permute-start | bytes 786440 | tf_op jit(solution)/shard_map/ppermute | solution.py:51
  74.2 13.3 %collective-permute-start.6 = (bf16[2,128,512]{2,1,0:T(8,128)(2,1)}, bf16[2,128,512]{2,1,0:T(8,128)(2,1)S(1)}, u32[]{:S(2)}, u32[]{:S(2)}) collective-permute-start(bf16[2,128,512]{2,1,0:T(8,128)(2,1)} %collective-permute-done.5), channel_id=1, source_target_pairs={{0,4},{4,0},{8,12},{12,8},{16,20},{20,16},{24,28},{28,24},{1,5},{5... | collective-permute-start | bytes 786440 | tf_op jit(solution)/shard_map/ppermute | solution.py:51
  75.7 15.3 %collective-permute-start.14 = (bf16[2,128,512]{2,1,0:T(8,128)(2,1)S(1)}, bf16[2,128,512]{2,1,0:T(8,128)(2,1)S(1)}, u32[]{:S(2)}, u32[]{:S(2)}) collective-permute-start(bf16[2,128,512]{2,1,0:T(8,128)(2,1)S(1)} %collective-permute-done.13), channel_id=1, source_target_pairs={{0,4},{4,0},{8,12},{12,8},{16,20},{20,16},{24,28},{28,24},{1,5},{5... | collective-permute-start | bytes 786440 | tf_op jit(solution)/shard_map/ppermute | solution.py:51
  76.2 17.7 %collective-permute-start.16 = (bf16[2,128,512]{2,1,0:T(8,128)(2,1)S(1)}, bf16[2,128,512]{2,1,0:T(8,128)(2,1)}, u32[]{:S(2)}, u32[]{:S(2)}) collective-permute-start(bf16[2,128,512]{2,1,0:T(8,128)(2,1)S(1)} %collective-permute-done.15), channel_id=1, source_target_pairs={{0,4},{4,0},{8,12},{12,8},{16,20},{20,16},{24,28},{28,24},{1,5},{5... | collective-permute-start | bytes 786440 | tf_op jit(solution)/shard_map/ppermute | solution.py:51
  98.3 3.3 copy-start.19
  116.9 2.1 collective-permute-start.17
  117.4 2.2 collective-permute-start.7
  119.5 14.8 %collective-permute-start.18 = (bf16[256,1024]{1,0:T(8,128)(2,1)S(1)}, bf16[256,1024]{1,0:T(8,128)(2,1)S(1)}, u32[]{:S(2)}, u32[]{:S(2)}) collective-permute-start(bf16[256,1024]{1,0:T(8,128)(2,1)S(1)} %add_convert_fusion.1), channel_id=1, source_target_pairs={{0,2},{1,3},{2,0},{3,1},{4,6},{5,7},{6,4},{7,5},{8,10},{9,11},{10,... | collective-permute-start | bytes 1572872 | tf_op jit(solution)/shard_map/ppermute | solution.py:51
  120.0 25.5 %copy-start.4 = (bf16[2,8,128,512]{3,2,1,0:T(8,128)(2,1)S(1)}, bf16[2,8,128,512]{3,2,1,0:T(8,128)(2,1)}, u32[]{:S(2)}) copy-start(bf16[2,8,128,512]{3,2,1,0:T(8,128)(2,1)} %copy-done.3) | copy-start | bytes 6291460
  120.0 24.6 %collective-permute-start.8 = (bf16[256,1024]{1,0:T(8,128)(2,1)S(1)}, bf16[256,1024]{1,0:T(8,128)(2,1)S(1)}, u32[]{:S(2)}, u32[]{:S(2)}) collective-permute-start(bf16[256,1024]{1,0:T(8,128)(2,1)S(1)} %add_convert_fusion.3), channel_id=1, source_target_pairs={{0,2},{1,3},{2,0},{3,1},{4,6},{5,7},{6,4},{7,5},{8,10},{9,11},{10,... | collective-permute-start | bytes 1572872 | tf_op jit(solution)/shard_map/ppermute | solution.py:51
  134.5 15.0 %collective-permute-start.19 = (bf16[256,1024]{1,0:T(8,128)(2,1)S(1)}, bf16[256,1024]{1,0:T(8,128)(2,1)S(1)}, u32[]{:S(2)}, u32[]{:S(2)}) collective-permute-start(bf16[256,1024]{1,0:T(8,128)(2,1)S(1)} %add_convert_fusion), channel_id=1, source_target_pairs={{0,1},{1,0},{2,3},{3,2},{4,5},{5,4},{6,7},{7,6},{8,9},{9,8},{10,11... | collective-permute-start | bytes 1572872 | tf_op jit(solution)/shard_map/ppermute | solution.py:51
  144.8 4.8 collective-permute-start.9
  506.3 3.3 copy-start.10
  509.6 3.5 copy-start.21
  510.9 3.0 copy-start.20
  510.9 3.8 copy-start.14
  (22 other events, 45.1 us)

commit v4 on v3

--- a/solution.py
+++ b/solution.py
@@ -6,7 +6,6 @@
 from jax.sharding import PartitionSpec as P
 
 epsilon = 1e-06
-CHUNKS = 2
 
 
 def norm_scale(value):
@@ -40,15 +39,6 @@
 
 def wide(value):
     return value.astype(jnp.float32)
-
-
-def bits_of(axis):
-    return (lax.axis_size(axis) - 1).bit_length()
-
-
-def swap(value, axis, mask):
-    size = lax.axis_size(axis)
-    return lax.ppermute(value, axis, [(i, i ^ mask) for i in range(size)])
 
 
 def positions(block_order, device, row_count, block_rows):
@@ -59,21 +49,6 @@
         jnp.where(slots[:, None] == slot_index[None, :], block_order[None, :], 0), axis=1
     )
     return picked * block_rows + stored % block_rows
-
-
-def head_sum(left, weight, apply, cut):
-    mine = lax.axis_index("head") & 1
-    away = low(apply(left, cut(weight, 1 - mine)))
-    got = swap(away, "head", 1)
-    total = apply(left, cut(weight, mine)) + wide(got)
-    for bit in range(1, bits_of("head")):
-        part = low(total)
-        total = wide(part) + wide(swap(part, "head", 1 << bit))
-    part = low(total)
-    other = swap(part, "head", 1)
-    low_half = jnp.where(mine == 0, part, other)
-    high_half = jnp.where(mine == 0, other, part)
-    return wide(jnp.concatenate([low_half, high_half], axis=1))
 
 
 MESH = pl.DeviceIdType.MESH
@@ -1013,6 +988,280 @@
     )(*hbm, *vmem)
 
 
+def forward_kernel(
+    x_hbm, wq_hbm, wk_hbm, wv_hbm, wga_hbm, wo_hbm,
+    n1_ref, qg_ref, kg_ref, kpos_ref, qpos_ref,
+    h_out, xt_out, q_out, kv_out, o_out, sig_out, y_out, qraw_out, kraw_out, lse_ref,
+    xv, xn, wqv, wkv, wvv, wgav, wov, kv, qv, qraw, kraw, sig, ov, yv, xtv, hv,
+    csend, crecv, fin, xrecv,
+    x_sem, w_sem, out_sem, h_sem, kz_s, kz_r, ky_s, ky_r, c1_s, c1_r, x_s, x_r, c2_s, c2_r,
+):
+    seq, head = lax.axis_index("seq"), lax.axis_index("head")
+    z, y = lax.div(seq, 2), lax.rem(seq, 2)
+    c = lax.rem(head, 2)
+    y_dev = {"seq": z * 2 + 1 - y}
+    z_dev = [None] + [{"seq": other_z(z, t) * 2 + y} for t in (1, 2, 3)]
+    core_dev = {"head": head + 1 - 2 * c}
+    x_dev = {"head": head + 2 - 4 * lax.div(head, 2)}
+    seqs, slots, rows = kv.shape[0], kv.shape[1], kv.shape[2]
+    tokens, width = x_hbm.shape
+    half = width // 2
+    epsilon_k = 1e-06
+
+    def rms(value):
+        return lax.rsqrt(jnp.mean(value * value, axis=-1, keepdims=True) + epsilon_k)
+
+    def rows_at(s):
+        return pl.ds(pl.multiple_of(s * rows, 128), rows)
+
+    def x_load(s):
+        return pltpu.make_async_copy(x_hbm.at[rows_at(s)], xv.at[rows_at(s)], x_sem.at[s])
+
+    weight_loads = [
+        pltpu.make_async_copy(src, dst, w_sem.at[i])
+        for i, (src, dst) in enumerate(
+            ((wk_hbm, wkv), (wv_hbm, wvv), (wq_hbm, wqv), (wga_hbm, wgav), (wo_hbm, wov))
+        )
+    ]
+    for s in range(seqs):
+        x_load(s).start()
+    for load in weight_loads:
+        load.start()
+
+    barrier = pltpu.get_barrier_semaphore()
+    for device in (y_dev, *z_dev[1:], core_dev, x_dev):
+        pl.semaphore_signal(barrier, inc=1, device_id=device, device_id_type=MESH)
+    pl.semaphore_wait(barrier, 6)
+
+    def remote(src, dst, send, recv, device):
+        return pltpu.make_async_remote_copy(
+            src_ref=src, dst_ref=dst, send_sem=send, recv_sem=recv, device_id=device, device_id_type=MESH
+        )
+
+    def z_copy(s, t):
+        return remote(kv.at[s, 0], kv.at[s, 2 * t], kz_s.at[s, t], kz_r.at[s, t], z_dev[t])
+
+    def y_copy(s, t):
+        return remote(kv.at[s, 2 * t], kv.at[s, 2 * t + 1], ky_s.at[s, t], ky_r.at[s, t], y_dev)
+
+    def core_copy(s):
+        return remote(csend.at[s], crecv.at[s], c1_s.at[s], c1_r.at[s], core_dev)
+
+    def x_copy(s):
+        return remote(fin.at[s, c], xrecv.at[s], x_s.at[s], x_r.at[s], x_dev)
+
+    def fin_copy(s):
+        return remote(fin.at[s, c], fin.at[s, c], c2_s.at[s], c2_r.at[s], core_dev)
+
+    def fin_copy_in(s):
+        piece = fin.at[s, 1 - c]
+        return remote(piece, piece, c2_s.at[s], c2_r.at[s], core_dev)
+
+    @pl.loop(0, seqs)
+    def _(s):
+        x_load(s).wait()
+        at = rows_at(s)
+        value = wide(xv[at])
+        xn[at] = low(value * rms(value) * n1_ref[...])
+
+    weight_loads[0].wait()
+    weight_loads[1].wait()
+
+    @pl.loop(0, seqs)
+    def _(s):
+        at = rows_at(s)
+        raw = dot_plain(xn[at], wkv[...])
+        kraw[at] = raw
+        for n in range(2):
+            lane = slice(n * 128, (n + 1) * 128)
+            part = raw[:, lane]
+            kv[s, 0, :, lane] = low(part * rms(part) * kg_ref[...])
+        kv[s, 0, :, 256:512] = low(dot_plain(xn[at], wvv[...]))
+        y_copy(s, 0).start()
+        for t in (1, 2, 3):
+            z_copy(s, t).start()
+
+    outs = []
+
+    def leave(src, dst):
+        copy = pltpu.make_async_copy(src, dst, out_sem.at[len(outs)])
+        copy.start()
+        outs.append(copy)
+
+    leave(kraw, kraw_out)
+
+    def forward_keys(s):
+        for t in (1, 2, 3):
+            z_copy(s, t).wait_recv()
+            y_copy(s, t).start()
+
+    weight_loads[2].wait()
+    weight_loads[3].wait()
+    scale_q = 128.0**-0.5
+
+    @pl.loop(0, seqs)
+    def _(s):
+        at = rows_at(s)
+        raw = dot_plain(xn[at], wqv[...])
+        qraw[at] = raw
+        for n in range(4):
+            lane = slice(n * 128, (n + 1) * 128)
+            part = raw[:, lane]
+            qv[at, lane] = low(part * rms(part) * (qg_ref[...] * scale_q))
+        sig[at] = jax.nn.sigmoid(dot_plain(xn[at], wgav[...]))
+
+    leave(qraw, qraw_out)
+    leave(qv, q_out)
+    leave(sig, sig_out)
+    forward_keys(0)
+
+    @pl.loop(0, width // TILE)
+    def _(n):
+        at = pl.ds(pl.multiple_of(n * TILE, TILE), TILE)
+        xtv[n] = xn[:, at].T
+
+    leave(xtv, xt_out)
+    weight_loads[4].wait()
+
+    def finish(s):
+        x_copy(s).wait()
+        fin[s, c] = low(wide(fin[s, c]) + wide(xrecv[s]))
+        fin_copy(s).start()
+
+    def h_store(s, slot):
+        return pltpu.make_async_copy(hv.at[slot], h_out.at[rows_at(s)], h_sem.at[slot])
+
+    def finish_rows(s):
+        slot = lax.rem(s, 2)
+        fin_copy_in(s).wait_recv()
+
+        @pl.when(s >= 2)
+        def _():
+            h_store(s - 2, slot).wait()
+
+        hv[slot, :, 0:half] = wide(xv[rows_at(s), 0:half]) + wide(fin[s, 0])
+        hv[slot, :, half:width] = wide(xv[rows_at(s), half:width]) + wide(fin[s, 1])
+        h_store(s, slot).start()
+
+    @pl.loop(0, seqs)
+    def _(s):
+        @pl.when(s < seqs - 1)
+        def _():
+            forward_keys(s + 1)
+
+        for t in range(4):
+            y_copy(s, t).wait_recv()
+        at = rows_at(s)
+        allowed = kpos_ref[...] <= qpos_ref[...]
+        for n in range(2):
+            lanes = [slice((2 * n + g) * 128, (2 * n + g + 1) * 128) for g in range(2)]
+            key = kv[s, :, :, n * 128 : (n + 1) * 128].reshape(slots * rows, 128)
+            value = kv[s, :, :, 256 + n * 128 : 256 + (n + 1) * 128].reshape(slots * rows, 128)
+            q = jnp.concatenate([qv[at, lane] for lane in lanes], axis=0)
+            scores = jnp.where(allowed, dot_rows(key, q), -1e30)
+            top = jnp.max(scores, axis=0, keepdims=True)
+            probs = jnp.exp(scores - top)
+            total = jnp.sum(probs, axis=0, keepdims=True)
+            out = (dot_first(value, low(probs)) / total).T
+            lse_ref[s, n] = top + jnp.log(total)
+            for g in range(2):
+                ov[at, lanes[g]] = out[g * rows : (g + 1) * rows]
+        gated = low(ov[at] * sig[at])
+        yv[at] = gated
+        away = pl.ds(pl.multiple_of((1 - c) * half, 128), half)
+        mine = pl.ds(pl.multiple_of(c * half, 128), half)
+        csend[s] = low(dot_plain(gated, wov[:, away]))
+        core_copy(s).start()
+        part = dot_plain(gated, wov[:, mine])
+        core_copy(s).wait_recv()
+        fin[s, c] = low(part + wide(crecv[s]))
+        x_copy(s).start()
+
+        @pl.when(s >= 1)
+        def _():
+            finish(s - 1)
+
+        @pl.when(s >= 2)
+        def _():
+            finish_rows(s - 2)
+
+    leave(kv, kv_out)
+    leave(ov, o_out)
+    leave(yv, y_out)
+    finish_rows(seqs - 2)
+    finish(seqs - 1)
+    finish_rows(seqs - 1)
+    h_store(seqs - 2, seqs % 2).wait()
+    h_store(seqs - 1, (seqs - 1) % 2).wait()
+    for copy in outs:
+        copy.wait()
+
+    @pl.loop(0, seqs)
+    def _(s):
+        for t in (1, 2, 3):
+            z_copy(s, t).wait_send()
+        for t in range(4):
+            y_copy(s, t).wait_send()
+        core_copy(s).wait_send()
+        fin_copy(s).wait_send()
+
+
+def forward_call(hbm, vmem, sizes):
+    tokens, width, seqs, rows, slots = sizes
+    bf, f32 = jnp.bfloat16, jnp.float32
+    dma = pltpu.SemaphoreType.DMA
+    half = width // 2
+    kv_shape = (seqs, slots, rows, 512)
+    scratch = [
+        pltpu.VMEM((tokens, width), bf),
+        pltpu.VMEM((tokens, width), bf),
+        pltpu.VMEM((width, 512), bf),
+        pltpu.VMEM((width, 256), bf),
+        pltpu.VMEM((width, 256), bf),
+        pltpu.VMEM((width, 512), bf),
+        pltpu.VMEM((512, width), bf),
+        pltpu.VMEM(kv_shape, bf),
+        pltpu.VMEM((tokens, 512), bf),
+        pltpu.VMEM((tokens, 512), f32),
+        pltpu.VMEM((tokens, 256), f32),
+        pltpu.VMEM((tokens, 512), f32),
+        pltpu.VMEM((tokens, 512), f32),
+        pltpu.VMEM((tokens, 512), bf),
+        pltpu.VMEM((width // TILE, TILE, tokens), bf),
+        pltpu.VMEM((2, rows, width), f32),
+        pltpu.VMEM((seqs, rows, half), bf),
+        pltpu.VMEM((seqs, rows, half), bf),
+        pltpu.VMEM((seqs, 2, rows, half), bf),
+        pltpu.VMEM((seqs, rows, half), bf),
+        dma((seqs,)), dma((5,)), dma((8,)), dma((2,)),
+        *(dma((seqs, 4)) for _ in range(4)),
+        *(dma((seqs,)) for _ in range(6)),
+    ]
+    any_spec = pl.BlockSpec(memory_space=pl.ANY)
+    vmem_spec = pl.BlockSpec(memory_space=pltpu.VMEM)
+    return pl.pallas_call(
+        forward_kernel,
+        out_shape=[
+            jax.ShapeDtypeStruct((tokens, width), f32),
+            jax.ShapeDtypeStruct((width // TILE, TILE, tokens), bf),
+            jax.ShapeDtypeStruct((tokens, 512), bf),
+            jax.ShapeDtypeStruct(kv_shape, bf),
+            jax.ShapeDtypeStruct((tokens, 512), f32),
+            jax.ShapeDtypeStruct((tokens, 512), f32),
+            jax.ShapeDtypeStruct((tokens, 512), bf),
+            jax.ShapeDtypeStruct((tokens, 512), f32),
+            jax.ShapeDtypeStruct((tokens, 256), f32),
+            jax.ShapeDtypeStruct((seqs, 2, 1, 2 * rows), f32),
+        ],
+        in_specs=[any_spec] * len(hbm) + [vmem_spec] * len(vmem),
+        out_specs=[any_spec] * 9 + [vmem_spec],
+        scratch_shapes=scratch,
+        compiler_params=pltpu.CompilerParams(
+            collective_id=2, has_side_effects=True, vmem_limit_bytes=60 << 20
+        ),
+    )(*hbm, *vmem)
+
+
 def on_device(
     x_in,
     cot,
@@ -1042,49 +1291,16 @@
     devices = lax.axis_size("seq")
     own = lax.axis_index("seq")
     block_rows = local_rows * devices // block_order.shape[0]
-    query_factor = head_dim ** (-0.5)
     q_gain, k_gain = wide(query_gain), wide(key_gain)
     gain_one, gain_two = wide(norm1), wide(norm2)
 
-    def cut_columns(weight, half):
-        return lax.dynamic_slice_in_dim(weight, half * (width // 2), width // 2, 1)
-
     x_rows = x_in.reshape(row_total, width)
-    x_float = wide(x_rows)
-    x_normed = low(x_float * norm_scale(x_float) * gain_one)
-    key_raw = product(x_normed, w_key)
-    by_head = key_raw.reshape(row_total, kv_local, head_dim)
-    key_rows = low(by_head * norm_scale(by_head) * k_gain).reshape(row_total, -1)
-    value_rows = low(product(x_normed, w_value))
-    pair = jnp.concatenate([key_rows, value_rows], axis=1).reshape(sequences, local_rows, -1)
-    kv_width = kv_local * head_dim
-
-    seqs_of = sequences // CHUNKS
-    rows_of = row_total // CHUNKS
-
-    def gather(value):
-        slots = {0: value}
-        for mask in range(2, devices, 2):
-            slots[mask] = swap(value, "seq", mask)
-        for mask in range(0, devices, 2):
-            slots[mask + 1] = swap(slots[mask], "seq", 1)
-        return jnp.stack([slots[j] for j in range(devices)], axis=1).reshape(
-            seqs_of, devices * local_rows, -1
-        )
-
-    gathered = [gather(pair[c * seqs_of : (c + 1) * seqs_of]) for c in range(CHUNKS)]
-
-    query_raw = product(x_normed, w_query)
-    gate_pre = product(x_normed, w_gate_attn)
-    by_head = query_raw.reshape(row_total, q_local, head_dim)
-    query = low(by_head * norm_scale(by_head) * q_gain * query_factor)
-    gate_sig = jax.nn.sigmoid(gate_pre)
-
     query_pos = positions(block_order, own, local_rows, block_rows)
     key_pos = jnp.concatenate(
         [positions(block_order, own ^ j, local_rows, block_rows) for j in range(devices)]
     )
-    allowed = key_pos[None, :] <= query_pos[:, None]
+    key_column = key_pos[:, None]
+    query_row = jnp.concatenate([query_pos] * group)[None, :]
 
     domain_total = domain_weights.shape[0]
     domain_index = jnp.arange(domain_total, dtype=jnp.int32)
@@ -1092,46 +1308,21 @@
     picked = domain_ids.reshape(row_total)[:, None] == domain_index[None, :]
     row_scale = jnp.sum(jnp.where(picked, factor[None, :], 0.0), axis=1)
 
-    saved = []
-    for c in range(CHUNKS):
-        rows = slice(c * rows_of, (c + 1) * rows_of)
-        heads = (
-            query[rows]
-            .reshape(seqs_of, local_rows, kv_local, group, head_dim)
-            .transpose(0, 2, 3, 1, 4)
-        )
-        keys = gathered[c][..., :kv_width].reshape(seqs_of, -1, kv_local, head_dim)
-        values = gathered[c][..., kv_width:].reshape(seqs_of, -1, kv_local, head_dim)
-        scores = jnp.einsum("skgqd,spkd->skgqp", heads, keys, preferred_element_type=jnp.float32)
-        scores = jnp.where(allowed, scores, -1e30)
-        top = jnp.max(scores, axis=-1)
-        weights = jnp.where(allowed, jnp.exp(scores - top[..., None]), 0.0)
-        total = jnp.sum(weights, axis=-1)
-        mixed = jnp.einsum(
-            "skgqp,spkd->skgqd", low(weights), values, preferred_element_type=jnp.float32
-        )
-        attn_heads = mixed / total[..., None]
-        log_total = top + jnp.log(total)
-        attn_flat = attn_heads.transpose(0, 3, 1, 2, 4).reshape(rows_of, q_local * head_dim)
-        gated = low(attn_flat * gate_sig[rows])
-        attn_sum = head_sum(gated, w_out, product, cut_columns)
-        residual = x_float[rows] + attn_sum
-        log_total = log_total.reshape(seqs_of, kv_local, 1, group * local_rows)
-        saved.append((residual, attn_flat, gated, log_total))
-
-    residual, attn_flat, gated, log_total = (
-        jnp.concatenate([part[i] for part in saved], axis=0) for i in range(4)
+    h, xt, query, kv, attn, sig, gated, query_raw, key_raw, lse = forward_call(
+        (x_rows, w_query, w_key, w_value, w_gate_attn, w_out),
+        (gain_one[None, :], q_gain[None, :], k_gain[None, :], key_column, query_row),
+        (row_total, width, sequences, local_rows, devices),
     )
     out, x_grad, down, gate, up, wout, wga, wquery, wkey, wvalue, norms, gains, *_ = back_call(
         (
-            residual,
+            h,
             cot.reshape(row_total, width),
             x_rows,
-            x_normed.T.reshape(devices, width // devices, row_total),
-            query.reshape(row_total, q_local * head_dim),
-            jnp.concatenate(gathered, axis=0),
-            attn_flat,
-            gate_sig,
+            xt,
+            query,
+            kv.reshape(sequences, devices * local_rows, -1),
+            attn,
+            sig,
             gated,
             query_raw,
             key_raw,
@@ -1146,9 +1337,9 @@
         ),
         (
             row_scale[:, None],
-            log_total,
-            key_pos[:, None],
-            jnp.concatenate([query_pos] * group)[None, :],
+            lse,
+            key_column,
+            query_row,
             gain_one[None, :],
             gain_two[None, :],
             q_gain[None, :],

time: 529 us -> 447 us (0.84); the launches traced: 519 us -> 445 us
  Pallas kernels: 347 us -> 421 us
  local copies, waits for them, and re-layouts: 62 us -> 18.5 us
  waiting for transfers between devices: 42.2 us -> 0 us
  starting transfers between devices: 22.1 us -> 0 us
  other arithmetic: 24.5 us -> 4.65 us
  matrix products: 19.4 us -> 0 us
    pallas_call x0 -> x1, Pallas kernels: none -> 77.8 us  [forward_call(): pl.pallas_call(forward_kernel, out_shape=[jax.ShapeDtypeStruct((tokens, w...]
    ppermute x20 -> x0, waiting for transfers between devices: 42.2 us -> none  [swap(): return lax.ppermute(value, axis, [(i, i ^ mask) for i in range(size)])]
    ppermute x20 -> x0, starting transfers between devices: 22.1 us -> none  [swap(): return lax.ppermute(value, axis, [(i, i ^ mask) for i in range(size)])]
    dot_general x12 -> x0, matrix products: 19.4 us -> none  [the longest x8 11.8 us: product(): return jnp.dot(left, right, preferred_element_type=jnp.float32)]
    unnamed x93 -> x36, local copies, waits for them, and re-layouts: 28.9 us -> 12.7 us
    reshape x7 -> x0, local copies, waits for them, and re-layouts: 8.94 us -> none  [the longest x1 2.91 us: on_device(): by_head = query_raw.reshape(row_total, q_local, head_dim)]
    concatenate x7 -> x1, other arithmetic: 9.41 us -> 0.57 us  [on_device(): query_row = jnp.concatenate([query_pos] * group)[None, :]]
    convert_element_type x9 -> x0, other arithmetic: 8.6 us -> none  [the longest x7 5.15 us: low(): return value.astype(jnp.bfloat16)]
  transfers between devices with their start and end apart: 20 -> 0, of which waited for: 8 -> 0; matrix products, arithmetic and copies ran while one was open for 10% -> 0% of each run, Pallas kernels for 0% -> 0%
where the time goes in v4:
time: 447 us; the launch traced here: 445 us
  Pallas kernels  421 us (94%)
  local copies, waits for them, and re-layouts  18.5 us (4%)
  other arithmetic  4.65 us (1%)
    pallas_call x1, Pallas kernels, back_call(): pl.pallas_call(back_kernel, out_shape=[jax.ShapeDtypeStruct((tokens, widt...  343 us
    pallas_call x1, Pallas kernels, forward_call(): pl.pallas_call(forward_kernel, out_shape=[jax.ShapeDtypeStruct((tokens, w...  77.8 us
    unnamed x36, local copies, waits for them, and re-layouts  12.7 us

profile of v4, /device:TPU:0, one launch (start us, length us, event | category | flops | bytes accessed | tf_op | source)
XLA Modules:
  0.0 444.8 jit_solution(1355182993175901547)
XLA Ops:
  0.7 0.8 select_reduce_fusion.1
  1.7 1.0 copy.35.kpos_ref
  2.7 0.6 pad_add_fusion
  3.3 1.2 bitcast_convert_fusion
  4.4 1.3 broadcast_in_dim.132
  5.7 77.8 %shard_map.281 = (f32[512,2048]{1,0:T(8,128)}, bf16[8,256,512]{2,1,0:T(8,128)(2,1)}, bf16[512,512]{1,0:T(8,128)(2,1)}, bf16[4,8,128,512]{3,2,1,0:T(8,128)(2,1)},...) custom-call(bf16[512,2048]{1,0:T(8,128)(2,1)} %bitcast.23, ...), custom_call_target="tpu_custom_call" | custom-call | tf_op jit(solution)/shard_map/pallas_call | solution.py:1242
  83.5 0.0 copy-done.10
  83.5 0.1 select_reduce_fusion
  83.6 0.9 copy.36.factor_ref
  84.5 0.0 copy-done.9
  84.5 0.6 broadcast_in_dim.135
  85.1 343.0 %shard_map.282 = (bf16[512,2048]{1,0:T(8,128)(2,1)}, bf16[512,2048]{1,0:T(8,128)(2,1)}, f32[1536,256]{1,0:T(8,128)}, f32[256,1536]{1,0:T(8,128)}, f32[256,1536]{...) custom-call(f32[512,2048]{1,0:T(8,128)} %get-tuple-element.36.h_hbm,, ...), custom_call_target="tpu_custom_call" | custom-call | tf_op jit(solution)/shard_map/pallas_call | solution.py:963
  428.1 0.9 fusion.11
  429.1 0.6 constant_dynamic-slice_fusion.3
  429.6 0.6 constant_dynamic-slice_fusion
  430.2 0.7 fusion.12
  430.9 0.6 fusion.8
  431.5 0.6 fusion.9
  432.0 3.3 copy.56
  435.4 0.0 copy-start.5
  435.4 1.3 copy.57
  436.7 0.8 copy.58
  437.5 0.7 copy.59
  438.2 0.0 copy-done.7
  438.2 0.7 copy.60
  438.9 0.8 copy.61
  439.7 0.8 copy.62
  440.5 1.1 copy.63
  441.6 0.0 copy-done.2
  441.6 1.1 copy.64
  442.8 0.8 copy-done.1
  443.6 1.1 copy.65
  (34 shorter events, 0.2 us)
Async XLA Ops:
  5.7 77.8 %copy-start.11 = (s32[8]{0:T(128)S(1)}, s32[8]{0:T(128)}, u32[]{:S(2)}) copy-start(s32[8]{0:T(128)} %param.21) | copy-start | bytes 100
  5.7 77.8 %copy-start.12 = (f32[8]{0:T(128)S(1)}, f32[8]{0:T(128)}, u32[]{:S(2)}) copy-start(f32[8]{0:T(128)} %param.22) | copy-start | bytes 100
  5.7 77.8 %copy-start.10 = (s32[4,128]{1,0:T(4,128)S(1)}, s32[4,128]{1,0:T(4,128)}, u32[]{:S(2)}) copy-start(s32[4,128]{1,0:T(4,128)} %param.20) | copy-start | bytes 6148
  5.7 78.8 %copy-start.9 = (bf16[2048]{0:T(1024)(128)(2,1)S(1)}, bf16[2048]{0:T(1024)(128)(2,1)}, u32[]{:S(2)}) copy-start(bf16[2048]{0:T(1024)(128)(2,1)} %param.32) | copy-start | bytes 12292
  432.0 3.3 copy-start
  435.4 1.3 copy-start.6
  435.4 2.1 copy-start.8
  435.4 2.8 copy-start.7
  435.4 3.5 copy-start.5
  436.7 3.0 copy-start.4
  436.7 3.8 copy-start.3
  439.7 1.9 copy-start.2
  441.6 2.0 copy-start.1

commit v5 on v4

--- a/solution.py
+++ b/solution.py
@@ -55,6 +55,122 @@
 TILE = 256
 
 
+PLAN = {
+    "p1.0": (
+        ("a", 0),
+    ),
+    "p1.1": (
+        ("r1", 1),
+    ),
+    "p1.3": (
+        ("a", 1), ("r2", 1),
+    ),
+    "p1.4": (
+        ("a", 2), ("r1", 0), ("s1", 0),
+    ),
+    "p1.5": (
+        ("a", 3),
+    ),
+    "p2.0": (
+        ("r2", 0),
+    ),
+    "p2.2": (
+        ("s1", 1), ("a", 4), ("s2", 0), ("s1", 2),
+    ),
+    "p2.3": (
+        ("s1", 3), ("a", 5),
+    ),
+    "p2.5": (
+        ("s3", 0),
+    ),
+    "p2.6": (
+        ("a", 6), ("s2", 1), ("s1", 4),
+    ),
+    "p3.0": (
+        ("s4", 0), ("a", 7),
+    ),
+    "p3.2": (
+        ("s3", 1), ("s2", 2), ("s1", 5),
+    ),
+    "p3.3": (
+        ("a", 8),
+    ),
+    "p3.4": (
+        ("s4", 1),
+    ),
+    "p3.6": (
+        ("s2", 3), ("s1", 6), ("a", 9), ("s3", 2),
+    ),
+    "e0.3": (
+        ("s4", 2), ("s3", 3), ("s2", 4), ("s1", 7), ("a", 10),
+    ),
+    "p4b": (
+        ("s2", 5), ("s1", 8), ("a", 11), ("s3", 4),
+    ),
+    "p5.0": (
+        ("s2", 6), ("s1", 9), ("s3", 5),
+    ),
+    "p5.1": (
+        ("s2", 7), ("s1", 10), ("s3", 6),
+    ),
+    "p5.2": (
+        ("ky", 0), ("s2", 8), ("s3", 7),
+    ),
+    "p5.3": (
+        ("ky", 1), ("s2", 9), ("s3", 8),
+    ),
+    "qp": (
+        ("s2", 10), ("s1", 11),
+    ),
+    "e1.2": (
+        ("s3", 9),
+    ),
+    "e1.3": (
+        ("s4", 3), ("s4", 4), ("s4", 5), ("ky", 2), ("s4", 6), ("s4", 7), ("s4", 8),
+    ),
+    "e1.4": (
+        ("kl", 0),
+    ),
+    "op": (
+        ("s3", 10), ("s4", 9), ("km", 0), ("kl", 1), ("ky", 3), ("s4", 10), ("r1", 3), ("a", 12), ("km", 1),
+        ("s2", 11), ("r1", 2), ("a", 13), ("r2", 3), ("s3", 11), ("kl", 2), ("s1", 12), ("a", 14), ("r2", 2),
+        ("s4", 11), ("s1", 13), ("a", 15), ("km", 2), ("kl", 3), ("s1", 14), ("a", 16), ("km", 3), ("s2", 12),
+        ("s1", 15), ("a", 17),
+    ),
+    "p7.0": (
+        ("a", 18), ("s3", 12), ("s2", 13), ("s1", 16),
+    ),
+    "p7.2": (
+        ("a", 19), ("s4", 12),
+    ),
+    "p7.4": (
+        ("s3", 13), ("s2", 14), ("s1", 17), ("a", 20),
+    ),
+    "p7.6": (
+        ("s4", 13),
+    ),
+    "e2.1": (
+        ("s2", 15), ("s1", 18), ("a", 21), ("s3", 14),
+    ),
+    "e2.2": (
+        ("s4", 14), ("s3", 15), ("s2", 16), ("s1", 19), ("a", 22),
+    ),
+    "e2.3": (
+        ("s4", 15),
+    ),
+    "lp": (
+        ("s2", 17), ("s1", 20), ("a", 23), ("s3", 16),
+    ),
+    "vec": (
+        ("s2", 18), ("s1", 21), ("a", 24), ("s3", 17), ("s4", 16), ("s4", 17), ("s2", 19), ("s1", 22),
+        ("a", 25), ("s3", 18), ("s4", 18), ("s3", 19), ("s2", 20), ("s1", 23), ("s4", 19), ("s3", 20),
+        ("s2", 21), ("s1", 24), ("s4", 20), ("s2", 22), ("s1", 25), ("s3", 21), ("s4", 21), ("s3", 22),
+        ("s2", 23), ("s4", 22), ("s3", 23), ("s2", 24), ("s4", 23), ("s2", 25), ("s3", 24), ("s4", 24),
+        ("s3", 25), ("s4", 25),
+    ),
+}
+
+
 def other_z(z, t):
     low_z, high_z = lax.rem(z, 2), lax.div(z, 2)
     low_t, high_t = lax.rem(t, 2), lax.div(t, 2)
@@ -82,12 +198,12 @@
     wg_hbm, wu_hbm, wd_hbm, wo_hbm, wq_hbm, wk_hbm, wv_hbm, wga_hbm,
     factor_ref, lse_ref, kpos_ref, qpos_ref, n1_ref, n2_ref, qg_ref, kg_ref,
     block_out, x_out, dwd_out, dwg_out, dwu_out, dwo_out, dwga_out, dwq_out, dwk_out, dwv_out,
-    norms_out, gains_out, dh_hbm, zlo_hbm, zhi_hbm,
-    acts, lt, odd, csend, crecv, xrecv, fin, yrecv, lrecv, hrecv,
-    zlo_send, zhi_send, stage, ostage, wide_a, wide_b, delta,
+    norms_out, gains_out, dh_hbm, z1_hbm, z2_hbm, z3_hbm,
+    acts, lt, odd, csend, crecv, xrecv, fin, yrecv, lrecv, mrecv, hrecv,
+    zsend, stage, ostage, wide_a, wide_b, delta,
     vec, vec_got, gvec, gvec_got,
-    ya_s, ya_r, zl_s, zl_r, zh_s, zh_r, lt_s, lt_r, lc_s, lc_r,
-    c1_s, c1_r, x_s, x_r, c2_s, c2_r, ky_s, ky_r, kl_s, kl_r, kh_s, kh_r,
+    ya_s, ya_r, z1_s, z1_r, z2_s, z2_r, z3_s, z3_r, lt_s, lt_r, lc_s, lc_r, lx_s, lx_r, lf_s, lf_r,
+    c1_s, c1_r, x_s, x_r, c2_s, c2_r, ky_s, ky_r, kl_s, kl_r, km_s, km_r, kh_s, kh_r,
     nv_s, nv_r, gv_s, gv_r, st_sem, out_sem, misc, credit,
 ):
     seq, head = lax.axis_index("seq"), lax.axis_index("head")
@@ -96,8 +212,10 @@
     y_dev = {"seq": z * 2 + 1 - y}
     lo_dev = {"seq": other_z(z, 1) * 2 + y}
     hi_dev = {"seq": other_z(z, 2) * 2 + y}
+    mid_dev = {"seq": (3 - z) * 2 + y}
     core_dev = {"head": head + 1 - 2 * c}
     x_dev = {"head": head + 2 - 4 * lax.div(head, 2)}
+    at_end, inside = lax.rem(z, 3) == 0, lax.rem(z, 3) != 0
     tokens = cot_hbm.shape[0]
     rows = kpos_ref.shape[0] // 8
     seqs = tokens // rows
@@ -109,7 +227,16 @@
     barrier = pltpu.get_barrier_semaphore()
     for device in (y_dev, lo_dev, hi_dev, core_dev, x_dev):
         pl.semaphore_signal(barrier, inc=1, device_id=device, device_id_type=MESH)
-    pl.semaphore_wait(barrier, 5)
+
+    @pl.when(inside)
+    def _():
+        pl.semaphore_signal(barrier, inc=1, device_id=mid_dev, device_id_type=MESH)
+        pl.semaphore_wait(barrier, 6)
+
+    @pl.when(at_end)
+    def _():
+        pl.semaphore_wait(barrier, 5)
+
 
     def remote(src, dst, send, recv, device):
         return pltpu.make_async_remote_copy(
@@ -120,94 +247,103 @@
         return remote(acts.at[i, 0], acts.at[i, 1], ya_s.at[i], ya_r.at[i], y_dev)
 
     def lt_copy(l):
-        return remote(odd.at[l], lt.at[l, 1, pl.ds(2 * c, 2)], lt_s.at[l], lt_r.at[l], y_dev)
-
-    def lt_relay(l):
-        piece = lt.at[l, 1, pl.ds(2 * c, 2)]
+        return remote(odd.at[l], lt.at[l, 1, head], lt_s.at[l], lt_r.at[l], y_dev)
+
+    x_head = head + 2 - 4 * lax.div(head, 2)
+    core_head = head + 1 - 2 * c
+    far_head = x_head + 1 - 2 * c
+
+    def lt_core(l, part):
+        piece = lt.at[l, 1, part]
         return remote(piece, piece, lc_s.at[l], lc_r.at[l], core_dev)
 
-    def lt_relay_in(l):
-        piece = lt.at[l, 1, pl.ds(2 - 2 * c, 2)]
-        return remote(piece, piece, lc_s.at[l], lc_r.at[l], core_dev)
-
-    def zlo_copy(i):
-        return remote(zlo_send.at[lax.rem(i, 4)], zlo_hbm.at[i], zl_s.at[i], zl_r.at[i], lo_dev)
-
-    def zhi_copy(i):
-        return remote(zhi_send.at[lax.rem(i, 4)], zhi_hbm.at[i], zh_s.at[i], zh_r.at[i], hi_dev)
-
-    def item_dot(i, l, t):
-        return dot_plain(lt[l, 0, t], acts[i, 0]) + dot_plain(lt[l, 1, t], acts[i, 1])
-
-    def stage_one(i, l):
+    def lt_x(l, part):
+        piece = lt.at[l, 1, part]
+        return remote(piece, piece, lx_s.at[l], lx_r.at[l], x_dev)
+
+    def lt_far(l, part):
+        piece = lt.at[l, 1, part]
+        return remote(piece, piece, lf_s.at[l], lf_r.at[l], core_dev)
+
+    def z1_copy(i):
+        return remote(zsend.at[i % 4], z1_hbm.at[i], z1_s.at[i], z1_r.at[i], lo_dev)
+
+    def z2_copy(i):
+        return remote(zsend.at[i % 4, pl.ds(0, 2)], z2_hbm.at[i], z2_s.at[i], z2_r.at[i], mid_dev)
+
+    def z3_copy(i):
+        return remote(zsend.at[i % 4, 2], z3_hbm.at[i], z3_s.at[i], z3_r.at[i], lo_dev)
+
+    def item_dot(i, l, first, last):
+        count = (last - first) * TILE
+        mine = dot_plain(lt[l, 0, first:last].reshape(count, tokens), acts[i, 0])
+        return mine + dot_plain(lt[l, 1, first:last].reshape(count, tokens), acts[i, 1])
+
+    def stage_load(src, slot):
+        copy = pltpu.make_async_copy(src, stage.at[slot], st_sem.at[slot])
+        copy.start()
+        return copy
+
+    def stage_one(i, l, place):
         act_copy(i).wait_recv()
 
-        @pl.when(i >= 4)
+        @pl.when(at_end)
         def _():
-            zlo_copy(i - 4).wait_send()
-
-        slot = lax.rem(i, 4)
-        for k in range(2):
-            zlo_send[slot, k] = low(item_dot(i, l, 2 * k + 1))
-        zlo_copy(i).start()
-
-    def stage_two(i, l):
-        zlo_copy(i).wait_recv()
-        here = pltpu.make_async_copy(zlo_hbm.at[i, 1], stage.at[0], st_sem.at[0])
-        here.start()
-
-        @pl.when(i >= 4)
+            if i >= 4:
+                z1_copy(i - 4).wait_send()
+            total = item_dot(i, l, 1, 4)
+            for k in range(3):
+                zsend[i % 4, k] = low(total[k * TILE : (k + 1) * TILE])
+            z1_copy(i).start()
+
+    def stage_two(i, l, place):
+        @pl.when(inside)
         def _():
-            zhi_copy(i - 4).wait_send()
-
-        total = item_dot(i, l, 2)
-        here.wait()
-        zhi_send[lax.rem(i, 4)] = low(total + wide(stage[0]))
-        zhi_copy(i).start()
+            z1_copy(i).wait_recv()
+            loads = [stage_load(z1_hbm.at[i, k], k) for k in (1, 2)]
+            if i >= 4:
+                z2_copy(i - 4).wait_send()
+            total = item_dot(i, l, 2, 4)
+            for load in loads:
+                load.wait()
+            zsend[i % 4, 0] = low(total[:TILE] + wide(stage[2]))
+            zsend[i % 4, 1] = low(total[TILE:] + wide(stage[1]))
+            z2_copy(i).start()
 
     def out_wait(i):
-        slot = lax.rem(i, 2)
-        pltpu.make_async_copy(ostage.at[slot], dwk_out, out_sem.at[slot]).wait()
-
-    def stage_three(i, l, places):
-        zhi_copy(i).wait_recv()
-        one = pltpu.make_async_copy(zlo_hbm.at[i, 0], stage.at[1], st_sem.at[1])
-        two = pltpu.make_async_copy(zhi_hbm.at[i], stage.at[2], st_sem.at[2])
-        one.start()
-        two.start()
-
-        @pl.when(i >= 2)
+        pltpu.make_async_copy(ostage.at[i % 2], dwk_out, out_sem.at[i % 2]).wait()
+
+    def put(i, total, place):
+        ref, n, turned = place
+        if i >= 2:
+            out_wait(i - 2)
+        ostage[i % 2] = total.T if turned else total
+        at = pl.ds(n * TILE, TILE)
+        target = ref.at[at] if turned else ref.at[:, at]
+        pltpu.make_async_copy(ostage.at[i % 2], target, out_sem.at[i % 2]).start()
+
+    def stage_three(i, l, place):
+        @pl.when(inside)
         def _():
-            out_wait(i - 2)
-
-        total = item_dot(i, l, 0)
-        one.wait()
-        two.wait()
-        total = total + wide(stage[1]) + wide(stage[2])
-        slot = lax.rem(i, 2)
-        for chosen, ref, n, turned in places:
-
-            def put():
-                at = pl.ds(pl.multiple_of(n * TILE, TILE), TILE)
-                ostage[slot] = total.T if turned else total
-                target = ref.at[at] if turned else ref.at[:, at]
-                pltpu.make_async_copy(ostage.at[slot], target, out_sem.at[slot]).start()
-
-            if chosen is None:
-                put()
-            else:
-                pl.when(chosen)(put)
-
-    def ff_l(i):
-        return 1 - lax.div(lax.rem(i, 3) + 1, 2)
-
-    def ff_places(i):
-        kind, j = lax.rem(i, 3), lax.div(i, 3)
-        return (
-            (kind == 0, dwd_out, j, True),
-            (kind == 1, dwg_out, j, False),
-            (kind == 2, dwu_out, j, False),
-        )
+            z2_copy(i).wait_recv()
+            loads = [stage_load(z1_hbm.at[i, 0], 0), stage_load(z2_hbm.at[i, 0], 1), stage_load(z2_hbm.at[i, 1], 2)]
+            if i >= 4:
+                z3_copy(i - 4).wait_send()
+            total = item_dot(i, l, 0, 2)
+            for load in loads:
+                load.wait()
+            zsend[i % 4, 2] = low(total[TILE:] + wide(stage[1]))
+            z3_copy(i).start()
+            put(i, total[:TILE] + wide(stage[0]) + wide(stage[2]), place)
+
+    def stage_four(i, l, place):
+        @pl.when(at_end)
+        def _():
+            z3_copy(i).wait_recv()
+            load = stage_load(z3_hbm.at[i], 3)
+            total = item_dot(i, l, 0, 1)
+            load.wait()
+            put(i, total + wide(stage[3]), place)
 
     late = (
         (3, dwo_out, 0, True),
@@ -220,24 +356,37 @@
         (2, dwv_out, 0, False),
     )
     item_count = ff_items + 8
-    lead, lag = 4, 2
-
-    def tick(k, steady=False):
-        if steady or k + lead < item_count:
-            act_copy(k + lead).start()
-        for stage_of, i in ((stage_one, k), (stage_two, k - lag), (stage_three, k - 2 * lag)):
-            if not steady and not 0 <= i < item_count:
-                continue
-            is_ff = steady or i < ff_items
-            l = ff_l(i) if is_ff else late[i - ff_items][0]
-            if stage_of is stage_three:
-                if is_ff:
-                    stage_three(i, l, ff_places(i))
-                else:
-                    _, ref, n, turned = late[i - ff_items]
-                    stage_three(i, l, ((None, ref, n, turned),))
-            else:
-                stage_of(i, l)
+    shown = set()
+
+    def item_step(stage_of, i):
+        l = (1 if i % 3 == 0 else 0) if i < ff_items else late[i - ff_items][0]
+        if stage_of is stage_one and l not in shown:
+            shown.add(l)
+            relay_in(l)
+        if i < ff_items:
+            place = ((dwd_out, dwg_out, dwu_out)[i % 3], i // 3, i % 3 == 0)
+        else:
+            place = late[i - ff_items][1:]
+        stage_of(i, l, place)
+
+    actions = {
+        "a": lambda i: act_copy(i).start(),
+        "s1": lambda i: item_step(stage_one, i),
+        "s2": lambda i: item_step(stage_two, i),
+        "s3": lambda i: item_step(stage_three, i),
+        "s4": lambda i: item_step(stage_four, i),
+        "r1": lambda l: relay_one(l),
+        "r2": lambda l: relay_two(l),
+    }
+
+    def after(place):
+        for name, i in PLAN.get(place, ()):
+            actions[name](i)
+
+    def after_step(place, step, count):
+        for k in range(count):
+            if f"{place}.{k}" in PLAN:
+                pl.when(step == k)(lambda k=k: after(f"{place}.{k}"))
 
     def spread(l, source):
         @pl.loop(0, 4)
@@ -245,16 +394,21 @@
             at = pl.multiple_of((other_z(z, t) * 2 + y) * TILE, TILE)
             lt[l, 0, t] = source[:, pl.ds(at, TILE)].T
 
-        @pl.loop(0, 2)
-        def _(k):
-            at = pl.multiple_of((other_z(z, 2 * c + k) * 2 + 1 - y) * TILE, TILE)
-            odd[l, k] = source[:, pl.ds(at, TILE)].T
-
-        lt_copy(l).start()
-
-    def relay(l):
+        at = pl.multiple_of((other_z(z, head) * 2 + 1 - y) * TILE, TILE)
+        odd[l] = source[:, pl.ds(at, TILE)].T
+
+    def relay_one(l):
         lt_copy(l).wait_recv()
-        lt_relay(l).start()
+        lt_core(l, head).start()
+        lt_x(l, head).start()
+
+    def relay_two(l):
+        lt_x(l, x_head).wait_recv()
+        lt_far(l, x_head).start()
+
+    def relay_in(l):
+        lt_core(l, core_head).wait_recv()
+        lt_far(l, far_head).wait_recv()
 
     def core_copy(k, b):
         return remote(csend.at[b], crecv.at[k % 2, b], c1_s.at[k, b], c1_r.at[k, b], core_dev)
@@ -270,7 +424,7 @@
         piece = fin.at[k % 2, (1 - c) * 4 + b]
         return remote(piece, piece, c2_s.at[k, b], c2_r.at[k, b], core_dev)
 
-    def reduce_start(k, loads, compute, hooks=()):
+    def reduce_start(k, loads, compute, place):
         def block_of(step):
             return lax.rem(c + 1 + step, 2) * 4 + lax.div(step, 2)
 
@@ -301,24 +455,22 @@
                 fin[k % 2, c * 4 + b] = low(part + wide(crecv[k % 2, b]))
                 x_copy(k, b).start()
 
-            for when, hook in hooks:
-                pl.when(step == when)(hook)
+            after_step(place, step, 8)
 
         @pl.loop(0, 4)
         def _(b):
             core_copy(k, b).wait_send()
 
     def reduce_end(k):
-        @pl.loop(0, 4)
-        def _(b):
+        for b in range(4):
             x_copy(k, b).wait()
             fin[k % 2, c * 4 + b] = low(wide(fin[k % 2, c * 4 + b]) + wide(xrecv[k % 2, b]))
             fin_copy(k, b).start()
-
-        @pl.loop(0, 4)
-        def _(b):
+            after(f"e{k}.{b}")
+        for b in range(4):
             fin_copy_in(k, b).wait_recv()
             fin_copy(k, b).wait_send()
+        after(f"e{k}.4")
 
     def fin_rows(k, at, count):
         return jnp.concatenate([wide(fin[k % 2, n, pl.ds(at, count)]) for n in range(8)], axis=1)
@@ -366,6 +518,8 @@
             wide_b[at] = low(wide(cbuf[slot]) * factor_ref[at])
 
         spread(1, wide_b)
+        lt_copy(1).start()
+        after("p0")
 
         @pl.loop(0, hidden_tiles)
         def _(j):
@@ -391,20 +545,17 @@
                 acts[3 * j + 1, 0, at] = low(dm * u * sig * (1.0 + a * (1.0 - sig)))
                 acts[3 * j + 2, 0, at] = low(dm * act)
 
+            after_step("p1", j, 1)
+
             @pl.when(j == 0)
             def _():
-                act_copy(0).start()
                 spread(0, wide_a)
-                act_copy(1).start()
-                act_copy(2).start()
-
-            @pl.when(j == 1)
-            def _():
-                act_copy(3).start()
-
-            @pl.when(j == 3)
-            def _():
-                relay(1)
+                lt_copy(0).start()
+                after("sp0")
+
+            for k in range(1, hidden_tiles):
+                if f"p1.{k}" in PLAN:
+                    pl.when(j == k)(lambda k=k: after(f"p1.{k}"))
 
     pl.run_scoped(
         first_phase,
@@ -417,9 +568,6 @@
         pltpu.SemaphoreType.DMA((2, 3)),
     )
 
-    lt_relay_in(1).wait_recv()
-    tick(0)
-
     def second_phase(wa, wb, sems):
         def loads(n, slot):
             at = pl.ds(pl.multiple_of(n * TILE, TILE), TILE)
@@ -437,7 +585,7 @@
                 total = part if total is None else total + part
             return total
 
-        reduce_start(0, loads, compute, ((5, lambda: relay(0)),))
+        reduce_start(0, loads, compute, "p2")
 
     pl.run_scoped(
         second_phase,
@@ -445,9 +593,6 @@
         pltpu.VMEM((2, TILE, wg_hbm.shape[1]), jnp.bfloat16),
         pltpu.SemaphoreType.DMA((2, 2)),
     )
-
-    lt_relay_in(0).wait_recv()
-    tick(1)
 
     def third_phase(wa, sems):
         def loads(n, slot):
@@ -461,15 +606,13 @@
                 total = part if total is None else total + part
             return total
 
-        reduce_start(1, loads, compute)
+        reduce_start(1, loads, compute, "p3")
 
     pl.run_scoped(
         third_phase,
         pltpu.VMEM((2, wd_hbm.shape[0], TILE), jnp.bfloat16),
         pltpu.SemaphoreType.DMA((2,)),
     )
-
-    tick(2)
 
     base = ff_items
     for n in range(2):
@@ -481,24 +624,21 @@
         shard = other_z(z, t) * 2 + y
         return pltpu.make_async_copy(xt_hbm.at[shard], lt.at[2, 0, t], misc.at[2 + t])
 
-    def xt_odd(k):
-        shard = other_z(z, 2 * c + k) * 2 + 1 - y
-        return pltpu.make_async_copy(xt_hbm.at[shard], odd.at[2, k], misc.at[6 + k])
+    def xt_odd():
+        shard = other_z(z, head) * 2 + 1 - y
+        return pltpu.make_async_copy(xt_hbm.at[shard], odd.at[2], misc.at[6])
 
     for t in range(4):
         xt_own(t).start()
-    for k in range(2):
-        xt_odd(k).start()
+    xt_odd().start()
     for t in range(4):
         xt_own(t).wait()
-    for k in range(2):
-        xt_odd(k).wait()
+    xt_odd().wait()
     for n in range(2):
         pltpu.make_async_copy(
             y_hbm.at[:, pl.ds(n * TILE, TILE)], acts.at[base + n, 0], misc.at[n]
         ).wait()
-
-    tick(3)
+    after("xt")
     reduce_end(0)
 
     def fourth_phase(hbuf, cbuf, dbuf, wob, obuf, sbuf, sems, d_sems, w_sems):
@@ -559,7 +699,7 @@
         spill(n_chunks - 2, n_chunks % 2).wait()
         spill(n_chunks - 1, (n_chunks - 1) % 2).wait()
 
-        tick(4)
+        after("p4a")
         ones = jnp.ones((8, 128), jnp.bfloat16)
         for n in range(2):
             for copy in tile_loads(n):
@@ -577,6 +717,7 @@
                 delta[n, g] = dot_rows(ones, top) + dot_rows(ones, rest)
 
         spread(3, wide_a)
+        after("p4b")
         for device in (core_dev, x_dev):
             pl.semaphore_signal(credit, inc=1, device_id=device, device_id_type=MESH)
 
@@ -593,18 +734,50 @@
         pltpu.SemaphoreType.DMA((2, 3)),
     )
 
-    tick(5)
-
-    def attention_back(keep, ysend, lsend, hsend, dq_ref, dkv_ref):
+    def attention_back(keep, ysend, lsend, dq_ref, dkv_ref):
         def ky_copy(s):
             return remote(ysend.at[lax.rem(s, 2)], yrecv.at[s], ky_s.at[s], ky_r.at[s], y_dev)
 
         def kl_copy(s):
             return remote(lsend.at[s], lrecv.at[s], kl_s.at[s], kl_r.at[s], lo_dev)
 
+        def km_copy(s):
+            return remote(lsend.at[s, pl.ds(0, 2)], mrecv.at[s], km_s.at[s], km_r.at[s], mid_dev)
+
         def kh_copy(s):
-            return remote(hsend.at[s], hrecv.at[s], kh_s.at[s], kh_r.at[s], hi_dev)
-
+            return remote(lsend.at[s, 2], hrecv.at[s], kh_s.at[s], kh_r.at[s], lo_dev)
+
+        def ky_step(s):
+            ky_copy(s).wait_recv()
+            for m in range(4):
+                keep[s, m] += wide(yrecv[s, m])
+
+            @pl.when(at_end)
+            def _():
+                for k in range(3):
+                    lsend[s, k] = low(keep[s, k + 1])
+                kl_copy(s).start()
+
+        def kl_step(s):
+            @pl.when(inside)
+            def _():
+                kl_copy(s).wait_recv()
+                keep[s, 0] += wide(lrecv[s, 0])
+                lsend[s, 0] = low(keep[s, 2] + wide(lrecv[s, 2]))
+                lsend[s, 1] = low(keep[s, 3] + wide(lrecv[s, 1]))
+                km_copy(s).start()
+
+        def km_step(s):
+            @pl.when(inside)
+            def _():
+                km_copy(s).wait_recv()
+                keep[s, 0] += wide(mrecv[s, 1])
+                lsend[s, 2] = low(keep[s, 1] + wide(mrecv[s, 0]))
+                kh_copy(s).start()
+
+        actions["ky"] = ky_step
+        actions["kl"] = kl_step
+        actions["km"] = km_step
         keys_total = kpos_ref.shape[0]
 
         def fifth_phase(qbuf, kvbuf, q_sem, sems):
@@ -652,7 +825,7 @@
                         dq_ref[at, lanes[g]] = dq[g * rows : (g + 1) * rows]
 
                 ky_copy(s).start()
-                tick(6 + s, True)
+                after_step("p5", s, seqs)
 
         pl.run_scoped(
             fifth_phase,
@@ -662,21 +835,9 @@
             pltpu.SemaphoreType.DMA((2,)),
         )
 
+        lt_copy(3).start()
         lt_copy(2).start()
-        relay(3)
-        tick(6 + seqs)
-        tick(7 + seqs)
-
-        @pl.loop(0, seqs)
-        def _(s):
-            ky_copy(s).wait_recv()
-            for m in range(4):
-                keep[s, m] += wide(yrecv[s, m])
-            for k in range(2):
-                lsend[s, k] = low(keep[s, 2 * k + 1])
-            kl_copy(s).start()
-
-        tick(8 + seqs)
+        after("sl3")
 
         def query_phase(rbuf, sem):
             load = pltpu.make_async_copy(qraw_hbm, rbuf, sem)
@@ -700,16 +861,7 @@
         gvec[0] = jnp.zeros_like(gvec[0])
         pl.run_scoped(query_phase, pltpu.VMEM(qraw_hbm.shape, jnp.float32), pltpu.SemaphoreType.DMA)
 
-        @pl.loop(0, seqs)
-        def _(s):
-            kl_copy(s).wait_recv()
-            for k in range(2):
-                keep[s, 2 * k] += wide(lrecv[s, k])
-            hsend[s] = low(keep[s, 2])
-            kh_copy(s).start()
-
-        tick(9 + seqs)
-        relay(2)
+        after("qp")
         reduce_end(1)
 
         def out_phase(hbuf, obuf, sems, o_sems):
@@ -749,12 +901,20 @@
             pltpu.SemaphoreType.DMA((2,)),
         )
 
-        tick(10 + seqs)
+        after("op")
 
         @pl.loop(0, seqs)
         def _(s):
-            kh_copy(s).wait_recv()
-            dkv_ref[pl.ds(pl.multiple_of(s * rows, 128), rows)] = keep[s, 0] + wide(hrecv[s])
+            at = pl.ds(pl.multiple_of(s * rows, 128), rows)
+
+            @pl.when(inside)
+            def _():
+                dkv_ref[at] = keep[s, 0]
+
+            @pl.when(at_end)
+            def _():
+                kh_copy(s).wait_recv()
+                dkv_ref[at] = keep[s, 0] + wide(hrecv[s])
 
         def key_phase(rbuf, sem):
             load = pltpu.make_async_copy(kraw_hbm, rbuf, sem)
@@ -776,6 +936,7 @@
             acts[base + 7, 0] = low(dkv_ref[:, 256:512])
 
         pl.run_scoped(key_phase, pltpu.VMEM(kraw_hbm.shape, jnp.float32), pltpu.SemaphoreType.DMA)
+        after("kp")
 
         @pl.loop(seqs - 2, seqs)
         def _(s):
@@ -783,15 +944,20 @@
 
         @pl.loop(0, seqs)
         def _(s):
-            kl_copy(s).wait_send()
-            kh_copy(s).wait_send()
+            @pl.when(at_end)
+            def _():
+                kl_copy(s).wait_send()
+
+            @pl.when(inside)
+            def _():
+                km_copy(s).wait_send()
+                kh_copy(s).wait_send()
 
     pl.run_scoped(
         attention_back,
         pltpu.VMEM((seqs, 4, rows, 512), jnp.float32),
         pltpu.VMEM((2, 4, rows, 512), jnp.bfloat16),
-        pltpu.VMEM((seqs, 2, rows, 512), jnp.bfloat16),
-        pltpu.VMEM((seqs, rows, 512), jnp.bfloat16),
+        pltpu.VMEM((seqs, 3, rows, 512), jnp.bfloat16),
         pltpu.VMEM((tokens, 512), jnp.float32),
         pltpu.VMEM((tokens, 512), jnp.float32),
     )
@@ -821,7 +987,7 @@
             return total
 
         pl.semaphore_wait(credit, 2)
-        reduce_start(2, loads, compute, ((3, lambda: tick(11 + seqs)),))
+        reduce_start(2, loads, compute, "p7")
 
     pl.run_scoped(
         sixth_phase,
@@ -837,10 +1003,6 @@
         gvec[step + 1] = gvec[step] + gvec_got[step]
     gains_out[...] = gvec[5]
 
-    lt_relay_in(2).wait_recv()
-    lt_relay_in(3).wait_recv()
-    tick(12 + seqs)
-    tick(13 + seqs)
     reduce_end(2)
 
     def last_phase(xbuf, dbuf, obuf, sems, o_sems):
@@ -895,6 +1057,7 @@
         pltpu.SemaphoreType.DMA((2,)),
     )
 
+    after("lp")
     for step in range(3):
         device = (y_dev, lo_dev, hi_dev)[step]
         copy = remote(vec.at[step], vec_got.at[step], nv_s.at[step], nv_r.at[step], device)
@@ -903,25 +1066,31 @@
         vec[step + 1] = vec[step] + vec_got[step]
     norms_out[...] = vec[3]
 
-    for k in range(14 + seqs, item_count + 2 * lag):
-        tick(k)
+    after("vec")
 
     @pl.loop(0, item_count)
     def _(i):
         act_copy(i).wait_send()
 
-    @pl.loop(item_count - 4, item_count)
-    def _(i):
-        zlo_copy(i).wait_send()
-        zhi_copy(i).wait_send()
-
-    @pl.loop(item_count - 2, item_count)
-    def _(i):
+    for i in range(item_count - 4, item_count):
+
+        @pl.when(at_end)
+        def _():
+            z1_copy(i).wait_send()
+
+        @pl.when(inside)
+        def _():
+            z2_copy(i).wait_send()
+            z3_copy(i).wait_send()
+
+    for i in range(item_count - 2, item_count):
         out_wait(i)
 
     for l in range(4):
         lt_copy(l).wait_send()
-        lt_relay(l).wait_send()
+        lt_core(l, head).wait_send()
+        lt_x(l, head).wait_send()
+        lt_far(l, x_head).wait_send()
 
 
 def back_call(hbm, vmem, sizes):
@@ -932,17 +1101,17 @@
     scratch = [
         pltpu.VMEM((count, 2, tokens, TILE), bf),
         pltpu.VMEM((4, 2, 4, TILE, tokens), bf),
-        pltpu.VMEM((4, 2, TILE, tokens), bf),
+        pltpu.VMEM((4, TILE, tokens), bf),
         pltpu.VMEM((4, tokens, TILE), bf),
         pltpu.VMEM((2, 4, tokens, TILE), bf),
         pltpu.VMEM((2, 4, tokens, TILE), bf),
         pltpu.VMEM((2, 8, tokens, TILE), bf),
         pltpu.VMEM((seqs, 4, rows, 512), bf),
+        pltpu.VMEM((seqs, 3, rows, 512), bf),
         pltpu.VMEM((seqs, 2, rows, 512), bf),
         pltpu.VMEM((seqs, rows, 512), bf),
-        pltpu.VMEM((4, 2, TILE, TILE), bf),
+        pltpu.VMEM((4, 3, TILE, TILE), bf),
         pltpu.VMEM((4, TILE, TILE), bf),
-        pltpu.VMEM((3, TILE, TILE), bf),
         pltpu.VMEM((2, TILE, TILE), f32),
         pltpu.VMEM((tokens, width), bf),
         pltpu.VMEM((tokens, width), bf),
@@ -951,12 +1120,12 @@
         pltpu.VMEM((3, 8, width), f32),
         pltpu.VMEM((6, 8, 256), f32),
         pltpu.VMEM((5, 8, 256), f32),
-        *(dma((count,)) for _ in range(6)),
-        *(dma((4,)) for _ in range(4)),
+        *(dma((count,)) for _ in range(8)),
+        *(dma((4,)) for _ in range(8)),
         *(dma((3, 4)) for _ in range(6)),
-        *(dma((seqs,)) for _ in range(6)),
+        *(dma((seqs,)) for _ in range(8)),
         dma((3,)), dma((3,)), dma((5,)), dma((5,)),
-        dma((3,)), dma((2,)), dma((8,)), pltpu.SemaphoreType.REGULAR,
+        dma((4,)), dma((2,)), dma((8,)), pltpu.SemaphoreType.REGULAR,
     ]
     any_spec = pl.BlockSpec(memory_space=pl.ANY)
     vmem_spec = pl.BlockSpec(memory_space=pltpu.VMEM)
@@ -976,11 +1145,12 @@
             jax.ShapeDtypeStruct((8, width), f32),
             jax.ShapeDtypeStruct((8, 256), f32),
             jax.ShapeDtypeStruct((tokens, width), f32),
+            jax.ShapeDtypeStruct((count, 3, TILE, TILE), bf),
             jax.ShapeDtypeStruct((count, 2, TILE, TILE), bf),
             jax.ShapeDtypeStruct((count, TILE, TILE), bf),
         ],
         in_specs=[any_spec] * len(hbm) + [vmem_spec] * len(vmem),
-        out_specs=[any_spec] * 10 + [vmem_spec] * 2 + [any_spec] * 3,
+        out_specs=[any_spec] * 10 + [vmem_spec] * 2 + [any_spec] * 4,
         scratch_shapes=scratch,
         compiler_params=pltpu.CompilerParams(
             collective_id=1, has_side_effects=True, vmem_limit_bytes=61 << 20

time: 447 us -> 429 us (0.960)
  Pallas kernels: 421 us -> 399 us
    pallas_call x1, Pallas kernels: 343 us -> 321 us  [back_call(): pl.pallas_call(back_kernel, out_shape=[jax.ShapeDtypeStruct((tokens, widt...]
where the time goes in v5:
time: 429 us; the launch traced here: 423 us
  Pallas kernels  399 us (93%)
  local copies, waits for them, and re-layouts  18.5 us (4%)
  other arithmetic  4.65 us (1%)
    pallas_call x1, Pallas kernels, back_call(): pl.pallas_call(back_kernel, out_shape=[jax.ShapeDtypeStruct((tokens, widt...  321 us
    pallas_call x1, Pallas kernels, forward_call(): pl.pallas_call(forward_kernel, out_shape=[jax.ShapeDtypeStruct((tokens, w...  77.8 us
    unnamed x36, local copies, waits for them, and re-layouts  12.7 us

profile of v5, /device:TPU:0, one launch (start us, length us, event | category | flops | bytes accessed | tf_op | source)
XLA Modules:
  0.0 423.2 jit_solution(18288396930938569135)
XLA Ops:
  0.7 0.8 select_reduce_fusion.1
  1.7 1.0 copy.35.kpos_ref
  2.7 0.6 pad_add_fusion
  3.3 1.2 bitcast_convert_fusion
  4.4 1.3 broadcast_in_dim.132
  5.7 77.8 %shard_map.281 = (f32[512,2048]{1,0:T(8,128)}, bf16[8,256,512]{2,1,0:T(8,128)(2,1)}, bf16[512,512]{1,0:T(8,128)(2,1)}, bf16[4,8,128,512]{3,2,1,0:T(8,128)(2,1)},...) custom-call(bf16[512,2048]{1,0:T(8,128)(2,1)} %bitcast.23, ...), custom_call_target="tpu_custom_call" | custom-call | tf_op jit(solution)/shard_map/pallas_call | solution.py:1412
  83.5 0.0 copy-done.11
  83.5 0.0 copy-done.12
  83.5 0.0 copy-done.10
  83.5 0.1 select_reduce_fusion
  83.6 0.9 copy.36.factor_ref
  84.5 0.6 broadcast_in_dim.135
  85.1 321.3 %shard_map.282 = (bf16[512,2048]{1,0:T(8,128)(2,1)}, bf16[512,2048]{1,0:T(8,128)(2,1)}, f32[1536,256]{1,0:T(8,128)}, f32[256,1536]{1,0:T(8,128)}, f32[256,1536]{...) custom-call(f32[512,2048]{1,0:T(8,128)} %get-tuple-element.36.h_hbm,, ...), custom_call_target="tpu_custom_call" | custom-call | tf_op jit(solution)/shard_map/pallas_call | solution.py:1132
  406.4 0.9 fusion.11
  407.3 0.6 constant_dynamic-slice_fusion.3
  407.9 0.6 constant_dynamic-slice_fusion
  408.4 0.7 fusion.12
  409.1 0.6 fusion.8
  409.7 0.6 fusion.9
  410.3 3.3 copy.56
  413.6 1.3 copy.57
  414.9 0.0 copy-done.6
  415.0 0.8 copy.58
  415.8 0.7 copy.59
  416.5 0.7 copy.60
  417.2 0.8 copy.61
  418.0 0.0 copy-done.4
  418.0 0.8 copy.62
  418.8 1.1 copy.63
  419.9 1.1 copy.64
  421.1 0.8 copy-done.1
  421.9 1.1 copy.65
  (34 shorter events, 0.2 us)
Async XLA Ops:
  5.7 77.8 %copy-start.11 = (s32[8]{0:T(128)S(1)}, s32[8]{0:T(128)}, u32[]{:S(2)}) copy-start(s32[8]{0:T(128)} %param.21) | copy-start | bytes 100
  5.7 77.8 %copy-start.12 = (f32[8]{0:T(128)S(1)}, f32[8]{0:T(128)}, u32[]{:S(2)}) copy-start(f32[8]{0:T(128)} %param.22) | copy-start | bytes 100
  5.7 77.8 %copy-start.10 = (s32[4,128]{1,0:T(4,128)S(1)}, s32[4,128]{1,0:T(4,128)}, u32[]{:S(2)}) copy-start(s32[4,128]{1,0:T(4,128)} %param.20) | copy-start | bytes 6148
  5.7 78.8 %copy-start.9 = (bf16[2048]{0:T(1024)(128)(2,1)S(1)}, bf16[2048]{0:T(1024)(128)(2,1)}, u32[]{:S(2)}) copy-start(bf16[2048]{0:T(1024)(128)(2,1)} %param.32) | copy-start | bytes 12292
  410.3 3.3 copy-start
  413.6 1.3 copy-start.6
  413.6 2.1 copy-start.8
  413.6 2.8 copy-start.7
  413.6 3.5 copy-start.5
  415.0 3.0 copy-start.4
  415.0 3.8 copy-start.3
  418.0 1.9 copy-start.2
  419.9 2.0 copy-start.1

commit v6 on v5

--- a/solution.py
+++ b/solution.py
@@ -59,114 +59,104 @@
     "p1.0": (
         ("a", 0),
     ),
-    "p1.1": (
-        ("r1", 1),
-    ),
     "p1.3": (
-        ("a", 1), ("r2", 1),
-    ),
-    "p1.4": (
-        ("a", 2), ("r1", 0), ("s1", 0),
+        ("a", 1), ("s1", 0),
     ),
     "p1.5": (
-        ("a", 3),
+        ("a", 2), ("r1", 0),
     ),
     "p2.0": (
-        ("r2", 0),
+        ("a", 3), ("s1", 1),
+    ),
+    "p2.1": (
+        ("s2", 0),
     ),
     "p2.2": (
-        ("s1", 1), ("a", 4), ("s2", 0), ("s1", 2),
-    ),
-    "p2.3": (
-        ("s1", 3), ("a", 5),
-    ),
-    "p2.5": (
-        ("s3", 0),
+        ("r2", 0), ("a", 4), ("s1", 2),
+    ),
+    "p2.4": (
+        ("a", 5), ("s1", 3), ("s3", 0), ("s2", 1),
     ),
     "p2.6": (
-        ("a", 6), ("s2", 1), ("s1", 4),
+        ("a", 6), ("s1", 4), ("s4", 0),
     ),
     "p3.0": (
-        ("s4", 0), ("a", 7),
+        ("s2", 2), ("a", 7), ("s3", 1), ("s1", 5),
     ),
     "p3.2": (
-        ("s3", 1), ("s2", 2), ("s1", 5),
-    ),
-    "p3.3": (
-        ("a", 8),
+        ("a", 8), ("s4", 1), ("s2", 3), ("s1", 6), ("s3", 2),
     ),
     "p3.4": (
-        ("s4", 1),
+        ("a", 9),
     ),
     "p3.6": (
-        ("s2", 3), ("s1", 6), ("a", 9), ("s3", 2),
+        ("s2", 4), ("s1", 7), ("a", 10), ("s3", 3), ("s4", 2),
     ),
     "e0.3": (
-        ("s4", 2), ("s3", 3), ("s2", 4), ("s1", 7), ("a", 10),
+        ("s4", 3), ("s2", 5), ("s1", 8), ("a", 11), ("s3", 4),
     ),
     "p4b": (
-        ("s2", 5), ("s1", 8), ("a", 11), ("s3", 4),
+        ("s2", 6), ("s1", 9), ("a", 12), ("s3", 5),
     ),
     "p5.0": (
-        ("s2", 6), ("s1", 9), ("s3", 5),
+        ("s2", 7), ("s1", 10), ("s3", 6),
     ),
     "p5.1": (
-        ("s2", 7), ("s1", 10), ("s3", 6),
+        ("s2", 8), ("s1", 11), ("s3", 7),
     ),
     "p5.2": (
-        ("ky", 0), ("s2", 8), ("s3", 7),
+        ("ky", 0), ("s2", 9), ("s3", 8),
     ),
     "p5.3": (
-        ("ky", 1), ("s2", 9), ("s3", 8),
+        ("s2", 10), ("s1", 12), ("ky", 1), ("s3", 9),
     ),
     "qp": (
-        ("s2", 10), ("s1", 11),
-    ),
-    "e1.2": (
-        ("s3", 9),
+        ("s2", 11),
     ),
     "e1.3": (
-        ("s4", 3), ("s4", 4), ("s4", 5), ("ky", 2), ("s4", 6), ("s4", 7), ("s4", 8),
-    ),
-    "e1.4": (
-        ("kl", 0),
+        ("s4", 4), ("s4", 5), ("s3", 10), ("s4", 6), ("s4", 7), ("s4", 8), ("s4", 9), ("kl", 0), ("ky", 2),
     ),
     "op": (
-        ("s3", 10), ("s4", 9), ("km", 0), ("kl", 1), ("ky", 3), ("s4", 10), ("r1", 3), ("a", 12), ("km", 1),
-        ("s2", 11), ("r1", 2), ("a", 13), ("r2", 3), ("s3", 11), ("kl", 2), ("s1", 12), ("a", 14), ("r2", 2),
-        ("s4", 11), ("s1", 13), ("a", 15), ("km", 2), ("kl", 3), ("s1", 14), ("a", 16), ("km", 3), ("s2", 12),
-        ("s1", 15), ("a", 17),
+        ("s3", 11), ("s4", 10), ("s2", 12), ("km", 0), ("ky", 3), ("s4", 11), ("a", 13), ("kl", 1), ("r1", 3),
+        ("s3", 12), ("a", 14), ("r1", 2), ("s4", 12), ("kl", 2), ("km", 1), ("r2", 3), ("a", 15), ("s1", 13),
+        ("r2", 2), ("a", 16), ("kl", 3), ("s1", 14), ("km", 2), ("a", 17), ("s1", 15), ("s2", 13), ("km", 3),
+        ("a", 18), ("s1", 16),
+    ),
+    "kp": (
+        ("a", 19), ("s2", 14), ("s1", 17), ("s3", 13),
     ),
     "p7.0": (
-        ("a", 18), ("s3", 12), ("s2", 13), ("s1", 16),
+        ("a", 20),
+    ),
+    "p7.1": (
+        ("s2", 15), ("s1", 18),
     ),
     "p7.2": (
-        ("a", 19), ("s4", 12),
+        ("a", 21), ("s3", 14), ("s4", 13),
     ),
     "p7.4": (
-        ("s3", 13), ("s2", 14), ("s1", 17), ("a", 20),
-    ),
-    "p7.6": (
-        ("s4", 13),
+        ("s2", 16), ("s1", 19), ("a", 22), ("s3", 15), ("s4", 14),
+    ),
+    "p7.7": (
+        ("s2", 17), ("s1", 20), ("a", 23), ("s3", 16),
     ),
     "e2.1": (
-        ("s2", 15), ("s1", 18), ("a", 21), ("s3", 14),
+        ("s4", 15),
     ),
     "e2.2": (
-        ("s4", 14), ("s3", 15), ("s2", 16), ("s1", 19), ("a", 22),
+        ("s2", 18), ("s1", 21), ("a", 24), ("s3", 17),
     ),
     "e2.3": (
-        ("s4", 15),
+        ("s4", 16),
     ),
     "lp": (
-        ("s2", 17), ("s1", 20), ("a", 23), ("s3", 16),
+        ("s2", 19), ("s1", 22), ("a", 25), ("s3", 18),
     ),
     "vec": (
-        ("s2", 18), ("s1", 21), ("a", 24), ("s3", 17), ("s4", 16), ("s4", 17), ("s2", 19), ("s1", 22),
-        ("a", 25), ("s3", 18), ("s4", 18), ("s3", 19), ("s2", 20), ("s1", 23), ("s4", 19), ("s3", 20),
-        ("s2", 21), ("s1", 24), ("s4", 20), ("s2", 22), ("s1", 25), ("s3", 21), ("s4", 21), ("s3", 22),
-        ("s2", 23), ("s4", 22), ("s3", 23), ("s2", 24), ("s4", 23), ("s2", 25), ("s3", 24), ("s4", 24),
-        ("s3", 25), ("s4", 25),
+        ("s2", 20), ("s1", 23), ("s4", 17), ("s3", 19), ("s4", 18), ("s2", 21), ("s1", 24), ("s4", 19),
+        ("s3", 20), ("s2", 22), ("s1", 25), ("s3", 21), ("s4", 20), ("s4", 21), ("s2", 23), ("s3", 22),
+        ("s4", 22), ("s2", 24), ("s3", 23), ("s4", 23), ("s2", 25), ("s3", 24), ("s4", 24), ("s3", 25),
+        ("s4", 25),
     ),
 }
 
@@ -177,6 +167,40 @@
     return (low_z + low_t - 2 * low_z * low_t) + 2 * (high_z + high_t - 2 * high_z * high_t)
 
 
+def fill_bias(order_ref, bias, rows, z, y, seq):
+    block = bias.shape[0] // order_ref.shape[0]
+    each = rows // block
+    lane = lax.broadcasted_iota(jnp.int32, (block, bias.shape[1]), 1)
+    down = lax.broadcasted_iota(jnp.int32, (block, bias.shape[1]), 0)
+    within = lax.rem(lane, rows)
+    query = lax.rem(lane, block)
+    for i in range(each):
+        query += jnp.where(lax.div(within, block) == i, order_ref[seq * each + i] * block, 0)
+    for j in range(8):
+        other_y = 1 - y if j % 2 else y
+        device = other_z(z, j // 2) * 2 + other_y
+        for i in range(each):
+            key = order_ref[device * each + i] * block + down
+            bias[j * rows + i * block : j * rows + (i + 1) * block] = jnp.where(key <= query, 0.0, -1e30)
+
+
+def fill_factor(ids_ref, counts_ref, weights_ref, factor, total):
+    seqs, rows = ids_ref.shape
+    domains = counts_ref.shape[0]
+    across = jnp.zeros((seqs, rows), jnp.float32)
+    ids = ids_ref[...]
+    for d in range(domains):
+        count = jnp.full((seqs, rows), counts_ref[d], jnp.int32).astype(jnp.float32)
+        weight = jnp.full((seqs, rows), weights_ref[d], jnp.float32) * total / (domains * count)
+        across = jnp.where(ids == d, weight, across)
+    here = lax.broadcasted_iota(jnp.int32, (rows, rows), 0) == lax.broadcasted_iota(
+        jnp.int32, (rows, rows), 1
+    )
+    for s in range(seqs):
+        spread = jnp.where(here, across[s : s + 1], 0.0)
+        factor[s * rows : (s + 1) * rows] = jnp.sum(spread, axis=1, keepdims=True)
+
+
 def dot_plain(left, right):
     return jnp.dot(left, right, preferred_element_type=jnp.float32)
 
@@ -194,14 +218,14 @@
 
 
 def back_kernel(
-    h_hbm, cot_hbm, x_hbm, xt_hbm, q_hbm, kv_hbm, o_hbm, sig_hbm, y_hbm, qraw_hbm, kraw_hbm,
+    h_hbm, cot_hbm, x_hbm, xt_hbm, ltd_hbm, dm_hbm, q_hbm, kv_hbm, o_hbm, sig_hbm, y_hbm, qraw_hbm, kraw_hbm,
     wg_hbm, wu_hbm, wd_hbm, wo_hbm, wq_hbm, wk_hbm, wv_hbm, wga_hbm,
-    factor_ref, lse_ref, kpos_ref, qpos_ref, n1_ref, n2_ref, qg_ref, kg_ref,
+    ids_ref, lse_ref, n1_ref, n2_ref, qg_ref, kg_ref, order_ref, counts_ref, weights_ref,
     block_out, x_out, dwd_out, dwg_out, dwu_out, dwo_out, dwga_out, dwq_out, dwk_out, dwv_out,
-    norms_out, gains_out, dh_hbm, z1_hbm, z2_hbm, z3_hbm,
+    n1_out, n2_out, qg_out, kg_out, dh_hbm, z1_hbm, z2_hbm, z3_hbm,
     acts, lt, odd, csend, crecv, xrecv, fin, yrecv, lrecv, mrecv, hrecv,
     zsend, stage, ostage, wide_a, wide_b, delta,
-    vec, vec_got, gvec, gvec_got,
+    vec, vec_got, gvec, gvec_got, bias, factor_ref,
     ya_s, ya_r, z1_s, z1_r, z2_s, z2_r, z3_s, z3_r, lt_s, lt_r, lc_s, lc_r, lx_s, lx_r, lf_s, lf_r,
     c1_s, c1_r, x_s, x_r, c2_s, c2_r, ky_s, ky_r, kl_s, kl_r, km_s, km_r, kh_s, kh_r,
     nv_s, nv_r, gv_s, gv_r, st_sem, out_sem, misc, credit,
@@ -217,7 +241,7 @@
     x_dev = {"head": head + 2 - 4 * lax.div(head, 2)}
     at_end, inside = lax.rem(z, 3) == 0, lax.rem(z, 3) != 0
     tokens = cot_hbm.shape[0]
-    rows = kpos_ref.shape[0] // 8
+    rows = bias.shape[0] // 8
     seqs = tokens // rows
     hidden_tiles = wd_hbm.shape[0] // TILE
     ff_items = 3 * hidden_tiles
@@ -237,6 +261,9 @@
     def _():
         pl.semaphore_wait(barrier, 5)
 
+
+    fill_bias(order_ref, bias, rows, z, y, seq)
+    fill_factor(ids_ref, counts_ref, weights_ref, factor_ref, float(tokens * 8))
 
     def remote(src, dst, send, recv, device):
         return pltpu.make_async_remote_copy(
@@ -345,6 +372,13 @@
             load.wait()
             put(i, total + wide(stage[3]), place)
 
+    def at_tile(j, kind):
+        later = j // 3 if isinstance(j, int) else lax.div(j, 3)
+        if kind == 0:
+            return j + 2 * j * later
+        return (2 + 2 * j + kind) * (1 - later) + (3 * j + kind) * later
+
+    ff_kind = {at_tile(j, kind): (j, kind) for j in range(hidden_tiles) for kind in range(3)}
     late = (
         (3, dwo_out, 0, True),
         (3, dwo_out, 1, True),
@@ -357,14 +391,19 @@
     )
     item_count = ff_items + 8
     shown = set()
+    ltd_load = pltpu.make_async_copy(ltd_hbm, lt.at[1], misc.at[7])
 
     def item_step(stage_of, i):
-        l = (1 if i % 3 == 0 else 0) if i < ff_items else late[i - ff_items][0]
+        l = (1 if ff_kind[i][1] == 0 else 0) if i < ff_items else late[i - ff_items][0]
         if stage_of is stage_one and l not in shown:
             shown.add(l)
-            relay_in(l)
+            if l == 1:
+                ltd_load.wait()
+            else:
+                relay_in(l)
         if i < ff_items:
-            place = ((dwd_out, dwg_out, dwu_out)[i % 3], i // 3, i % 3 == 0)
+            j, kind = ff_kind[i]
+            place = ((dwd_out, dwg_out, dwu_out)[kind], j, kind == 0)
         else:
             place = late[i - ff_items][1:]
         stage_of(i, l, place)
@@ -480,26 +519,22 @@
 
     n_chunks = tokens // 128
 
-    def first_phase(hbuf, cbuf, wgb, wub, wdb, sems, w_sems):
-        def row_loads(r, slot):
-            at = pl.ds(r * 128, 128)
-            return (
-                pltpu.make_async_copy(h_hbm.at[at], hbuf.at[slot], sems.at[slot, 0]),
-                pltpu.make_async_copy(cot_hbm.at[at], cbuf.at[slot], sems.at[slot, 1]),
-            )
+    def first_phase(hbuf, wgb, wub, dmb, sems, w_sems):
+        def row_load(r, slot):
+            return pltpu.make_async_copy(h_hbm.at[pl.ds(r * 128, 128)], hbuf.at[slot], sems.at[slot])
 
         def tile_loads(j, slot):
             at = pl.ds(pl.multiple_of(j * TILE, TILE), TILE)
             return (
                 pltpu.make_async_copy(wg_hbm.at[:, at], wgb.at[slot], w_sems.at[slot, 0]),
                 pltpu.make_async_copy(wu_hbm.at[:, at], wub.at[slot], w_sems.at[slot, 1]),
-                pltpu.make_async_copy(wd_hbm.at[at], wdb.at[slot], w_sems.at[slot, 2]),
+                pltpu.make_async_copy(dm_hbm.at[j], dmb.at[slot], w_sems.at[slot, 2]),
             )
 
-        for copy in row_loads(0, 0):
-            copy.start()
+        row_load(0, 0).start()
         for copy in tile_loads(0, 0):
             copy.start()
+        ltd_load.start()
 
         @pl.loop(0, n_chunks)
         def _(r):
@@ -507,18 +542,13 @@
 
             @pl.when(r < n_chunks - 1)
             def _():
-                for copy in row_loads(r + 1, 1 - slot):
-                    copy.start()
-
-            for copy in row_loads(r, slot):
-                copy.wait()
+                row_load(r + 1, 1 - slot).start()
+
+            row_load(r, slot).wait()
             value = hbuf[slot]
             at = pl.ds(pl.multiple_of(r * 128, 128), 128)
-            wide_a[at] = low(value * rms(value) * n2_ref[...])
-            wide_b[at] = low(wide(cbuf[slot]) * factor_ref[at])
-
-        spread(1, wide_b)
-        lt_copy(1).start()
+            wide_a[at] = low(value * rms(value) * wide(n2_ref[...]))
+
         after("p0")
 
         @pl.loop(0, hidden_tiles)
@@ -538,12 +568,12 @@
                 at = pl.ds(pl.multiple_of(half * (tokens // 2), 128), tokens // 2)
                 a = dot_plain(wide_a[at], wgb[slot])
                 u = dot_plain(wide_a[at], wub[slot])
-                dm = dot_rows(wide_b[at], wdb[slot])
+                dm = dmb[slot, at]
                 sig = jax.nn.sigmoid(a)
                 act = a * sig
-                acts[3 * j, 0, at] = low(act * u)
-                acts[3 * j + 1, 0, at] = low(dm * u * sig * (1.0 + a * (1.0 - sig)))
-                acts[3 * j + 2, 0, at] = low(dm * act)
+                acts[at_tile(j, 0), 0, at] = low(act * u)
+                acts[at_tile(j, 1), 0, at] = low(dm * u * sig * (1.0 + a * (1.0 - sig)))
+                acts[at_tile(j, 2), 0, at] = low(dm * act)
 
             after_step("p1", j, 1)
 
@@ -560,11 +590,10 @@
     pl.run_scoped(
         first_phase,
         pltpu.VMEM((2, 128, width), jnp.float32),
-        pltpu.VMEM((2, 128, width), jnp.bfloat16),
         pltpu.VMEM((2, width, TILE), jnp.bfloat16),
         pltpu.VMEM((2, width, TILE), jnp.bfloat16),
-        pltpu.VMEM((2, TILE, width), jnp.bfloat16),
-        pltpu.SemaphoreType.DMA((2, 2)),
+        pltpu.VMEM((2, tokens, TILE), jnp.float32),
+        pltpu.SemaphoreType.DMA((2,)),
         pltpu.SemaphoreType.DMA((2, 3)),
     )
 
@@ -580,8 +609,8 @@
             total = None
             for j in range(hidden_tiles):
                 at = pl.ds(j * TILE, TILE)
-                part = dot_rows(acts[3 * j + 1, 0], wa[slot, :, at])
-                part += dot_rows(acts[3 * j + 2, 0], wb[slot, :, at])
+                part = dot_rows(acts[at_tile(j, 1), 0], wa[slot, :, at])
+                part += dot_rows(acts[at_tile(j, 2), 0], wb[slot, :, at])
                 total = part if total is None else total + part
             return total
 
@@ -602,7 +631,7 @@
         def compute(slot):
             total = None
             for j in range(hidden_tiles):
-                part = dot_plain(acts[3 * j, 0], wa[slot, pl.ds(j * TILE, TILE)])
+                part = dot_plain(acts[at_tile(j, 0), 0], wa[slot, pl.ds(j * TILE, TILE)])
                 total = part if total is None else total + part
             return total
 
@@ -689,7 +718,7 @@
             normed = value * scale
             grad = fin_rows(0, pl.multiple_of(r * 128, 128), 128)
             vec[0, 1:2] += jnp.sum(grad * normed, axis=0, keepdims=True)
-            scaled = grad * n2_ref[...]
+            scaled = grad * wide(n2_ref[...])
             inner = jnp.mean(scaled * normed, axis=-1, keepdims=True)
             dh = wide(cbuf[slot]) * factor_ref[at] + scale * (scaled - normed * inner)
             dbuf[slot] = dh
@@ -778,7 +807,7 @@
         actions["ky"] = ky_step
         actions["kl"] = kl_step
         actions["km"] = km_step
-        keys_total = kpos_ref.shape[0]
+        keys_total = bias.shape[0]
 
         def fifth_phase(qbuf, kvbuf, q_sem, sems):
             def kv_load(s, slot):
@@ -803,7 +832,6 @@
                 def _():
                     ky_copy(s - 2).wait_send()
 
-                allowed = kpos_ref[...] <= qpos_ref[...]
                 for n in range(2):
                     lanes = [slice((2 * n + g) * 128, (2 * n + g + 1) * 128) for g in range(2)]
                     key = kvbuf[slot, :, n * 128 : (n + 1) * 128]
@@ -812,7 +840,7 @@
                     do = jnp.concatenate([wide_b[at, lane] for lane in lanes], axis=0)
                     drow = jnp.concatenate([delta[n, g, 0:1, at] for g in range(2)], axis=1)
                     scores = dot_rows(key, q)
-                    probs = jnp.exp(jnp.where(allowed, scores - lse_ref[s, n], -1e30))
+                    probs = jnp.exp(scores - lse_ref[s, n] + bias[...])
                     grad_probs = dot_rows(value, do)
                     ds = low(probs * (grad_probs - drow))
                     for start, grad in ((0, dot_plain(ds, q)), (256, dot_plain(low(probs), do))):
@@ -854,7 +882,7 @@
                     jnp.sum(grad * normed * factor, axis=0, keepdims=True)
                     + (gvec[0, 0:1, 0:128] if hd else 0.0)
                 )
-                scaled = grad * (qg_ref[...] * factor)
+                scaled = grad * (wide(qg_ref[...]) * factor)
                 out = scale * (scaled - normed * jnp.mean(scaled * normed, axis=-1, keepdims=True))
                 acts[base + 4 + hd // 2, 0, :, (hd % 2) * 128 : (hd % 2 + 1) * 128] = low(out)
 
@@ -930,7 +958,7 @@
                     jnp.sum(grad * normed, axis=0, keepdims=True)
                     + (gvec[0, 0:1, 128:256] if hd else 0.0)
                 )
-                scaled = grad * kg_ref[...]
+                scaled = grad * wide(kg_ref[...])
                 out = scale * (scaled - normed * jnp.mean(scaled * normed, axis=-1, keepdims=True))
                 acts[base + 6, 0, :, lane] = low(out)
             acts[base + 7, 0] = low(dkv_ref[:, 256:512])
@@ -1001,7 +1029,10 @@
         copy.start()
         copy.wait()
         gvec[step + 1] = gvec[step] + gvec_got[step]
-    gains_out[...] = gvec[5]
+    piece = qg_out.shape[1]
+    turn = lax.rem(128 - seq * piece, 128)
+    for out, at in ((qg_out, 0), (kg_out, 128)):
+        out[...] = pltpu.roll(gvec[5, :, at : at + 128], turn, 1)[0:1, 0:piece]
 
     reduce_end(2)
 
@@ -1040,7 +1071,7 @@
             normed = value * scale
             grad = fin_rows(2, pl.multiple_of(r * 128, 128), 128)
             vec[0, 0:1] += jnp.sum(grad * normed, axis=0, keepdims=True)
-            scaled = grad * n1_ref[...]
+            scaled = grad * wide(n1_ref[...])
             inner = jnp.mean(scaled * normed, axis=-1, keepdims=True)
             obuf[slot] = low(dbuf[slot] + scale * (scaled - normed * inner))
             store(r, slot).start()
@@ -1064,7 +1095,9 @@
         copy.start()
         copy.wait()
         vec[step + 1] = vec[step] + vec_got[step]
-    norms_out[...] = vec[3]
+    own = pl.ds(pl.multiple_of(seq * TILE, TILE), TILE)
+    n1_out[...] = vec[3, 0:1, own]
+    n2_out[...] = vec[3, 1:2, own]
 
     after("vec")
 
@@ -1086,14 +1119,14 @@
     for i in range(item_count - 2, item_count):
         out_wait(i)
 
-    for l in range(4):
+    for l in (0, 2, 3):
         lt_copy(l).wait_send()
         lt_core(l, head).wait_send()
         lt_x(l, head).wait_send()
         lt_far(l, x_head).wait_send()
 
 
-def back_call(hbm, vmem, sizes):
+def back_call(hbm, vmem, smem, sizes):
     tokens, width, seqs, rows, keys_total, hidden = sizes
     count = 3 * (hidden // TILE) + 8
     bf, f32 = jnp.bfloat16, jnp.float32
@@ -1120,6 +1153,8 @@
         pltpu.VMEM((3, 8, width), f32),
         pltpu.VMEM((6, 8, 256), f32),
         pltpu.VMEM((5, 8, 256), f32),
+        pltpu.VMEM((keys_total, 2 * rows), f32),
+        pltpu.VMEM((tokens, 1), f32),
         *(dma((count,)) for _ in range(8)),
         *(dma((4,)) for _ in range(8)),
         *(dma((3, 4)) for _ in range(6)),
@@ -1129,6 +1164,7 @@
     ]
     any_spec = pl.BlockSpec(memory_space=pl.ANY)
     vmem_spec = pl.BlockSpec(memory_space=pltpu.VMEM)
+    smem_spec = pl.BlockSpec(memory_space=pltpu.SMEM)
     return pl.pallas_call(
         back_kernel,
         out_shape=[
@@ -1142,35 +1178,39 @@
             jax.ShapeDtypeStruct((TILE, 512), f32),
             jax.ShapeDtypeStruct((TILE, TILE), f32),
             jax.ShapeDtypeStruct((TILE, TILE), f32),
-            jax.ShapeDtypeStruct((8, width), f32),
-            jax.ShapeDtypeStruct((8, 256), f32),
+            jax.ShapeDtypeStruct((1, width // 8), f32),
+            jax.ShapeDtypeStruct((1, width // 8), f32),
+            jax.ShapeDtypeStruct((1, 16), f32),
+            jax.ShapeDtypeStruct((1, 16), f32),
             jax.ShapeDtypeStruct((tokens, width), f32),
             jax.ShapeDtypeStruct((count, 3, TILE, TILE), bf),
             jax.ShapeDtypeStruct((count, 2, TILE, TILE), bf),
             jax.ShapeDtypeStruct((count, TILE, TILE), bf),
         ],
-        in_specs=[any_spec] * len(hbm) + [vmem_spec] * len(vmem),
-        out_specs=[any_spec] * 10 + [vmem_spec] * 2 + [any_spec] * 4,
+        in_specs=[any_spec] * len(hbm) + [vmem_spec] * len(vmem) + [smem_spec] * len(smem),
+        out_specs=[any_spec] * 10 + [vmem_spec] * 4 + [any_spec] * 4,
         scratch_shapes=scratch,
         compiler_params=pltpu.CompilerParams(
             collective_id=1, has_side_effects=True, vmem_limit_bytes=61 << 20
         ),
-    )(*hbm, *vmem)
+    )(*hbm, *vmem, *smem)
 
 
 def forward_kernel(
-    x_hbm, wq_hbm, wk_hbm, wv_hbm, wga_hbm, wo_hbm,
-    n1_ref, qg_ref, kg_ref, kpos_ref, qpos_ref,
-    h_out, xt_out, q_out, kv_out, o_out, sig_out, y_out, qraw_out, kraw_out, lse_ref,
+    x_hbm, wq_hbm, wk_hbm, wv_hbm, wga_hbm, wo_hbm, cot_hbm, wd_hbm,
+    ids_ref, n1_ref, qg_ref, kg_ref, order_ref, counts_ref, weights_ref,
+    h_out, xt_out, q_out, kv_out, o_out, sig_out, y_out, qraw_out, kraw_out, ltd_out, dm_out, lse_ref,
     xv, xn, wqv, wkv, wvv, wgav, wov, kv, qv, qraw, kraw, sig, ov, yv, xtv, hv,
+    dout, ltd, odd, wdv, dmv, bias, factor_ref,
     csend, crecv, fin, xrecv,
-    x_sem, w_sem, out_sem, h_sem, kz_s, kz_r, ky_s, ky_r, c1_s, c1_r, x_s, x_r, c2_s, c2_r,
+    x_sem, w_sem, out_sem, h_sem, kz_s, kz_r, kf_s, ky_s, ky_r, l_sem, d_sem, m_sem, c1_s, c1_r, x_s, x_r, c2_s, c2_r,
 ):
     seq, head = lax.axis_index("seq"), lax.axis_index("head")
     z, y = lax.div(seq, 2), lax.rem(seq, 2)
     c = lax.rem(head, 2)
     y_dev = {"seq": z * 2 + 1 - y}
-    z_dev = [None] + [{"seq": other_z(z, t) * 2 + y} for t in (1, 2, 3)]
+    lo_dev, mid_dev = {"seq": other_z(z, 1) * 2 + y}, {"seq": (3 - z) * 2 + y}
+    at_end, inside = lax.rem(z, 3) == 0, lax.rem(z, 3) != 0
     core_dev = {"head": head + 1 - 2 * c}
     x_dev = {"head": head + 2 - 4 * lax.div(head, 2)}
     seqs, slots, rows = kv.shape[0], kv.shape[1], kv.shape[2]
@@ -1197,19 +1237,41 @@
         x_load(s).start()
     for load in weight_loads:
         load.start()
+    for s in range(seqs):
+        pltpu.make_async_copy(cot_hbm.at[rows_at(s)], dout.at[rows_at(s)], d_sem.at[s]).start()
 
     barrier = pltpu.get_barrier_semaphore()
-    for device in (y_dev, *z_dev[1:], core_dev, x_dev):
+    for device in (y_dev, lo_dev, core_dev, x_dev):
         pl.semaphore_signal(barrier, inc=1, device_id=device, device_id_type=MESH)
-    pl.semaphore_wait(barrier, 6)
+
+    @pl.when(inside)
+    def _():
+        pl.semaphore_signal(barrier, inc=1, device_id=mid_dev, device_id_type=MESH)
+        pl.semaphore_wait(barrier, 5)
+
+    @pl.when(at_end)
+    def _():
+        pl.semaphore_wait(barrier, 4)
 
     def remote(src, dst, send, recv, device):
         return pltpu.make_async_remote_copy(
             src_ref=src, dst_ref=dst, send_sem=send, recv_sem=recv, device_id=device, device_id_type=MESH
         )
 
-    def z_copy(s, t):
-        return remote(kv.at[s, 0], kv.at[s, 2 * t], kz_s.at[s, t], kz_r.at[s, t], z_dev[t])
+    def own_out(s):
+        return remote(kv.at[s, 0], kv.at[s, 2], kz_s.at[s, 1], kz_r.at[s, 1], lo_dev)
+
+    def own_over(s):
+        return remote(kv.at[s, 0], kv.at[s, 6], kz_s.at[s, 3], kz_r.at[s, 3], mid_dev)
+
+    def end_over(s):
+        return remote(kv.at[s, 2], kv.at[s, 4], kz_s.at[s, 2], kz_r.at[s, 2], mid_dev)
+
+    def mid_out(s):
+        return remote(kv.at[s, 6], kv.at[s, 4], kf_s.at[s, 0], kz_r.at[s, 2], lo_dev)
+
+    def far_out(s):
+        return remote(kv.at[s, 4], kv.at[s, 6], kf_s.at[s, 1], kz_r.at[s, 3], lo_dev)
 
     def y_copy(s, t):
         return remote(kv.at[s, 2 * t], kv.at[s, 2 * t + 1], ky_s.at[s, t], ky_r.at[s, t], y_dev)
@@ -1226,30 +1288,29 @@
     def fin_copy_in(s):
         piece = fin.at[s, 1 - c]
         return remote(piece, piece, c2_s.at[s], c2_r.at[s], core_dev)
+
+    weight_loads[0].wait()
+    weight_loads[1].wait()
 
     @pl.loop(0, seqs)
     def _(s):
         x_load(s).wait()
         at = rows_at(s)
         value = wide(xv[at])
-        xn[at] = low(value * rms(value) * n1_ref[...])
-
-    weight_loads[0].wait()
-    weight_loads[1].wait()
-
-    @pl.loop(0, seqs)
-    def _(s):
-        at = rows_at(s)
+        xn[at] = low(value * rms(value) * wide(n1_ref[...]))
         raw = dot_plain(xn[at], wkv[...])
         kraw[at] = raw
         for n in range(2):
             lane = slice(n * 128, (n + 1) * 128)
             part = raw[:, lane]
-            kv[s, 0, :, lane] = low(part * rms(part) * kg_ref[...])
+            kv[s, 0, :, lane] = low(part * rms(part) * wide(kg_ref[...]))
         kv[s, 0, :, 256:512] = low(dot_plain(xn[at], wvv[...]))
         y_copy(s, 0).start()
-        for t in (1, 2, 3):
-            z_copy(s, t).start()
+        own_out(s).start()
+
+        @pl.when(inside)
+        def _():
+            own_over(s).start()
 
     outs = []
 
@@ -1261,9 +1322,62 @@
     leave(kraw, kraw_out)
 
     def forward_keys(s):
-        for t in (1, 2, 3):
-            z_copy(s, t).wait_recv()
-            y_copy(s, t).start()
+        own_out(s).wait_recv()
+
+        @pl.when(inside)
+        def _():
+            end_over(s).start()
+            y_copy(s, 1).start()
+            own_over(s).wait_recv()
+            mid_out(s).start()
+            y_copy(s, 3).start()
+            end_over(s).wait_recv()
+            far_out(s).start()
+            y_copy(s, 2).start()
+
+        @pl.when(at_end)
+        def _():
+            y_copy(s, 1).start()
+            mid_out(s).wait_recv()
+            y_copy(s, 2).start()
+            far_out(s).wait_recv()
+            y_copy(s, 3).start()
+
+    hidden_tiles = wd_hbm.shape[0] // TILE
+
+    def cot_load(s):
+        return pltpu.make_async_copy(cot_hbm.at[rows_at(s)], dout.at[rows_at(s)], d_sem.at[s])
+
+    def wd_load(j):
+        at = pl.ds(pl.multiple_of(j * TILE, TILE), TILE)
+        return pltpu.make_async_copy(wd_hbm.at[at], wdv.at[lax.rem(j, 2)], l_sem.at[lax.rem(j, 2)])
+
+    def dm_store(j):
+        return pltpu.make_async_copy(dmv.at[lax.rem(j, 2)], dm_out.at[j], m_sem.at[lax.rem(j, 2)])
+
+    def spread_copy():
+        return remote(odd, ltd.at[1, pl.ds(2 * c, 2)], l_sem.at[2], l_sem.at[3], y_dev)
+
+    def relay_copy(part):
+        piece = ltd.at[1, pl.ds(2 * part, 2)]
+        return remote(piece, piece, l_sem.at[4], l_sem.at[5], core_dev)
+
+    def dm_tile(j):
+        @pl.when(j < hidden_tiles - 1)
+        def _():
+            wd_load(j + 1).start()
+
+        wd_load(j).wait()
+
+        @pl.when(j >= 2)
+        def _():
+            dm_store(j - 2).wait()
+
+        dmv[lax.rem(j, 2)] = dot_rows(dout[...], wdv[lax.rem(j, 2)])
+        dm_store(j).start()
+
+    fill_bias(order_ref, bias, rows, z, y, seq)
+    fill_factor(ids_ref, counts_ref, weights_ref, factor_ref, float(tokens * 8))
 
     weight_loads[2].wait()
     weight_loads[3].wait()
@@ -1277,7 +1391,7 @@
         for n in range(4):
             lane = slice(n * 128, (n + 1) * 128)
             part = raw[:, lane]
-            qv[at, lane] = low(part * rms(part) * (qg_ref[...] * scale_q))
+            qv[at, lane] = low(part * rms(part) * (wide(qg_ref[...]) * scale_q))
         sig[at] = jax.nn.sigmoid(dot_plain(xn[at], wgav[...]))
 
     leave(qraw, qraw_out)
@@ -1291,6 +1405,24 @@
         xtv[n] = xn[:, at].T
 
     leave(xtv, xt_out)
+    wd_load(0).start()
+
+    @pl.loop(0, seqs)
+    def _(s):
+        cot_load(s).wait()
+        at = rows_at(s)
+        dout[at] = low(wide(dout[at]) * factor_ref[at])
+
+    @pl.loop(0, 4)
+    def _(t):
+        at = pl.multiple_of((other_z(z, t) * 2 + y) * TILE, TILE)
+        ltd[0, t] = dout[:, pl.ds(at, TILE)].T
+
+    @pl.loop(0, 2)
+    def _(k):
+        at = pl.multiple_of((other_z(z, 2 * c + k) * 2 + 1 - y) * TILE, TILE)
+        odd[k] = dout[:, pl.ds(at, TILE)].T
+
     weight_loads[4].wait()
 
     def finish(s):
@@ -1319,16 +1451,22 @@
         def _():
             forward_keys(s + 1)
 
+            @pl.when(s == seqs - 2)
+            def _():
+                spread_copy().start()
+
+            dm_tile(2 * s)
+            dm_tile(2 * s + 1)
+
         for t in range(4):
             y_copy(s, t).wait_recv()
         at = rows_at(s)
-        allowed = kpos_ref[...] <= qpos_ref[...]
         for n in range(2):
             lanes = [slice((2 * n + g) * 128, (2 * n + g + 1) * 128) for g in range(2)]
             key = kv[s, :, :, n * 128 : (n + 1) * 128].reshape(slots * rows, 128)
             value = kv[s, :, :, 256 + n * 128 : 256 + (n + 1) * 128].reshape(slots * rows, 128)
             q = jnp.concatenate([qv[at, lane] for lane in lanes], axis=0)
-            scores = jnp.where(allowed, dot_rows(key, q), -1e30)
+            scores = dot_rows(key, q) + bias[...]
             top = jnp.max(scores, axis=0, keepdims=True)
             probs = jnp.exp(scores - top)
             total = jnp.sum(probs, axis=0, keepdims=True)
@@ -1359,25 +1497,38 @@
     leave(ov, o_out)
     leave(yv, y_out)
     finish_rows(seqs - 2)
+    spread_copy().wait_recv()
+    relay_copy(c).start()
     finish(seqs - 1)
     finish_rows(seqs - 1)
     h_store(seqs - 2, seqs % 2).wait()
     h_store(seqs - 1, (seqs - 1) % 2).wait()
+    relay_copy(1 - c).wait_recv()
+    leave(ltd, ltd_out)
+    spread_copy().wait_send()
+    relay_copy(c).wait_send()
+    dm_store(hidden_tiles - 2).wait()
+    dm_store(hidden_tiles - 1).wait()
     for copy in outs:
         copy.wait()
 
     @pl.loop(0, seqs)
     def _(s):
-        for t in (1, 2, 3):
-            z_copy(s, t).wait_send()
+        own_out(s).wait_send()
+
+        @pl.when(inside)
+        def _():
+            for copy in (own_over, end_over, mid_out, far_out):
+                copy(s).wait_send()
+
         for t in range(4):
             y_copy(s, t).wait_send()
         core_copy(s).wait_send()
         fin_copy(s).wait_send()
 
 
-def forward_call(hbm, vmem, sizes):
-    tokens, width, seqs, rows, slots = sizes
+def forward_call(hbm, vmem, smem, sizes):
+    tokens, width, seqs, rows, slots, hidden = sizes
     bf, f32 = jnp.bfloat16, jnp.float32
     dma = pltpu.SemaphoreType.DMA
     half = width // 2
@@ -1399,16 +1550,25 @@
         pltpu.VMEM((tokens, 512), bf),
         pltpu.VMEM((width // TILE, TILE, tokens), bf),
         pltpu.VMEM((2, rows, width), f32),
+        pltpu.VMEM((tokens, width), bf),
+        pltpu.VMEM((2, 4, TILE, tokens), bf),
+        pltpu.VMEM((2, TILE, tokens), bf),
+        pltpu.VMEM((2, TILE, width), bf),
+        pltpu.VMEM((2, tokens, TILE), f32),
+        pltpu.VMEM((slots * rows, 2 * rows), f32),
+        pltpu.VMEM((tokens, 1), f32),
         pltpu.VMEM((seqs, rows, half), bf),
         pltpu.VMEM((seqs, rows, half), bf),
         pltpu.VMEM((seqs, 2, rows, half), bf),
         pltpu.VMEM((seqs, rows, half), bf),
-        dma((seqs,)), dma((5,)), dma((8,)), dma((2,)),
-        *(dma((seqs, 4)) for _ in range(4)),
+        dma((seqs,)), dma((5,)), dma((9,)), dma((2,)),
+        *(dma((seqs, 4)) for _ in range(5)),
+        dma((6,)), dma((seqs,)), dma((2,)),
         *(dma((seqs,)) for _ in range(6)),
     ]
     any_spec = pl.BlockSpec(memory_space=pl.ANY)
     vmem_spec = pl.BlockSpec(memory_space=pltpu.VMEM)
+    smem_spec = pl.BlockSpec(memory_space=pltpu.SMEM)
     return pl.pallas_call(
         forward_kernel,
         out_shape=[
@@ -1421,15 +1581,17 @@
             jax.ShapeDtypeStruct((tokens, 512), bf),
             jax.ShapeDtypeStruct((tokens, 512), f32),
             jax.ShapeDtypeStruct((tokens, 256), f32),
+            jax.ShapeDtypeStruct((2, 4, TILE, tokens), bf),
+            jax.ShapeDtypeStruct((hidden // TILE, tokens, TILE), f32),
             jax.ShapeDtypeStruct((seqs, 2, 1, 2 * rows), f32),
         ],
-        in_specs=[any_spec] * len(hbm) + [vmem_spec] * len(vmem),
-        out_specs=[any_spec] * 9 + [vmem_spec],
+        in_specs=[any_spec] * len(hbm) + [vmem_spec] * len(vmem) + [smem_spec] * len(smem),
+        out_specs=[any_spec] * 11 + [vmem_spec],
         scratch_shapes=scratch,
         compiler_params=pltpu.CompilerParams(
             collective_id=2, has_side_effects=True, vmem_limit_bytes=60 << 20
         ),
-    )(*hbm, *vmem)
+    )(*hbm, *vmem, *smem)
 
 
 def on_device(
@@ -1454,41 +1616,23 @@
 ):
     sequences, local_rows, width = x_in.shape
     row_total = sequences * local_rows
-    head_dim = query_gain.shape[0]
-    kv_local = w_key.shape[1] // head_dim
-    q_local = w_query.shape[1] // head_dim
-    group = q_local // kv_local
     devices = lax.axis_size("seq")
-    own = lax.axis_index("seq")
-    block_rows = local_rows * devices // block_order.shape[0]
-    q_gain, k_gain = wide(query_gain), wide(key_gain)
-    gain_one, gain_two = wide(norm1), wide(norm2)
-
     x_rows = x_in.reshape(row_total, width)
-    query_pos = positions(block_order, own, local_rows, block_rows)
-    key_pos = jnp.concatenate(
-        [positions(block_order, own ^ j, local_rows, block_rows) for j in range(devices)]
-    )
-    key_column = key_pos[:, None]
-    query_row = jnp.concatenate([query_pos] * group)[None, :]
-
-    domain_total = domain_weights.shape[0]
-    domain_index = jnp.arange(domain_total, dtype=jnp.int32)
-    factor = domain_weights * (row_total * devices) / (domain_total * wide(domain_counts))
-    picked = domain_ids.reshape(row_total)[:, None] == domain_index[None, :]
-    row_scale = jnp.sum(jnp.where(picked, factor[None, :], 0.0), axis=1)
-
-    h, xt, query, kv, attn, sig, gated, query_raw, key_raw, lse = forward_call(
-        (x_rows, w_query, w_key, w_value, w_gate_attn, w_out),
-        (gain_one[None, :], q_gain[None, :], k_gain[None, :], key_column, query_row),
-        (row_total, width, sequences, local_rows, devices),
-    )
-    out, x_grad, down, gate, up, wout, wga, wquery, wkey, wvalue, norms, gains, *_ = back_call(
+    scalars = (block_order, domain_counts, domain_weights)
+    h, xt, query, kv, attn, sig, gated, query_raw, key_raw, ltd, dm, lse = forward_call(
+        (x_rows, w_query, w_key, w_value, w_gate_attn, w_out, cot.reshape(row_total, width), w_down),
+        (domain_ids, norm1[None, :], query_gain[None, :], key_gain[None, :]),
+        scalars,
+        (row_total, width, sequences, local_rows, devices, w_down.shape[0]),
+    )
+    out, x_grad, down, gate, up, wout, wga, wquery, wkey, wvalue, *small = back_call(
         (
             h,
             cot.reshape(row_total, width),
             x_rows,
             xt,
+            ltd,
+            dm,
             query,
             kv.reshape(sequences, devices * local_rows, -1),
             attn,
@@ -1506,34 +1650,29 @@
             w_gate_attn,
         ),
         (
-            row_scale[:, None],
+            domain_ids,
             lse,
-            key_column,
-            query_row,
-            gain_one[None, :],
-            gain_two[None, :],
-            q_gain[None, :],
-            k_gain[None, :],
+            norm1[None, :],
+            norm2[None, :],
+            query_gain[None, :],
+            key_gain[None, :],
         ),
+        scalars,
         (row_total, width, sequences, local_rows, local_rows * devices, w_down.shape[0]),
     )
-
-    def own_part(value):
-        size = value.shape[0] // devices
-        return lax.dynamic_slice_in_dim(value, own * size, size, 0)
 
     return (
         out.reshape(x_in.shape),
         x_grad.reshape(x_in.shape),
-        own_part(norms[0]),
+        small[0].reshape(-1),
         wquery,
         wkey,
         wvalue,
         wga,
         wout,
-        own_part(gains[0, :head_dim]),
-        own_part(gains[0, head_dim:]),
-        own_part(norms[1]),
+        small[2].reshape(-1),
+        small[3].reshape(-1),
+        small[1].reshape(-1),
         gate,
         up,
         down,

time: 429 us -> 411 us (0.958)
  Pallas kernels: 399 us -> 386 us
  other arithmetic: 4.65 us -> 0 us
    pallas_call x1, Pallas kernels: 321 us -> 310 us  [back_call(): pl.pallas_call(back_kernel, out_shape=[jax.ShapeDtypeStruct((tokens, widt...]
    unnamed x36 -> x40, local copies, waits for them, and re-layouts: 12.7 us -> 14.9 us
where the time goes in v6:
time: 411 us; the launch traced here: 405 us
  Pallas kernels  386 us (94%)
  local copies, waits for them, and re-layouts  17.5 us (4%)
    pallas_call x1, Pallas kernels, back_call(): pl.pallas_call(back_kernel, out_shape=[jax.ShapeDtypeStruct((tokens, widt...  310 us
    pallas_call x1, Pallas kernels, forward_call(): pl.pallas_call(forward_kernel, out_shape=[jax.ShapeDtypeStruct((tokens, w...  76.2 us
    unnamed x40, local copies, waits for them, and re-layouts  14.9 us

profile of v6, /device:TPU:0, one launch (start us, length us, event | category | flops | bytes accessed | tf_op | source)
XLA Modules:
  0.0 404.8 jit_solution(2881719600428137901)
XLA Ops:
  0.6 1.3 broadcast_in_dim.15.n1_ref
  1.9 1.3 broadcast_in_dim.18.n2_ref
  3.2 76.2 %shard_map.281 = (f32[512,2048]{1,0:T(8,128)}, bf16[8,256,512]{2,1,0:T(8,128)(2,1)}, bf16[512,512]{1,0:T(8,128)(2,1)}, bf16[4,8,128,512]{3,2,1,0:T(8,128)(2,1)},...) custom-call(bf16[512,2048]{1,0:T(8,128)(2,1)} %bitcast.11, ...), custom_call_target="tpu_custom_call" | custom-call | tf_op jit(solution)/shard_map/pallas_call | solution.py:1572
  79.5 310.2 %shard_map.282 = (bf16[512,2048]{1,0:T(8,128)(2,1)}, bf16[512,2048]{1,0:T(8,128)(2,1)}, f32[1536,256]{1,0:T(8,128)}, f32[256,1536]{1,0:T(8,128)}, f32[256,1536]{...) custom-call(f32[512,2048]{1,0:T(8,128)} %get-tuple-element.40.h_hbm,, ...), custom_call_target="tpu_custom_call" | custom-call | tf_op jit(solution)/shard_map/pallas_call | solution.py:1168
  389.7 0.0 copy-start
  389.7 3.3 copy.46
  393.0 0.0 copy-done
  393.0 0.0 copy-start.7
  393.0 1.3 copy.47
  394.3 0.0 copy-done.10
  394.3 0.6 copy.48
  394.9 0.0 copy-done.6
  394.9 0.0 copy-start.3
  394.9 0.8 copy.49
  395.7 0.0 copy-done.8
  395.7 0.7 copy.50
  396.4 0.0 copy-done.7
  396.4 0.7 copy.51
  397.1 0.0 copy-done.5
  397.1 0.8 copy.52
  397.9 0.0 copy-done.4
  397.9 0.8 copy.53
  398.7 0.0 copy-done.12
  398.7 0.5 copy.54
  399.2 0.0 copy-done.11
  399.2 0.5 copy.55
  399.7 0.6 copy.56
  400.3 0.0 copy-done.3
  400.3 1.1 copy.57
  401.5 1.1 copy.58
  402.6 0.8 copy-done.1
  403.4 1.1 copy.59
  (12 shorter events, 0.0 us)
Async XLA Ops:
  389.7 3.3 copy-start
  393.0 1.3 copy-start.10
  393.0 1.9 copy-start.6
  393.0 2.7 copy-start.8
  393.0 3.4 copy-start.7
  394.3 2.8 copy-start.5
  394.3 3.6 copy-start.4
  394.9 3.8 copy-start.12
  394.9 4.3 %copy-start.11 = (f32[1,16]{1,0:T(1,128)S(1)}, f32[1,16]{1,0:T(1,128)}, u32[]{:S(2)}) copy-start(f32[1,16]{1,0:T(1,128)} %get-tuple-element.61) | copy-start | bytes 196
  394.9 4.8 %copy-start.9 = (f32[1,256]{1,0:T(1,128)S(1)}, f32[1,256]{1,0:T(1,128)}, u32[]{:S(2)}) copy-start(f32[1,256]{1,0:T(1,128)} %get-tuple-element.62) | copy-start | bytes 3076
  394.9 5.4 %copy-start.3 = (f32[256,1536]{1,0:T(8,128)S(1)}, f32[256,1536]{1,0:T(8,128)}, u32[]{:S(2)}) copy-start(f32[256,1536]{1,0:T(8,128)} %get-tuple-element.91) | copy-start | bytes 4718596
  397.9 3.5 copy-start.2
  401.5 2.0 copy-start.1

commit v7 on v6

--- a/solution.py
+++ b/solution.py
@@ -1,3 +1,5 @@
+import functools
+
 import jax
 import jax.numpy as jnp
 from jax import lax
@@ -262,9 +264,6 @@
         pl.semaphore_wait(barrier, 5)
 
 
-    fill_bias(order_ref, bias, rows, z, y, seq)
-    fill_factor(ids_ref, counts_ref, weights_ref, factor_ref, float(tokens * 8))
-
     def remote(src, dst, send, recv, device):
         return pltpu.make_async_remote_copy(
             src_ref=src, dst_ref=dst, send_sem=send, recv_sem=recv, device_id=device, device_id_type=MESH
@@ -667,6 +666,8 @@
         pltpu.make_async_copy(
             y_hbm.at[:, pl.ds(n * TILE, TILE)], acts.at[base + n, 0], misc.at[n]
         ).wait()
+    fill_bias(order_ref, bias, rows, z, y, seq)
+    fill_factor(ids_ref, counts_ref, weights_ref, factor_ref, float(tokens * 8))
     after("xt")
     reduce_end(0)
 
@@ -1196,6 +1197,35 @@
     )(*hbm, *vmem, *smem)
 
 
+def hand_over_kernel(count, *refs):
+    src, dst, held, sems = refs[:count], refs[count : 2 * count], refs[2 * count : -1], refs[-1]
+    into = [pltpu.make_async_copy(src[i], held[i], sems.at[0, i]) for i in range(count)]
+    out = [pltpu.make_async_copy(held[i], dst[i], sems.at[1, i]) for i in range(count)]
+    for copy in into:
+        copy.start()
+    for i in range(count):
+        into[i].wait()
+        out[i].start()
+    for copy in out:
+        copy.wait()
+
+
+def hand_over(arrays):
+    any_spec = pl.BlockSpec(memory_space=pl.ANY)
+    count = len(arrays)
+    return pl.pallas_call(
+        functools.partial(hand_over_kernel, count),
+        out_shape=[jax.ShapeDtypeStruct(a.shape, a.dtype) for a in arrays],
+        in_specs=[any_spec] * count,
+        out_specs=[any_spec] * count,
+        scratch_shapes=[
+            *(pltpu.VMEM(a.shape, a.dtype) for a in arrays),
+            pltpu.SemaphoreType.DMA((2, count)),
+        ],
+        compiler_params=pltpu.CompilerParams(vmem_limit_bytes=61 << 20),
+    )(*arrays)
+
+
 def forward_kernel(
     x_hbm, wq_hbm, wk_hbm, wv_hbm, wga_hbm, wo_hbm, cot_hbm, wd_hbm,
     ids_ref, n1_ref, qg_ref, kg_ref, order_ref, counts_ref, weights_ref,
@@ -1661,6 +1691,9 @@
         (row_total, width, sequences, local_rows, local_rows * devices, w_down.shape[0]),
     )
 
+    out, x_grad, down, gate, up, wout, wga, wquery, wkey, wvalue, *small = hand_over(
+        (out, x_grad, down, gate, up, wout, wga, wquery, wkey, wvalue, *small[:4])
+    )
     return (
         out.reshape(x_in.shape),
         x_grad.reshape(x_in.shape),

time: 411 us -> 404 us (0.983)
  local copies, waits for them, and re-layouts: 17.5 us -> 2.58 us
  Pallas kernels: 386 us -> 394 us
    unnamed x40 -> x0, local copies, waits for them, and re-layouts: 14.9 us -> none
    pallas_call x0 -> x1, Pallas kernels: none -> 7.99 us  [hand_over(): pl.pallas_call(functools.partial(hand_over_kernel, count), out_shape=[jax...]
where the time goes in v7:
time: 404 us; the launch traced here: 398 us
  Pallas kernels  394 us (98%)
    pallas_call x1, Pallas kernels, back_call(): pl.pallas_call(back_kernel, out_shape=[jax.ShapeDtypeStruct((tokens, widt...  310 us
    pallas_call x1, Pallas kernels, forward_call(): pl.pallas_call(forward_kernel, out_shape=[jax.ShapeDtypeStruct((tokens, w...  76.2 us

profile of v7, /device:TPU:0, one launch (start us, length us, event | category | flops | bytes accessed | tf_op | source)
XLA Modules:
  0.0 397.9 jit_solution(8142722470457159843)
XLA Ops:
  0.6 1.3 broadcast_in_dim.15.n1_ref
  1.9 1.3 broadcast_in_dim.18.n2_ref
  3.2 76.2 %shard_map.281 = (f32[512,2048]{1,0:T(8,128)}, bf16[8,256,512]{2,1,0:T(8,128)(2,1)}, bf16[512,512]{1,0:T(8,128)(2,1)}, bf16[4,8,128,512]{3,2,1,0:T(8,128)(2,1)},...) custom-call(bf16[512,2048]{1,0:T(8,128)(2,1)} %bitcast.11, ...), custom_call_target="tpu_custom_call" | custom-call | tf_op jit(solution)/shard_map/pallas_call | solution.py:1602
  79.5 310.2 %shard_map.282 = (bf16[512,2048]{1,0:T(8,128)(2,1)}, bf16[512,2048]{1,0:T(8,128)(2,1)}, f32[1536,256]{1,0:T(8,128)}, f32[256,1536]{1,0:T(8,128)}, f32[256,1536]{...) custom-call(f32[512,2048]{1,0:T(8,128)} %get-tuple-element.54.h_hbm,, ...), custom_call_target="tpu_custom_call" | custom-call | tf_op jit(solution)/shard_map/pallas_call | solution.py:1169
  389.7 8.0 %shard_map.283 = (bf16[512,2048]{1,0:T(8,128)(2,1)}, bf16[512,2048]{1,0:T(8,128)(2,1)}, f32[1536,256]{1,0:T(8,128)}, f32[256,1536]{1,0:T(8,128)}, f32[256,1536]{...) custom-call(bf16[512,2048]{1,0:T(8,128)(2,1)} %get-tuple-element.66., ...), custom_call_target="tpu_custom_call" | custom-call | tf_op jit(solution)/shard_map/pallas_call | solution.py:1216

commit v8 on v7

--- a/solution.py
+++ b/solution.py
@@ -77,88 +77,76 @@
         ("r2", 0), ("a", 4), ("s1", 2),
     ),
     "p2.4": (
-        ("a", 5), ("s1", 3), ("s3", 0), ("s2", 1),
+        ("a", 5), ("s3", 0), ("s2", 1), ("s1", 3),
     ),
     "p2.6": (
-        ("a", 6), ("s1", 4), ("s4", 0),
-    ),
-    "p3.0": (
-        ("s2", 2), ("a", 7), ("s3", 1), ("s1", 5),
+        ("a", 6), ("s4", 0),
+    ),
+    "p2.7": (
+        ("s2", 2), ("s1", 4), ("a", 7), ("s3", 1),
     ),
     "p3.2": (
-        ("a", 8), ("s4", 1), ("s2", 3), ("s1", 6), ("s3", 2),
-    ),
-    "p3.4": (
-        ("a", 9),
+        ("s2", 3), ("s1", 5), ("a", 8), ("s3", 2), ("s4", 1),
     ),
     "p3.6": (
-        ("s2", 4), ("s1", 7), ("a", 10), ("s3", 3), ("s4", 2),
+        ("s2", 4), ("s1", 6), ("a", 9), ("s3", 3), ("s4", 2),
     ),
     "e0.3": (
-        ("s4", 3), ("s2", 5), ("s1", 8), ("a", 11), ("s3", 4),
+        ("s2", 5), ("s1", 7), ("a", 10), ("s3", 4), ("s4", 3),
     ),
     "p4b": (
-        ("s2", 6), ("s1", 9), ("a", 12), ("s3", 5),
+        ("s2", 6), ("s1", 8), ("a", 11), ("s3", 5),
     ),
     "p5.0": (
-        ("s2", 7), ("s1", 10), ("s3", 6),
+        ("s2", 7), ("s1", 9), ("s3", 6),
     ),
     "p5.1": (
-        ("s2", 8), ("s1", 11), ("s3", 7),
+        ("s2", 8), ("s1", 10), ("s3", 7),
     ),
     "p5.2": (
-        ("ky", 0), ("s2", 9), ("s3", 8),
+        ("ky", 0), ("s2", 9), ("s1", 11), ("s3", 8),
     ),
     "p5.3": (
-        ("s2", 10), ("s1", 12), ("ky", 1), ("s3", 9),
+        ("ky", 1), ("s2", 10), ("s3", 9),
     ),
     "qp": (
-        ("s2", 11),
+        ("kl", 0),
     ),
     "e1.3": (
-        ("s4", 4), ("s4", 5), ("s3", 10), ("s4", 6), ("s4", 7), ("s4", 8), ("s4", 9), ("kl", 0), ("ky", 2),
+        ("s4", 4), ("s4", 5), ("s4", 6), ("s4", 7), ("s4", 8), ("s4", 9), ("s3", 10), ("ky", 2), ("s2", 11),
     ),
     "op": (
-        ("s3", 11), ("s4", 10), ("s2", 12), ("km", 0), ("ky", 3), ("s4", 11), ("a", 13), ("kl", 1), ("r1", 3),
-        ("s3", 12), ("a", 14), ("r1", 2), ("s4", 12), ("kl", 2), ("km", 1), ("r2", 3), ("a", 15), ("s1", 13),
-        ("r2", 2), ("a", 16), ("kl", 3), ("s1", 14), ("km", 2), ("a", 17), ("s1", 15), ("s2", 13), ("km", 3),
-        ("a", 18), ("s1", 16),
+        ("km", 0), ("s4", 10), ("kl", 1), ("s3", 11), ("ky", 3), ("a", 12), ("r1", 3), ("s4", 11), ("kl", 2),
+        ("km", 1), ("a", 13), ("r1", 2), ("r2", 3), ("kl", 3), ("km", 2), ("a", 14), ("s1", 12), ("r2", 2),
+        ("a", 15), ("s1", 13), ("km", 3), ("a", 16), ("s2", 12), ("s1", 14),
     ),
     "kp": (
-        ("a", 19), ("s2", 14), ("s1", 17), ("s3", 13),
+        ("a", 17),
     ),
     "p7.0": (
-        ("a", 20),
-    ),
-    "p7.1": (
-        ("s2", 15), ("s1", 18),
-    ),
-    "p7.2": (
-        ("a", 21), ("s3", 14), ("s4", 13),
+        ("s2", 13), ("s1", 15), ("a", 18), ("s3", 12),
+    ),
+    "p7.3": (
+        ("s2", 14), ("s1", 16), ("a", 19), ("s3", 13),
     ),
     "p7.4": (
-        ("s2", 16), ("s1", 19), ("a", 22), ("s3", 15), ("s4", 14),
-    ),
-    "p7.7": (
-        ("s2", 17), ("s1", 20), ("a", 23), ("s3", 16),
-    ),
-    "e2.1": (
-        ("s4", 15),
+        ("s4", 12),
+    ),
+    "p7.6": (
+        ("s2", 15), ("s1", 17), ("a", 20), ("s3", 14), ("s4", 13),
     ),
     "e2.2": (
-        ("s2", 18), ("s1", 21), ("a", 24), ("s3", 17),
+        ("s2", 16), ("s1", 18), ("a", 21), ("s3", 15), ("s4", 14),
     ),
     "e2.3": (
-        ("s4", 16),
-    ),
-    "lp": (
-        ("s2", 19), ("s1", 22), ("a", 25), ("s3", 18),
+        ("s4", 15), ("s2", 17), ("s1", 19), ("a", 22), ("s3", 16),
     ),
     "vec": (
-        ("s2", 20), ("s1", 23), ("s4", 17), ("s3", 19), ("s4", 18), ("s2", 21), ("s1", 24), ("s4", 19),
-        ("s3", 20), ("s2", 22), ("s1", 25), ("s3", 21), ("s4", 20), ("s4", 21), ("s2", 23), ("s3", 22),
-        ("s4", 22), ("s2", 24), ("s3", 23), ("s4", 23), ("s2", 25), ("s3", 24), ("s4", 24), ("s3", 25),
-        ("s4", 25),
+        ("s2", 18), ("s1", 20), ("a", 23), ("s3", 17), ("s4", 16), ("s2", 19), ("s1", 21), ("a", 24),
+        ("s4", 17), ("s3", 18), ("s2", 20), ("s1", 22), ("a", 25), ("s3", 19), ("s4", 18), ("s2", 21),
+        ("s1", 23), ("s3", 20), ("s4", 19), ("s4", 20), ("s2", 22), ("s1", 24), ("s3", 21), ("s4", 21),
+        ("s2", 23), ("s1", 25), ("s3", 22), ("s2", 24), ("s4", 22), ("s3", 23), ("s4", 23), ("s2", 25),
+        ("s3", 24), ("s4", 24), ("s3", 25), ("s4", 25),
     ),
 }
 

time: 404 us -> 401 us (level)
  no operation moved by 1% of the time
where the time goes in v8:
time: 401 us; the launch traced here: 394 us
  Pallas kernels  391 us (98%)
    pallas_call x1, Pallas kernels, back_call(): pl.pallas_call(back_kernel, out_shape=[jax.ShapeDtypeStruct((tokens, widt...  307 us
    pallas_call x1, Pallas kernels, forward_call(): pl.pallas_call(forward_kernel, out_shape=[jax.ShapeDtypeStruct((tokens, w...  76.2 us

profile of v8, /device:TPU:0, one launch (start us, length us, event | category | flops | bytes accessed | tf_op | source)
XLA Modules:
  0.0 394.3 jit_solution(3344319512804832151)
XLA Ops:
  0.6 1.3 broadcast_in_dim.15.n1_ref
  1.9 1.3 broadcast_in_dim.18.n2_ref
  3.2 76.2 %shard_map.281 = (f32[512,2048]{1,0:T(8,128)}, bf16[8,256,512]{2,1,0:T(8,128)(2,1)}, bf16[512,512]{1,0:T(8,128)(2,1)}, bf16[4,8,128,512]{3,2,1,0:T(8,128)(2,1)},...) custom-call(bf16[512,2048]{1,0:T(8,128)(2,1)} %bitcast.11, ...), custom_call_target="tpu_custom_call" | custom-call | tf_op jit(solution)/shard_map/pallas_call | solution.py:1590
  79.5 306.6 %shard_map.282 = (bf16[512,2048]{1,0:T(8,128)(2,1)}, bf16[512,2048]{1,0:T(8,128)(2,1)}, f32[1536,256]{1,0:T(8,128)}, f32[256,1536]{1,0:T(8,128)}, f32[256,1536]{...) custom-call(f32[512,2048]{1,0:T(8,128)} %get-tuple-element.54.h_hbm,, ...), custom_call_target="tpu_custom_call" | custom-call | tf_op jit(solution)/shard_map/pallas_call | solution.py:1157
  386.1 8.0 %shard_map.283 = (bf16[512,2048]{1,0:T(8,128)(2,1)}, bf16[512,2048]{1,0:T(8,128)(2,1)}, f32[1536,256]{1,0:T(8,128)}, f32[256,1536]{1,0:T(8,128)}, f32[256,1536]{...) custom-call(bf16[512,2048]{1,0:T(8,128)(2,1)} %get-tuple-element.66., ...), custom_call_target="tpu_custom_call" | custom-call | tf_op jit(solution)/shard_map/pallas_call | solution.py:1204

commit v9 on v8

--- a/solution.py
+++ b/solution.py
@@ -67,32 +67,38 @@
     "p1.5": (
         ("a", 2), ("r1", 0),
     ),
-    "p2.0": (
-        ("a", 3), ("s1", 1),
-    ),
     "p2.1": (
-        ("s2", 0),
+        ("a", 3), ("s1", 1), ("s2", 0),
     ),
     "p2.2": (
-        ("r2", 0), ("a", 4), ("s1", 2),
+        ("r2", 0),
+    ),
+    "p2.3": (
+        ("a", 4), ("s1", 2),
     ),
     "p2.4": (
-        ("a", 5), ("s3", 0), ("s2", 1), ("s1", 3),
+        ("s3", 0),
+    ),
+    "p2.5": (
+        ("a", 5), ("s2", 1), ("s1", 3),
     ),
     "p2.6": (
-        ("a", 6), ("s4", 0),
+        ("s4", 0),
     ),
     "p2.7": (
-        ("s2", 2), ("s1", 4), ("a", 7), ("s3", 1),
-    ),
-    "p3.2": (
-        ("s2", 3), ("s1", 5), ("a", 8), ("s3", 2), ("s4", 1),
-    ),
-    "p3.6": (
+        ("a", 6),
+    ),
+    "p3.0": (
+        ("s2", 2), ("s1", 4), ("s3", 1), ("a", 7),
+    ),
+    "p3.4": (
+        ("s4", 1), ("s2", 3), ("s1", 5), ("a", 8), ("s3", 2),
+    ),
+    "e0.3": (
         ("s2", 4), ("s1", 6), ("a", 9), ("s3", 3), ("s4", 2),
     ),
-    "e0.3": (
-        ("s2", 5), ("s1", 7), ("a", 10), ("s3", 4), ("s4", 3),
+    "p4a": (
+        ("s2", 5), ("s1", 7), ("a", 10), ("s3", 4),
     ),
     "p4b": (
         ("s2", 6), ("s1", 8), ("a", 11), ("s3", 5),
@@ -100,52 +106,44 @@
     "p5.0": (
         ("s2", 7), ("s1", 9), ("s3", 6),
     ),
-    "p5.1": (
-        ("s2", 8), ("s1", 10), ("s3", 7),
-    ),
     "p5.2": (
-        ("ky", 0), ("s2", 9), ("s1", 11), ("s3", 8),
+        ("s2", 8), ("ky", 0), ("s1", 10), ("s3", 7),
     ),
     "p5.3": (
-        ("ky", 1), ("s2", 10), ("s3", 9),
+        ("s2", 9), ("s1", 11), ("s3", 8),
     ),
     "qp": (
-        ("kl", 0),
+        ("kl", 0), ("ky", 1),
     ),
     "e1.3": (
-        ("s4", 4), ("s4", 5), ("s4", 6), ("s4", 7), ("s4", 8), ("s4", 9), ("s3", 10), ("ky", 2), ("s2", 11),
+        ("s4", 3), ("s4", 4), ("s4", 5), ("s3", 9), ("s4", 6), ("s4", 7), ("s4", 8), ("s2", 10),
     ),
     "op": (
-        ("km", 0), ("s4", 10), ("kl", 1), ("s3", 11), ("ky", 3), ("a", 12), ("r1", 3), ("s4", 11), ("kl", 2),
-        ("km", 1), ("a", 13), ("r1", 2), ("r2", 3), ("kl", 3), ("km", 2), ("a", 14), ("s1", 12), ("r2", 2),
-        ("a", 15), ("s1", 13), ("km", 3), ("a", 16), ("s2", 12), ("s1", 14),
+        ("km", 0), ("ky", 2), ("s4", 9), ("s2", 11), ("s3", 10), ("ky", 3), ("s4", 10), ("kl", 1), ("s3", 11),
+        ("r1", 3), ("a", 12), ("s4", 11), ("r1", 2), ("km", 1), ("a", 13), ("kl", 2), ("r2", 3), ("s1", 12),
+        ("a", 14), ("r2", 2), ("km", 2), ("kl", 3), ("s1", 13), ("a", 15), ("a", 16), ("s2", 12), ("km", 3),
+        ("s1", 14), ("a", 17),
     ),
     "kp": (
-        ("a", 17),
-    ),
-    "p7.0": (
-        ("s2", 13), ("s1", 15), ("a", 18), ("s3", 12),
-    ),
-    "p7.3": (
-        ("s2", 14), ("s1", 16), ("a", 19), ("s3", 13),
-    ),
-    "p7.4": (
-        ("s4", 12),
+        ("s2", 13), ("s1", 15), ("s3", 12), ("a", 18),
+    ),
+    "p7.2": (
+        ("s4", 12), ("s2", 14), ("s1", 16), ("a", 19), ("s3", 13),
     ),
     "p7.6": (
-        ("s2", 15), ("s1", 17), ("a", 20), ("s3", 14), ("s4", 13),
-    ),
-    "e2.2": (
-        ("s2", 16), ("s1", 18), ("a", 21), ("s3", 15), ("s4", 14),
+        ("s2", 15), ("s1", 17), ("a", 20), ("s3", 14),
+    ),
+    "e2.1": (
+        ("s4", 13), ("s4", 14), ("s2", 16), ("s1", 18), ("a", 21), ("s3", 15),
     ),
     "e2.3": (
         ("s4", 15), ("s2", 17), ("s1", 19), ("a", 22), ("s3", 16),
     ),
     "vec": (
         ("s2", 18), ("s1", 20), ("a", 23), ("s3", 17), ("s4", 16), ("s2", 19), ("s1", 21), ("a", 24),
-        ("s4", 17), ("s3", 18), ("s2", 20), ("s1", 22), ("a", 25), ("s3", 19), ("s4", 18), ("s2", 21),
-        ("s1", 23), ("s3", 20), ("s4", 19), ("s4", 20), ("s2", 22), ("s1", 24), ("s3", 21), ("s4", 21),
-        ("s2", 23), ("s1", 25), ("s3", 22), ("s2", 24), ("s4", 22), ("s3", 23), ("s4", 23), ("s2", 25),
+        ("s4", 17), ("s3", 18), ("s2", 20), ("s1", 22), ("a", 25), ("s3", 19), ("s4", 18), ("s4", 19),
+        ("s2", 21), ("s1", 23), ("s3", 20), ("s4", 20), ("s2", 22), ("s1", 24), ("s3", 21), ("s4", 21),
+        ("s2", 23), ("s1", 25), ("s3", 22), ("s4", 22), ("s2", 24), ("s3", 23), ("s4", 23), ("s2", 25),
         ("s3", 24), ("s4", 24), ("s3", 25), ("s4", 25),
     ),
 }

time: 401 us -> 403 us (level)
  no operation moved by 1% of the time
where the time goes in v9:
time: 403 us; the launch traced here: 397 us
  Pallas kernels  393 us (98%)
    pallas_call x1, Pallas kernels, back_call(): pl.pallas_call(back_kernel, out_shape=[jax.ShapeDtypeStruct((tokens, widt...  309 us
    pallas_call x1, Pallas kernels, forward_call(): pl.pallas_call(forward_kernel, out_shape=[jax.ShapeDtypeStruct((tokens, w...  76.2 us

profile of v9, /device:TPU:0, one launch (start us, length us, event | category | flops | bytes accessed | tf_op | source)
XLA Modules:
  0.0 396.7 jit_solution(9881201391515265042)
XLA Ops:
  0.6 1.3 broadcast_in_dim.15.n1_ref
  1.9 1.3 broadcast_in_dim.18.n2_ref
  3.2 76.2 %shard_map.281 = (f32[512,2048]{1,0:T(8,128)}, bf16[8,256,512]{2,1,0:T(8,128)(2,1)}, bf16[512,512]{1,0:T(8,128)(2,1)}, bf16[4,8,128,512]{3,2,1,0:T(8,128)(2,1)},...) custom-call(bf16[512,2048]{1,0:T(8,128)(2,1)} %bitcast.11, ...), custom_call_target="tpu_custom_call" | custom-call | tf_op jit(solution)/shard_map/pallas_call | solution.py:1588
  79.5 308.7 %shard_map.282 = (bf16[512,2048]{1,0:T(8,128)(2,1)}, bf16[512,2048]{1,0:T(8,128)(2,1)}, f32[1536,256]{1,0:T(8,128)}, f32[256,1536]{1,0:T(8,128)}, f32[256,1536]{...) custom-call(f32[512,2048]{1,0:T(8,128)} %get-tuple-element.54.h_hbm,, ...), custom_call_target="tpu_custom_call" | custom-call | tf_op jit(solution)/shard_map/pallas_call | solution.py:1155
  388.2 8.0 %shard_map.283 = (bf16[512,2048]{1,0:T(8,128)(2,1)}, bf16[512,2048]{1,0:T(8,128)(2,1)}, f32[1536,256]{1,0:T(8,128)}, f32[256,1536]{1,0:T(8,128)}, f32[256,1536]{...) custom-call(bf16[512,2048]{1,0:T(8,128)(2,1)} %get-tuple-element.66., ...), custom_call_target="tpu_custom_call" | custom-call | tf_op jit(solution)/shard_map/pallas_call | solution.py:1202
